TPU v7x, 256 devices: a whole 4x4x8 slice. The times are simulated.
256 devices in a mesh: leaf: 32 (over z, y), head: 8 (over x, core).
Axes of the slice: x: 4, y: 4, z: 8, core: 2. Of those that a mesh axis runs over, the one named last changes fastest.
Arguments:
- normed_input: bfloat16 [12288, 1024], P('leaf'), may hold values from -6 to 6
- queries: bfloat16 [12288, 2048], P('leaf', 'head'), may hold values from -128 to 128
- keys: bfloat16 [12288, 1024], P('leaf', 'head'), may hold values from -4 to 4
- values: bfloat16 [12288, 1024], P('leaf', 'head'), may hold values from -6 to 6
- grad_out: bfloat16 [12288, 1024], P('leaf'), may hold values from -6 to 6
- query_weight: bfloat16 [1024, 2048], P(None, 'head'), may hold values from -0.1875 to 0.1875
- key_projection_matrix: bfloat16 [1024, 1024], P(None, 'head'), may hold values from -0.1875 to 0.1875
- value_projection_matrix: bfloat16 [1024, 1024], P(None, 'head'), may hold values from -0.1875 to 0.1875
- output_weight: bfloat16 [2048, 1024], P('head'), may hold values from -0.125 to 0.125
- ancestors: int32 [96, 16], replicated, may hold values from -1 to 95, as said below
Outputs:
- input_grad: bfloat16 [12288, 1024], P('leaf', 'head')
- query_weight_grad: float32 [1024, 2048], P('leaf', 'head')
- key_weight_grad: float32 [1024, 1024], P('leaf', 'head')
- value_weight_grad: float32 [1024, 1024], P('leaf', 'head')
- output_weight_grad: float32 [2048, 1024], P('head', 'leaf')
Inputs may be any that keep to these rules, and one draw needn't show every extreme that they name: `ancestors`: row b lists b itself, then its parent, its parent's parent and so on to the root, then -1 in the remaining slots; every parent is an earlier block; some row lists exactly 16 blocks.
All inputs are finite; a program needn't handle non-finite values.
Results may differ from a plain program's by a relative error of at most 0.034.
Values may be sent and summed in bfloat16 or wider, within the bound.
No kernel may reach another device: no remote copies, remote signals or barrier semaphores. Data moves between devices by JAX's collectives and lax.ppermute only.
A program may use at most 128 MiB of HBM per device.

v0:
```python
import jax
import jax.numpy as jnp
from jax import lax
from jax.sharding import PartitionSpec as P

QUERY_HEADS = 16
KEY_VALUE_HEADS = 8
HEAD_WIDTH = 128
NODE_BLOCK_TOKENS = 128


def tile_visibility(anc_row, block_id, block_len):
    valid = anc_row >= 0
    itself = anc_row == block_id
    places = jnp.arange(block_len)
    causal = places[:, None] >= places[None, :]
    allowed = valid[None, :, None] & (jnp.logical_not(itself)[None, :, None] | causal[:, None, :])
    return allowed.reshape(block_len, -1)


def attend_block(query_tile, grad_tile, key_block_slice, value_block_slice, visible, score_scale):
    f32 = jnp.float32
    scores = (
        jnp.einsum("bhgd,lhd->hgbl", query_tile, key_block_slice, preferred_element_type=f32)
        * score_scale
    )
    scores = jnp.where(visible[None, None], scores, -jnp.inf)
    row_max = jnp.max(scores, axis=-1, keepdims=True)
    row_total = jnp.sum(jnp.exp(scores - row_max), axis=-1, keepdims=True)
    log_total = row_max + jnp.log(row_total)
    weights = jnp.exp(scores - log_total)
    probabilities = weights.astype(jnp.bfloat16)
    attended = jnp.einsum(
        "hgbl,lhd->bhgd", probabilities, value_block_slice, preferred_element_type=f32
    ).astype(jnp.bfloat16)
    row_delta = jnp.einsum("bhgd,bhgd->hgb", grad_tile, attended, preferred_element_type=f32)
    grad_probs = jnp.einsum(
        "bhgd,lhd->hgbl", grad_tile, value_block_slice, preferred_element_type=f32
    )
    dscore = (weights * (grad_probs - row_delta[..., None]) * score_scale).astype(jnp.bfloat16)
    grad_query = jnp.einsum(
        "hgbl,lhd->bhgd", dscore, key_block_slice, preferred_element_type=f32
    ).astype(jnp.bfloat16)
    return (attended, grad_query, dscore, probabilities, log_total[..., 0], row_delta)


def per_device(
    normed_input,
    queries,
    keys,
    values,
    grad_out,
    query_weight,
    key_projection_matrix,
    value_projection_matrix,
    output_weight,
    ancestors,
):
    f32 = jnp.float32
    query_group_count = QUERY_HEADS // KEY_VALUE_HEADS
    score_scale = HEAD_WIDTH ** (-0.5)
    rows_dev = queries.shape[0]
    blocks_dev = rows_dev // NODE_BLOCK_TOKENS
    query_cols = queries.shape[1]
    heads_kv = keys.shape[1] // HEAD_WIDTH
    block_count = ancestors.shape[0]
    anc_len = ancestors.shape[1]
    attention_grad = jnp.dot(grad_out, output_weight.T, preferred_element_type=f32).astype(
        jnp.bfloat16
    )
    full_keys, full_values = (
        lax.all_gather(keys, "leaf", axis=0, tiled=True),
        lax.all_gather(values, "leaf", axis=0, tiled=True),
    )
    blocked_keys = full_keys.reshape(block_count, NODE_BLOCK_TOKENS, heads_kv, HEAD_WIDTH)
    blocked_values = full_values.reshape(block_count, NODE_BLOCK_TOKENS, heads_kv, HEAD_WIDTH)
    leaf_pos = lax.axis_index("leaf")
    key_dense = jnp.zeros((block_count, NODE_BLOCK_TOKENS, heads_kv, HEAD_WIDTH), f32)
    value_dense = jnp.zeros((block_count, NODE_BLOCK_TOKENS, heads_kv, HEAD_WIDTH), f32)
    attended_list = []
    grad_list = []
    lse_list = []
    delta_list = []
    for number in range(blocks_dev):
        block_id = leaf_pos * blocks_dev + number
        anc_row = lax.dynamic_index_in_dim(ancestors, block_id, 0, keepdims=False)
        guarded_rows = jnp.maximum(anc_row, 0)
        key_block_slice = blocked_keys[guarded_rows].reshape(
            anc_len * NODE_BLOCK_TOKENS, heads_kv, HEAD_WIDTH
        )
        value_block_slice = blocked_values[guarded_rows].reshape(
            anc_len * NODE_BLOCK_TOKENS, heads_kv, HEAD_WIDTH
        )
        visible = tile_visibility(anc_row, block_id, NODE_BLOCK_TOKENS)
        query_tile = queries[number * NODE_BLOCK_TOKENS : (number + 1) * NODE_BLOCK_TOKENS].reshape(
            NODE_BLOCK_TOKENS, heads_kv, query_group_count, HEAD_WIDTH
        )
        grad_tile = attention_grad[
            number * NODE_BLOCK_TOKENS : (number + 1) * NODE_BLOCK_TOKENS
        ].reshape(NODE_BLOCK_TOKENS, heads_kv, query_group_count, HEAD_WIDTH)
        attended, grad_query, dscore, probabilities, log_total, row_delta = attend_block(
            query_tile, grad_tile, key_block_slice, value_block_slice, visible, score_scale
        )
        attended_list.append(attended.reshape(NODE_BLOCK_TOKENS, query_cols))
        grad_list.append(grad_query.reshape(NODE_BLOCK_TOKENS, query_cols))
        lse_list.append(
            log_total.transpose(2, 0, 1).reshape(NODE_BLOCK_TOKENS, heads_kv * query_group_count)
        )
        delta_list.append(
            row_delta.transpose(2, 0, 1).reshape(NODE_BLOCK_TOKENS, heads_kv * query_group_count)
        )
        key_contribution = jnp.einsum(
            "hgbl,bhgd->lhd", dscore, query_tile, preferred_element_type=f32
        )
        value_contribution = jnp.einsum(
            "hgbl,bhgd->lhd", probabilities, grad_tile, preferred_element_type=f32
        )
        key_dense = key_dense.at[guarded_rows].add(
            key_contribution.reshape(anc_len, NODE_BLOCK_TOKENS, heads_kv, HEAD_WIDTH)
        )
        value_dense = value_dense.at[guarded_rows].add(
            value_contribution.reshape(anc_len, NODE_BLOCK_TOKENS, heads_kv, HEAD_WIDTH)
        )
    attn_out = jnp.concatenate(attended_list, axis=0)
    grad_q = jnp.concatenate(grad_list, axis=0)
    key_sum, value_sum = (
        lax.psum_scatter(
            key_dense.reshape(block_count * NODE_BLOCK_TOKENS, heads_kv * HEAD_WIDTH),
            "leaf",
            scatter_dimension=0,
            tiled=True,
        ),
        lax.psum_scatter(
            value_dense.reshape(block_count * NODE_BLOCK_TOKENS, heads_kv * HEAD_WIDTH),
            "leaf",
            scatter_dimension=0,
            tiled=True,
        ),
    )
    key_gradient = key_sum.astype(jnp.bfloat16)
    value_gradient = value_sum.astype(jnp.bfloat16)
    query_part = jnp.dot(normed_input.T, grad_q, preferred_element_type=f32)
    output_part = jnp.dot(grad_out.T, attn_out, preferred_element_type=f32)
    query_weight_grad, output_sum = (
        lax.psum_scatter(
            query_part.astype(jnp.bfloat16), "leaf", scatter_dimension=0, tiled=True
        ).astype(jnp.float32),
        lax.psum_scatter(
            output_part.astype(jnp.bfloat16), "leaf", scatter_dimension=0, tiled=True
        ).astype(jnp.float32),
    )
    output_weight_grad = output_sum.T
    key_part = jnp.dot(normed_input.T, key_gradient, preferred_element_type=f32)
    value_part = jnp.dot(normed_input.T, value_gradient, preferred_element_type=f32)
    key_weight_grad, value_weight_grad = (
        lax.psum_scatter(
            key_part.astype(jnp.bfloat16), "leaf", scatter_dimension=0, tiled=True
        ).astype(jnp.float32),
        lax.psum_scatter(
            value_part.astype(jnp.bfloat16), "leaf", scatter_dimension=0, tiled=True
        ).astype(jnp.float32),
    )
    input_part = jnp.dot(grad_q, query_weight.T, preferred_element_type=f32)
    input_part = input_part + jnp.dot(
        key_gradient, key_projection_matrix.T, preferred_element_type=f32
    )
    input_part = input_part + jnp.dot(
        value_gradient, value_projection_matrix.T, preferred_element_type=f32
    )
    input_grad = lax.psum_scatter(
        input_part.astype(jnp.bfloat16), "head", scatter_dimension=1, tiled=True
    )
    return (input_grad, query_weight_grad, key_weight_grad, value_weight_grad, output_weight_grad)


def solution(mesh):
    return jax.shard_map(
        per_device,
        mesh=mesh,
        in_specs=(
            P("leaf", None),
            P("leaf", "head"),
            P("leaf", "head"),
            P("leaf", "head"),
            P("leaf", None),
            P(None, "head"),
            P(None, "head"),
            P(None, "head"),
            P("head", None),
            P(),
        ),
        out_specs=(
            P("leaf", "head"),
            P("leaf", "head"),
            P("leaf", "head"),
            P("leaf", "head"),
            P("head", "leaf"),
        ),
        check_vma=False,
    )
```

profile of v0, /device:TPU:6, one launch (start us, length us, event | category | flops | bytes accessed | tf_op | source)
XLA Modules:
  0.0 1565.5 jit_solution(5727279404444261416)
XLA Ops:
  11.9 2.9 fusion.31
  15.9 2.4 convolution_convert_fusion.4
  18.3 75.2 %all-gather.5.cloned.1.call-done = bf16[12288,128]{1,0:T(8,128)(2,1)} async-done(((bf16[384,128]{1,0:T(8,128)(2,1)}), bf16[12288,128]{1,0:T(8,128)(2,1)}) %all-gather.5.cloned.1.call-update) | async-done | bytes 3145744 | tf_op jit(solution)/shard_map/all_gather | solution.py:73
  93.5 2.5 gather_fusion.5
  96.0 76.6 %all-gather.3.cloned.1.call-done = bf16[12288,128]{1,0:T(8,128)(2,1)} async-done(((bf16[384,128]{1,0:T(8,128)(2,1)}), bf16[12288,128]{1,0:T(8,128)(2,1)}) %all-gather.3.cloned.1.call-update) | async-done | bytes 3145744 | tf_op jit(solution)/shard_map/all_gather | solution.py:72
  172.7 3.3 gather_fusion.4
  176.0 3.3 gather_fusion.1
  179.3 3.3 gather_fusion
  182.6 3.3 gather_fusion.3
  185.9 3.3 gather_fusion.2
  189.3 1.7 fusion.58
  202.2 3.4 broadcast.170.clone
  205.6 4.0 scatter_fusion
  209.6 4.0 scatter_fusion.1
  213.6 4.0 scatter_fusion.2
  220.0 2.7 copy.174
  222.7 1.6 convolution_bitcast_fusion.3
  224.2 2.7 copy.176
  228.5 1.5 copy.175
  230.0 3.4 broadcast.170.clone.1
  233.5 3.8 scatter_fusion.3
  237.3 3.7 scatter_fusion.4
  241.0 3.7 scatter_fusion.5
  245.9 1.5 convolution_convert_fusion.9
  251.5 185.9 %reduce-scatter.18.cloned.1.call-done = f32[384,128]{1,0:T(8,128)} async-done(((f32[12288,128]{1,0:T(8,128)}), f32[384,128]{1,0:T(8,128)}) %reduce-scatter.18.cloned.1.call-update) | async-done | bytes 196624 | tf_op jit(solution)/shard_map/reduce_scatter | solution.py:127
  440.0 224.5 %reduce-scatter.20.cloned.1.call-done = f32[384,128]{1,0:T(8,128)} async-done(((f32[12288,128]{1,0:T(8,128)}), f32[384,128]{1,0:T(8,128)}) %reduce-scatter.20.cloned.1.call-update) | async-done | bytes 196624 | tf_op jit(solution)/shard_map/reduce_scatter | solution.py:133
  670.7 208.9 %reduce-scatter.24.cloned.1.call-done = bf16[32,256]{1,0:T(8,128)(2,1)} async-done(((bf16[1024,256]{1,0:T(8,128)(2,1)}), bf16[32,256]{1,0:T(8,128)(2,1)}) %reduce-scatter.24.cloned.1.call-update) | async-done | bytes 16400
  881.1 214.1 %reduce-scatter.30.cloned.1.call-done = bf16[32,256]{1,0:T(8,128)(2,1)} async-done(((bf16[1024,256]{1,0:T(8,128)(2,1)}), bf16[32,256]{1,0:T(8,128)(2,1)}) %reduce-scatter.30.cloned.1.call-update) | async-done | bytes 16400
  1096.8 213.4 %reduce-scatter.26.cloned.1.call-done = bf16[32,128]{1,0:T(8,128)(2,1)} async-done(((bf16[1024,128]{1,0:T(8,128)(2,1)}), bf16[32,128]{1,0:T(8,128)(2,1)}) %reduce-scatter.26.cloned.1.call-update) | async-done | bytes 8208
  1311.7 213.9 %reduce-scatter.28.cloned.1.call-done = bf16[32,128]{1,0:T(8,128)(2,1)} async-done(((bf16[1024,128]{1,0:T(8,128)(2,1)}), bf16[32,128]{1,0:T(8,128)(2,1)}) %reduce-scatter.28.cloned.1.call-update) | async-done | bytes 8208
  1527.1 30.2 %reduce-scatter.22.cloned.1.call-done = bf16[128,384]{1,0:T(8,128)(2,1)} async-done(((bf16[1024,384]{1,0:T(8,128)(2,1)}), bf16[128,384]{1,0:T(8,128)(2,1)}) %reduce-scatter.22.cloned.1.call-update) | async-done | bytes 98320
  1557.3 1.6 copy.178
  (159 shorter events, 40.4 us)
Async XLA Ops:
  7.2 241.1 %copy-start = (bf16[384,1024]{1,0:T(8,128)(2,1)S(1)}, bf16[384,1024]{1,0:T(8,128)(2,1)}, u32[]{:S(2)}) copy-start(bf16[384,1024]{1,0:T(8,128)(2,1)} %param.10) | copy-start | bytes 2359300
  7.2 86.3 %all-gather.5.cloned.1.call-start = ((), (), s32[]{:S(2)}) async-start(), calls=%async_computation.8 | async-start | bytes 3244032 | tf_op jit(solution)/shard_map/all_gather | solution.py:73
  7.9 164.8 %all-gather.3.cloned.1.call-start = ((), (), s32[]{:S(2)}) async-start(), calls=%async_computation.7 | async-start | bytes 3244032 | tf_op jit(solution)/shard_map/all_gather | solution.py:72
  8.7 428.7 %reduce-scatter.18.cloned.1.call-start = ((), (), s32[]{:S(2)}) async-start(), calls=%async_computation.9 | async-start | bytes 6488064 | tf_op jit(solution)/shard_map/reduce_scatter | solution.py:127
  9.8 179.5 %copy-start.35 = (bf16[128,256]{0,1:T(8,128)(2,1)}, bf16[128,256]{0,1:T(8,128)(2,1)S(1)}, u32[]{:S(2)}) copy-start(bf16[128,256]{0,1:T(8,128)(2,1)S(1)} %copy.187) | copy-start | bytes 196612
  9.9 182.3 %copy-start.33 = (bf16[128,256]{0,1:T(8,128)(2,1)}, bf16[128,256]{0,1:T(8,128)(2,1)S(1)}, u32[]{:S(2)}) copy-start(bf16[128,256]{0,1:T(8,128)(2,1)S(1)} %copy.188) | copy-start | bytes 196612
  15.8 163.5 %copy-start.39 = (s32[16]{0:T(128)}, s32[16]{0:T(128)S(1)}, u32[]{:S(2)}) copy-start(s32[16]{0:T(128)S(1)} %get-tuple-element.28) | copy-start | bytes 196
  15.9 163.5 %copy-start.41 = (s32[16]{0:T(128)}, s32[16]{0:T(128)S(1)}, u32[]{:S(2)}) copy-start(s32[16]{0:T(128)S(1)} %get-tuple-element.26) | copy-start | bytes 196
  189.3 2.0 copy-start.21
  189.3 2.0 copy-start.37
  191.8 6.0 copy-start.1
  192.9 7.0 copy-start.3
  195.3 2.5 copy-start.25
  196.4 2.0 copy-start.5
  198.5 2.0 copy-start.7
  202.2 3.4 copy-start.42
  205.6 4.0 copy-start.40
  217.6 446.9 %reduce-scatter.20.cloned.1.call-start = ((), (), s32[]{:S(2)}) async-start(), calls=%async_computation.10 | async-start | bytes 6488064 | tf_op jit(solution)/shard_map/reduce_scatter | solution.py:133
  220.0 2.7 copy-start.2
  224.2 2.7 copy-start.4
  230.0 3.5 copy-start.18
  237.3 3.7 copy-start.17
  244.7 2.8 copy-start.8
  244.7 2.8 copy-start.14
  244.7 634.9 %reduce-scatter.24.cloned.1.call-start = ((), (), s32[]{:S(2)}) async-start(), calls=%async_computation.12 | async-start | bytes 540672
  249.8 845.4 %reduce-scatter.30.cloned.1.call-start = ((), (), s32[]{:S(2)}) async-start(), calls=%async_computation.15 | async-start | bytes 540672
  250.3 189.2 %copy-start.38 = (bf16[1024,256]{1,0:T(8,128)(2,1)S(1)}, bf16[1024,256]{1,0:T(8,128)(2,1)}, u32[]{:S(2)}) copy-start(bf16[1024,256]{1,0:T(8,128)(2,1)} %param.15) | copy-start | bytes 1572868
  251.4 1058.8 %reduce-scatter.26.cloned.1.call-start = ((), (), s32[]{:S(2)}) async-start(), calls=%async_computation.13 | async-start | bytes 270336
  439.5 227.3 %copy-start.24 = (f32[384,128]{1,0:T(8,128)S(1)}, f32[384,128]{1,0:T(8,128)}, u32[]{:S(2)}) copy-start(f32[384,128]{1,0:T(8,128)} %reduce-scatter.18.cloned.1.call-done) | copy-start | bytes 589828
  439.5 1086.1 %reduce-scatter.28.cloned.1.call-start = ((), (), s32[]{:S(2)}) async-start(), calls=%async_computation.14 | async-start | bytes 270336
  664.5 3.6 copy-start.22
  666.7 890.6 %reduce-scatter.22.cloned.1.call-start = ((), (), s32[]{:S(2)}) async-start(), calls=%async_computation.11 | async-start | bytes 884736
  (20 other events, 27.3 us)
Sparse Core Ops, SparseCore 0:
  10.6 82.8 all-gather.4
  96.1 76.5 all-gather.2
  217.8 219.5 reduce-scatter.17
  441.7 222.7 reduce-scatter.19
  668.2 211.3 reduce-scatter.23
  883.7 211.4 reduce-scatter.29
  1099.0 211.1 reduce-scatter.25
  1314.5 211.0 reduce-scatter.27
  1528.1 29.1 reduce-scatter.21
where the time goes:
time: 1570 us
  waiting for transfers between devices  1440 us (92%)
  local copies, waits for them, and re-layouts  50.9 us (3%)
  other arithmetic  29.2 us (2%)
  matrix products  26.1 us (2%)
    unnamed x14, waiting for transfers between devices  882 us
    reduce_scatter x1, waiting for transfers between devices, per_device(): lax.psum_scatter(value_dense.reshape(block_count * NODE_BLOCK_TOKENS, hea...  225 us
    reduce_scatter x1, waiting for transfers between devices, per_device(): lax.psum_scatter(key_dense.reshape(block_count * NODE_BLOCK_TOKENS, heads...  186 us
    all_gather x1, waiting for transfers between devices, per_device(): lax.all_gather(keys, 'leaf', axis=0, tiled=True)  76.6 us
    all_gather x1, waiting for transfers between devices, per_device(): lax.all_gather(values, 'leaf', axis=0, tiled=True)  75.2 us
  transfers between devices with their start and end apart: 9, of which 9 were waited for; matrix products, arithmetic and copies ran while one was open for 4% of the time, Pallas kernels for 0%

commit v1 on v0

v1 whole, which is shorter than its diff:
```python
import functools

import jax
import jax.numpy as jnp
from jax import lax
from jax.experimental import pallas as pl
from jax.experimental.pallas import tpu as pltpu
from jax.sharding import Mesh, PartitionSpec as P

HEAD_WIDTH = 128
BLOCK = 128
GROUP = 2
NZ, NY = 8, 4
DEV_BLOCKS = 3
ROW_BLOCKS = NY * DEV_BLOCKS
COL_BLOCKS = NZ * DEV_BLOCKS
PATH = 16
PAIR = GROUP * BLOCK
SCALE = HEAD_WIDTH ** (-0.5)
NEG = -1e30
STAT_ROWS = 16
VMEM_LIMIT = 48 * 1024 * 1024

f32 = jnp.float32
bf16 = jnp.bfloat16


def dot_nt(a, b):
    return lax.dot_general(a, b, (((1,), (1,)), ((), ())), preferred_element_type=f32)


def dot_nn(a, b):
    return jnp.dot(a, b, preferred_element_type=f32)


def fold(x, op):
    return op(x.reshape(BLOCK // 8, 8, PAIR), axis=0)


def collect(anc_ref, list_ref, block, y):
    def step(j, count):
        c = anc_ref[block, j]
        hit = jnp.logical_and(c >= 0, lax.rem(lax.div(c, DEV_BLOCKS), NY) == y)
        list_ref[count] = lax.div(c, ROW_BLOCKS) * DEV_BLOCKS + lax.rem(c, DEV_BLOCKS)
        return count + hit.astype(jnp.int32)

    return lax.fori_loop(0, PATH, step, jnp.int32(0))


def stack_queries(qd_refs, q_scr, d_scr):
    for s in range(NY):
        for r in range(DEV_BLOCKS):
            for h in range(GROUP):
                rows = slice(r * BLOCK, (r + 1) * BLOCK)
                put = slice(h * BLOCK, (h + 1) * BLOCK)
                cols = slice(h * HEAD_WIDTH, (h + 1) * HEAD_WIDTH)
                dcols = slice(PAIR + h * HEAD_WIDTH, PAIR + (h + 1) * HEAD_WIDTH)
                q_scr[s * DEV_BLOCKS + r, put, :] = qd_refs[s][rows, cols]
                d_scr[s * DEV_BLOCKS + r, put, :] = qd_refs[s][rows, dcols]


def place_of(i, z, y):
    s = lax.div(i, DEV_BLOCKS)
    r = lax.rem(i, DEV_BLOCKS)
    at = lax.rem(y - s + NY, NY) * DEV_BLOCKS + r
    own = jnp.where(s == 0, z * DEV_BLOCKS + r, -1)
    return at, z * ROW_BLOCKS + at, own


def score_tile(k, q, is_own):
    s = dot_nt(k, q) * SCALE
    key_at = lax.broadcasted_iota(jnp.int32, (BLOCK, PAIR), 0)
    query_at = lax.rem(lax.broadcasted_iota(jnp.int32, (BLOCK, PAIR), 1), BLOCK)
    return jnp.where(jnp.logical_and(is_own, key_at > query_at), NEG, s)


def stats_kernel(pos_ref, anc_ref, kv_ref, qd0, qd1, qd2, qd3, out_ref, q_scr, d_scr, s_scr, list_ref):
    z, y = pos_ref[0], pos_ref[1]
    stack_queries((qd0, qd1, qd2, qd3), q_scr, d_scr)

    def one_block(i, _):
        at, block, own = place_of(i, z, y)
        count = collect(anc_ref, list_ref, block, y)
        q = q_scr[i]
        d = d_scr[i]

        def scores(j, top):
            slot = list_ref[j]
            rows = pl.ds(pl.multiple_of(slot * BLOCK, BLOCK), BLOCK)
            s = score_tile(kv_ref[rows, :HEAD_WIDTH], q, slot == own)
            s_scr[j] = s
            return jnp.maximum(top, fold(s, jnp.max))

        top = lax.fori_loop(0, count, scores, jnp.full((8, PAIR), NEG, f32))
        m = jnp.max(top, axis=0, keepdims=True)

        def sums(j, carry):
            total, dsum = carry
            slot = list_ref[j]
            rows = pl.ds(pl.multiple_of(slot * BLOCK, BLOCK), BLOCK)
            p = jnp.exp(s_scr[j] - m)
            g = dot_nt(kv_ref[rows, HEAD_WIDTH:], d)
            return total + fold(p, jnp.sum), dsum + fold(p * g, jnp.sum)

        zero = jnp.zeros((8, PAIR), f32)
        total, dsum = lax.fori_loop(0, count, sums, (zero, zero))
        out_ref[pl.ds(at, 1), :] = m
        out_ref[pl.ds(STAT_ROWS + at, 1), :] = jnp.sum(total, axis=0, keepdims=True)
        out_ref[pl.ds(2 * STAT_ROWS + at, 1), :] = jnp.sum(dsum, axis=0, keepdims=True)
        return 0

    lax.fori_loop(0, ROW_BLOCKS, one_block, 0)


def grads_kernel(
    pos_ref, anc_ref, kv_ref, qd0, qd1, qd2, qd3, st0, st1, st2, st3,
    row_ref, col_ref,
    q_scr, d_scr, kt_scr, vt_scr, o_scr, dq_scr, dk_scr, dv_scr, list_ref,
):
    z, y = pos_ref[0], pos_ref[1]
    stats = (st0, st1, st2, st3)
    stack_queries((qd0, qd1, qd2, qd3), q_scr, d_scr)

    def prepare(c, _):
        rows = pl.ds(pl.multiple_of(c * BLOCK, BLOCK), BLOCK)
        kt_scr[c] = kv_ref[rows, :HEAD_WIDTH].T
        vt_scr[c] = kv_ref[rows, HEAD_WIDTH:].T
        dk_scr[c] = jnp.zeros((BLOCK, HEAD_WIDTH), f32)
        dv_scr[c] = jnp.zeros((BLOCK, HEAD_WIDTH), f32)
        return 0

    lax.fori_loop(0, COL_BLOCKS, prepare, 0)

    def one_block(i, _):
        at, block, own = place_of(i, z, y)
        count = collect(anc_ref, list_ref, block, y)
        q = q_scr[i]
        d = d_scr[i]
        tops = [st[pl.ds(at, 1), :] for st in stats]
        m = functools.reduce(jnp.maximum, tops)
        factors = [jnp.exp(t - m) for t in tops]
        total = sum(st[pl.ds(STAT_ROWS + at, 1), :] * f for st, f in zip(stats, factors))
        dsum = sum(st[pl.ds(2 * STAT_ROWS + at, 1), :] * f for st, f in zip(stats, factors))
        lse = m + jnp.log(total)
        delta = dsum / total
        o_scr[...] = jnp.zeros((HEAD_WIDTH, PAIR), f32)
        dq_scr[...] = jnp.zeros((HEAD_WIDTH, PAIR), f32)

        def one_key(j, _):
            slot = list_ref[j]
            rows = pl.ds(pl.multiple_of(slot * BLOCK, BLOCK), BLOCK)
            s = score_tile(kv_ref[rows, :HEAD_WIDTH], q, slot == own)
            w = jnp.exp(s - lse)
            p = w.astype(bf16)
            g = dot_nt(kv_ref[rows, HEAD_WIDTH:], d)
            ds = (w * (g - delta) * SCALE).astype(bf16)
            o_scr[...] += dot_nn(vt_scr[slot], p)
            dq_scr[...] += dot_nn(kt_scr[slot], ds)
            dk_scr[slot] += dot_nn(ds, q)
            dv_scr[slot] += dot_nn(p, d)
            return 0

        lax.fori_loop(0, count, one_key, 0)
        t = lax.rem(NY - lax.div(i, DEV_BLOCKS), NY)
        cols = pl.ds(pl.multiple_of(lax.rem(i, DEV_BLOCKS) * BLOCK, BLOCK), BLOCK)
        for h in range(GROUP):
            heads = slice(h * BLOCK, (h + 1) * BLOCK)
            row_ref[t, h * HEAD_WIDTH : (h + 1) * HEAD_WIDTH, cols] = o_scr[:, heads].astype(bf16)
            row_ref[t, PAIR + h * HEAD_WIDTH : PAIR + (h + 1) * HEAD_WIDTH, cols] = dq_scr[
                :, heads
            ].astype(bf16)
        return 0

    lax.fori_loop(0, ROW_BLOCKS, one_block, 0)

    def finish(c, _):
        rows = pl.ds(pl.multiple_of(c * BLOCK, BLOCK), BLOCK)
        col_ref[rows, :HEAD_WIDTH] = dk_scr[c].astype(bf16)
        col_ref[rows, HEAD_WIDTH:] = dv_scr[c].astype(bf16)
        return 0

    lax.fori_loop(0, COL_BLOCKS, finish, 0)


SMEM_SPEC = pl.BlockSpec(memory_space=pltpu.SMEM)
VMEM_SPEC = pl.BlockSpec(memory_space=pltpu.VMEM)


def stats_call(pos, anc, kv, qds):
    return pl.pallas_call(
        stats_kernel,
        out_shape=jax.ShapeDtypeStruct((3 * STAT_ROWS, PAIR), f32),
        in_specs=[SMEM_SPEC] * 2 + [VMEM_SPEC] * 5,
        out_specs=VMEM_SPEC,
        scratch_shapes=[
            pltpu.VMEM((ROW_BLOCKS, PAIR, HEAD_WIDTH), bf16),
            pltpu.VMEM((ROW_BLOCKS, PAIR, HEAD_WIDTH), bf16),
            pltpu.VMEM((PATH, BLOCK, PAIR), f32),
            pltpu.SMEM((PATH + 1,), jnp.int32),
        ],
        compiler_params=pltpu.CompilerParams(vmem_limit_bytes=VMEM_LIMIT),
        name="stats",
    )(pos, anc, kv, *qds)


def grads_call(pos, anc, kv, qds, stats):
    return pl.pallas_call(
        grads_kernel,
        out_shape=(
            jax.ShapeDtypeStruct((NY, 2 * PAIR, DEV_BLOCKS * BLOCK), bf16),
            jax.ShapeDtypeStruct((COL_BLOCKS * BLOCK, 2 * HEAD_WIDTH), bf16),
        ),
        in_specs=[SMEM_SPEC] * 2 + [VMEM_SPEC] * 9,
        out_specs=(VMEM_SPEC, VMEM_SPEC),
        scratch_shapes=[
            pltpu.VMEM((ROW_BLOCKS, PAIR, HEAD_WIDTH), bf16),
            pltpu.VMEM((ROW_BLOCKS, PAIR, HEAD_WIDTH), bf16),
            pltpu.VMEM((COL_BLOCKS, HEAD_WIDTH, BLOCK), bf16),
            pltpu.VMEM((COL_BLOCKS, HEAD_WIDTH, BLOCK), bf16),
            pltpu.VMEM((HEAD_WIDTH, PAIR), f32),
            pltpu.VMEM((HEAD_WIDTH, PAIR), f32),
            pltpu.VMEM((COL_BLOCKS, BLOCK, HEAD_WIDTH), f32),
            pltpu.VMEM((COL_BLOCKS, BLOCK, HEAD_WIDTH), f32),
            pltpu.SMEM((PATH + 1,), jnp.int32),
        ],
        compiler_params=pltpu.CompilerParams(vmem_limit_bytes=VMEM_LIMIT),
        name="grads",
    )(pos, anc, kv, *qds, *stats)


def shift(x, axis, size, by):
    return lax.ppermute(x, axis, [(i, (i + by) % size) for i in range(size)])


def per_device(
    nx, nc, normed_input, queries, keys, values, grad_out, query_weight, key_weight, value_weight, output_weight, ancestors
):
    z, y = lax.axis_index("z"), lax.axis_index("y")
    x, c = lax.axis_index("x"), lax.axis_index("c")
    rows = queries.shape[0]
    model = grad_out.shape[1]
    pos = jnp.stack([z, y]).astype(jnp.int32)

    kv = lax.all_gather(jnp.concatenate([keys, values], axis=1), "z", axis=0, tiled=True)
    attn_grad = dot_nt(grad_out, output_weight).astype(bf16)
    mine = jnp.concatenate([queries, attn_grad], axis=1)
    qds = [mine] + [shift(mine, "y", NY, s) for s in range(1, NY)]

    heads = nx * nc
    width = model // heads

    def laid_out(w):
        w = w.reshape(nx, nc, width, w.shape[1])
        w = jnp.roll(jnp.roll(w, -x, axis=0), -c, axis=1)
        return w.transpose(1, 0, 2, 3).reshape(model, w.shape[3])

    wq = laid_out(query_weight)
    wkv = laid_out(jnp.concatenate([key_weight, value_weight], axis=1))

    own = stats_call(pos, ancestors, kv, qds)
    stats = [own] + [shift(own, "y", NY, s) for s in range(1, NY)]
    row_part, col_part = grads_call(pos, ancestors, kv, qds, stats)

    got = [shift(row_part[s], "y", NY, s) for s in range(1, NY)]
    col_got = lax.all_to_all(col_part.reshape(NZ, rows, 2 * HEAD_WIDTH), "z", 0, 0, tiled=True)
    row_sum = sum((g.astype(f32) for g in got), row_part[0].astype(f32)).astype(bf16)
    attn_t, dq_t = row_sum[:PAIR], row_sum[PAIR:]
    dkv = jnp.sum(col_got.astype(f32), axis=0).astype(bf16)

    part = lax.dot_general(dq_t, wq, (((0,), (1,)), ((), ())), preferred_element_type=f32)
    part = part + dot_nt(dkv, wkv)
    part = part.reshape(rows, nc, nx * width)
    keep = part[:, 0]
    for s in range(1, nc):
        keep = keep + shift(part[:, s].astype(bf16), "c", nc, s).astype(f32)
    input_grad = keep[:, :width]
    for s in range(1, nx):
        piece = keep[:, s * width : (s + 1) * width].astype(bf16)
        input_grad = input_grad + shift(piece, "x", nx, s).astype(f32)
    input_grad = input_grad.astype(bf16)

    contract_rows = (((0,), (0,)), ((), ()))
    q_part = lax.dot_general(normed_input, dq_t, (((0,), (1,)), ((), ())), preferred_element_type=f32)
    kv_part = lax.dot_general(normed_input, dkv, contract_rows, preferred_element_type=f32)
    o_part = lax.dot_general(grad_out, attn_t, (((0,), (1,)), ((), ())), preferred_element_type=f32)
    parts = jnp.concatenate([q_part.astype(bf16), o_part.astype(bf16), kv_part.astype(bf16)], axis=1)
    leaves = NZ * NY
    parts = parts.reshape(leaves, model // leaves, parts.shape[1])
    sums = jnp.sum(lax.all_to_all(parts, ("z", "y"), 0, 0, tiled=True).astype(f32), axis=0)
    return (
        input_grad,
        sums[:, :PAIR],
        sums[:, 2 * PAIR : 2 * PAIR + HEAD_WIDTH],
        sums[:, 2 * PAIR + HEAD_WIDTH :],
        sums[:, PAIR : 2 * PAIR].T,
    )


def solution(mesh):
    heads = mesh.shape["head"]
    nc = 2 if heads % 2 == 0 else 1
    nx = heads // nc
    grid = Mesh(mesh.devices.reshape(NZ, NY, nx, nc), ("z", "y", "x", "c"))
    leaf, head = ("z", "y"), ("x", "c")
    return jax.shard_map(
        functools.partial(per_device, nx, nc),
        mesh=grid,
        in_specs=(
            P(leaf, None),
            P(leaf, head),
            P(leaf, head),
            P(leaf, head),
            P(leaf, None),
            P(None, head),
            P(None, head),
            P(None, head),
            P(head, None),
            P(),
        ),
        out_specs=(
            P(leaf, head),
            P(leaf, head),
            P(leaf, head),
            P(leaf, head),
            P(head, leaf),
        ),
        check_vma=False,
    )
```

time: 1570 us -> 212 us (0.14)
  waiting for transfers between devices: 1440 us -> 90.3 us
  starting transfers between devices: 0.55 us -> 40 us
  Pallas kernels: 0 us -> 39.4 us
  local copies, waits for them, and re-layouts: 50.9 us -> 14.6 us
  other arithmetic: 29.2 us -> 5.7 us
  matrix products: 26.1 us -> 4.98 us
    unnamed x14 -> x1, waiting for transfers between devices: 882 us -> 0.02 us
    reduce_scatter x2 -> x0, waiting for transfers between devices: 410 us -> none  [the longest x1 225 us: per_device(): lax.psum_scatter(value_dense.reshape(block_count * NODE_BLOCK_TOKENS, hea...]
    all_gather x2 -> x1, waiting for transfers between devices: 152 us -> 20.3 us  [per_device(): lax.all_gather(jnp.concatenate([keys, values], axis=1), 'z', axis=0, tile...]
    pallas_call x0 -> x2, Pallas kernels: none -> 39.4 us  [the longest x1 22.5 us: grads_call(): pl.pallas_call(grads_kernel, out_shape=(jax.ShapeDtypeStruct((NY, 2 * PAI...]
    ppermute x0 -> x13, waiting for transfers between devices: none -> 39.4 us  [shift(): return lax.ppermute(x, axis, [(i, (i + by) % size) for i in range(size)])]
    all_to_all x0 -> x2, waiting for transfers between devices: none -> 30.6 us  [the longest x1 17.6 us: per_device(): lax.all_to_all(col_part.reshape(NZ, rows, 2 * HEAD_WIDTH), 'z', 0, 0, til...]
    all_to_all x0 -> x2, starting transfers between devices: none -> 24.4 us  [the longest x1 20.1 us: per_device(): lax.all_to_all(col_part.reshape(NZ, rows, 2 * HEAD_WIDTH), 'z', 0, 0, til...]
    scatter-add x6 -> x0, other arithmetic: 23.2 us -> none  [the longest x3 12 us: per_device(): key_dense.at[guarded_rows]]
  transfers between devices with their start and end apart: 9 -> 16, of which waited for: 9 -> 13; matrix products, arithmetic and copies ran while one was open for 4% -> 6% of each run, Pallas kernels for 0% -> 0%
where the time goes in v1:
time: 212 us; the launch traced here: 209 us
  waiting for transfers between devices  90.3 us (43%)
  starting transfers between devices  40 us (19%)
  Pallas kernels  39.4 us (19%)
  local copies, waits for them, and re-layouts  14.6 us (7%)
  between operations  14.4 us (7%)
  other arithmetic  5.7 us (3%)
  matrix products  4.98 us (2%)
    ppermute x13, waiting for transfers between devices, shift(): return lax.ppermute(x, axis, [(i, (i + by) % size) for i in range(size)])  39.4 us
    pallas_call x1, Pallas kernels, grads_call(): pl.pallas_call(grads_kernel, out_shape=(jax.ShapeDtypeStruct((NY, 2 * PAI...  22.5 us
    all_gather x1, waiting for transfers between devices, per_device(): lax.all_gather(jnp.concatenate([keys, values], axis=1), 'z', axis=0, tile...  20.3 us
    all_to_all x1, starting transfers between devices, per_device(): lax.all_to_all(col_part.reshape(NZ, rows, 2 * HEAD_WIDTH), 'z', 0, 0, til...  20.1 us
    all_to_all x1, waiting for transfers between devices, per_device(): lax.all_to_all(col_part.reshape(NZ, rows, 2 * HEAD_WIDTH), 'z', 0, 0, til...  17.6 us
    pallas_call x1, Pallas kernels, stats_call(): pl.pallas_call(stats_kernel, out_shape=jax.ShapeDtypeStruct((3 * STAT_ROW...  16.9 us
    ppermute x13, starting transfers between devices, shift(): return lax.ppermute(x, axis, [(i, (i + by) % size) for i in range(size)])  15.6 us
    all_to_all x1, waiting for transfers between devices, per_device(): lax.all_to_all(parts, ('z', 'y'), 0, 0, tiled=True).astype(f32)  13 us
  transfers between devices with their start and end apart: 16, of which 13 were waited for; matrix products, arithmetic and copies ran while one was open for 6% of the time, Pallas kernels for 0%

profile of v1, /device:TPU:6, one launch (start us, length us, event | category | flops | bytes accessed | tf_op | source)
XLA Modules:
  0.0 209.4 jit_solution(23422973021198109)
XLA Ops:
  7.2 1.7 pad_maximum_fusion.3
  9.0 1.7 convolution_convert_fusion.3
  10.7 1.7 collective-permute-start
  12.4 2.9 %collective-permute-start.1 = (bf16[384,512]{1,0:T(8,128)(2,1)S(1)}, bf16[384,512]{1,0:T(8,128)(2,1)S(1)}, u32[]{:S(2)}, u32[]{:S(2)}) collective-permute-start(bf16[384,512]{1,0:T(8,128)(2,1)S(1)} %pad_maximum_fusion.2.qd0), channel_id=1, source_target_pairs={{0,16},{8,24},{16,0},{24,8},{1,17},{9,25},{17,1},{25,9},{2,18},{10... | collective-permute-start | bytes 1179656 | tf_op jit(solution)/shard_map/ppermute | solution.py:232
  15.3 1.3 collective-permute-start.2
  16.8 6.1 %collective-permute-done.qd1 = bf16[384,512]{1,0:T(8,128)(2,1)S(1)} collective-permute-done((bf16[384,512]{1,0:T(8,128)(2,1)S(1)}, bf16[384,512]{1,0:T(8,128)(2,1)S(1)}, u32[]{:S(2)}, u32[]{:S(2)}) %collective-permute-start) | collective-permute-done | bytes 393248 | tf_op jit(solution)/shard_map/ppermute | solution.py:232
  22.9 9.6 %collective-permute-done.1.qd2 = bf16[384,512]{1,0:T(8,128)(2,1)S(1)} collective-permute-done((bf16[384,512]{1,0:T(8,128)(2,1)S(1)}, bf16[384,512]{1,0:T(8,128)(2,1)S(1)}, u32[]{:S(2)}, u32[]{:S(2)}) %collective-permute-start.1) | collective-permute-done | bytes 393248 | tf_op jit(solution)/shard_map/ppermute | solution.py:232
  32.5 20.3 %all-gather.2.cloned.1.call-done.kv_ref = bf16[3072,256]{1,0:T(8,128)(2,1)} async-done(((bf16[384,256]{1,0:T(8,128)(2,1)}), bf16[3072,256]{1,0:T(8,128)(2,1)}) %all-gather.2.cloned.1.call-update) | async-done | bytes 1572880 | tf_op jit(solution)/shard_map/all_gather | solution.py:244
  52.8 1.4 copy-done.1
  54.2 16.9 %stats.1.st0 = f32[48,256]{1,0:T(8,128)S(1)} custom-call(s32[2]{0:T(128)S(1)} %pad_add_fusion.pos_ref, s32[96,16]{1,0:T(8,128)S(1)} %copy.28.anc_ref, bf16[3072,256]{1,0:T(8,128)(2,1)S(1)} %copy-done.1, bf16[384,512]{1,0:T(8,128)(2,1)S(1)} %pad_maximum_fusion.2.qd0, bf16[384,512]{1,0:T(8,128)(2,1)S(1)} %collective-permute-done.qd1, ...), custom_call_target="tpu_custom_call" | custom-call | tf_op jit(solution)/shard_map/stats/pallas_call | solution.py:190
  71.4 3.1 %collective-permute-start.5 = (f32[48,256]{1,0:T(8,128)S(1)}, f32[48,256]{1,0:T(8,128)S(1)}, u32[]{:S(2)}, u32[]{:S(2)}) collective-permute-start(f32[48,256]{1,0:T(8,128)S(1)} %stats.1.st0), channel_id=1, source_target_pairs={{0,24},{8,0},{16,8},{24,16},{1,25},{9,1},{17,9},{25,17},{2,26},{10... | collective-permute-start | bytes 147464 | tf_op jit(solution)/shard_map/ppermute | solution.py:232
  74.5 2.6 %collective-permute-done.3.st1 = f32[48,256]{1,0:T(8,128)S(1)} collective-permute-done((f32[48,256]{1,0:T(8,128)S(1)}, f32[48,256]{1,0:T(8,128)S(1)}, u32[]{:S(2)}, u32[]{:S(2)}) %collective-permute-start.3) | collective-permute-done | bytes 49184 | tf_op jit(solution)/shard_map/ppermute | solution.py:232
  77.1 0.9 collective-permute-done.5.st3
  78.0 1.0 copy-done.3
  79.8 22.5 %grads.1 = (bf16[4,512,384]{2,1,0:T(8,128)(2,1)S(1)}, bf16[3072,256]{1,0:T(8,128)(2,1)}) custom-call(s32[2]{0:T(128)S(1)} %pad_add_fusion.pos_ref, s32[96,16]{1,0:T(8,128)S(1)} %copy-done.5, bf16[3072,256]{1,0:T(8,128)(2,1)} %all-gather.2.cloned.1.call-done.kv_ref, bf16[384,512]{1,0:T(8,128)(2,1)S(1)} %pad_maximum_fusion.2.qd0, ...), custom_call_target="tpu_custom_call" | custom-call | tf_op jit(solution)/shard_map/grads/pallas_call | solution.py:207
  102.2 20.1 %all-to-all-start = ((bf16[8,384,256]{2,1,0:T(8,128)(2,1)}), bf16[8,384,256]{2,1,0:T(8,128)(2,1)}, u32[]{:S(2)}, u32[]{:S(2)}) async-start(bf16[8,384,256]{2,1,0:T(8,128)(2,1)} %bitcast.9), calls=%async_computation | async-start | bytes 3145728 | tf_op jit(solution)/shard_map/all_to_all | solution.py:265
  122.7 3.1 %collective-permute-start.8 = (bf16[512,384]{1,0:T(8,128)(2,1)S(1)}, bf16[512,384]{1,0:T(8,128)(2,1)S(1)}, u32[]{:S(2)}, u32[]{:S(2)}) collective-permute-start(bf16[512,384]{1,0:T(8,128)(2,1)S(1)} %get-tuple-element.14), channel_id=1, source_target_pairs={{0,24},{8,0},{16,8},{24,16},{1,25},{9,1},{17,9},{25,17},{2,26},{10... | collective-permute-start | bytes 1179656 | tf_op jit(solution)/shard_map/ppermute | solution.py:232
  125.8 12.0 %collective-permute-done.6 = bf16[512,384]{1,0:T(8,128)(2,1)S(1)} collective-permute-done((bf16[512,384]{1,0:T(8,128)(2,1)S(1)}, bf16[512,384]{1,0:T(8,128)(2,1)S(1)}, u32[]{:S(2)}, u32[]{:S(2)}) %collective-permute-start.6) | collective-permute-done | bytes 393248 | tf_op jit(solution)/shard_map/ppermute | solution.py:232
  139.9 17.6 %all-to-all-done = bf16[8,384,256]{2,1,0:T(8,128)(2,1)} async-done(((bf16[8,384,256]{2,1,0:T(8,128)(2,1)}), bf16[8,384,256]{2,1,0:T(8,128)(2,1)}, u32[]{:S(2)}, u32[]{:S(2)}) %all-to-all-start) | async-done | bytes 1572896 | tf_op jit(solution)/shard_map/all_to_all | solution.py:265
  157.5 1.7 reduce_sum.21
  160.4 1.6 copy.33
  162.0 4.3 %all-to-all-start.1 = ((bf16[32,32,768]{2,1,0:T(8,128)(2,1)}), bf16[32,32,768]{2,1,0:T(8,128)(2,1)S(1)}, u32[]{:S(2)}, u32[]{:S(2)}) async-start(bf16[32,32,768]{2,1,0:T(8,128)(2,1)} %bitcast.48), calls=%async_computation.1 | async-start | bytes 3145728 | tf_op jit(solution)/shard_map/all_to_all | solution.py:289
  168.1 0.8 copy-done.10
  169.3 1.6 convolution_add_fusion
  170.9 3.4 %reshape.39 = f32[384,2,512]{2,1,0:T(2,128)} reshape(f32[384,1024]{1,0:T(8,128)} %convolution_add_fusion) | data formatting | bytes 3145728 | tf_op jit(solution)/shard_map/reshape | solution.py:272
  174.3 2.2 %slice.70 = bf16[384,1,512]{2,1,0:T(2,128)(2,1)S(1)} slice(f32[384,2,512]{2,1,0:T(2,128)} %reshape.39), slice={[0:384], [1:2], [0:512]} | slice | bytes 786432 | tf_op jit(solution)/shard_map/slice | solution.py:275
  176.7 1.7 collective-permute-done.9
  179.2 2.4 %collective-permute-start.11 = (bf16[384,128]{1,0:T(8,128)(2,1)S(1)}, bf16[384,128]{1,0:T(8,128)(2,1)S(1)}, u32[]{:S(2)}, u32[]{:S(2)}) collective-permute-start(bf16[384,128]{1,0:T(8,128)(2,1)S(1)} %get-tuple-element.18), channel_id=1, source_target_pairs={{0,4},{2,6},{4,0},{6,2},{1,5},{3,7},{5,1},{7,3},{8,12},{10,14},{12... | collective-permute-start | bytes 294920 | tf_op jit(solution)/shard_map/ppermute | solution.py:232
  181.6 2.7 %collective-permute-done.10 = bf16[384,128]{1,0:T(8,128)(2,1)S(1)} collective-permute-done((bf16[384,128]{1,0:T(8,128)(2,1)S(1)}, bf16[384,128]{1,0:T(8,128)(2,1)S(1)}, u32[]{:S(2)}, u32[]{:S(2)}) %collective-permute-start.10) | collective-permute-done | bytes 98336 | tf_op jit(solution)/shard_map/ppermute | solution.py:232
  184.3 1.4 collective-permute-done.11
  185.7 1.7 collective-permute-done.12
  188.1 13.0 %all-to-all-done.1 = bf16[32,32,768]{2,1,0:T(8,128)(2,1)S(1)} async-done(((bf16[32,32,768]{2,1,0:T(8,128)(2,1)}), bf16[32,32,768]{2,1,0:T(8,128)(2,1)S(1)}, u32[]{:S(2)}, u32[]{:S(2)}) %all-to-all-start.1) | async-done | bytes 1572896 | tf_op jit(solution)/shard_map/all_to_all | solution.py:289
  (67 shorter events, 10.0 us)
Async XLA Ops:
  7.2 132.2 %copy-start = (bf16[384,1024]{1,0:T(8,128)(2,1)S(1)}, bf16[384,1024]{1,0:T(8,128)(2,1)}, u32[]{:S(2)}) copy-start(bf16[384,1024]{1,0:T(8,128)(2,1)} %param.14) | copy-start | bytes 2359300
  7.2 3.5 %copy-start.14 = (bf16[384,256]{1,0:T(8,128)(2,1)S(1)}, bf16[384,256]{1,0:T(8,128)(2,1)}, u32[]{:S(2)}) copy-start(bf16[384,256]{1,0:T(8,128)(2,1)} %param.15) | copy-start | bytes 589828
  7.2 9.4 %copy-start.15 = (s32[96,16]{0,1:T(8,128)S(1)}, s32[96,16]{0,1:T(8,128)}, u32[]{:S(2)}) copy-start(s32[96,16]{0,1:T(8,128)} %param.23) | copy-start | bytes 18436
  7.2 45.6 %all-gather.2.cloned.1.call-start = ((), (), s32[]{:S(2)}) async-start(), calls=%async_computation.2 | async-start | bytes 1769472 | tf_op jit(solution)/shard_map/all_gather | solution.py:244
  10.7 12.2 %collective-permute-start = (bf16[384,512]{1,0:T(8,128)(2,1)S(1)}, bf16[384,512]{1,0:T(8,128)(2,1)S(1)}, u32[]{:S(2)}, u32[]{:S(2)}) collective-permute-start(bf16[384,512]{1,0:T(8,128)(2,1)S(1)} %pad_maximum_fusion.2.qd0), channel_id=1, source_target_pairs={{0,8},{8,16},{16,24},{24,0},{1,9},{9,17},{17,25},{25,1},{2,10},{10... | collective-permute-start | bytes 1179656 | tf_op jit(solution)/shard_map/ppermute | solution.py:232
  12.4 20.2 %collective-permute-start.1 = (bf16[384,512]{1,0:T(8,128)(2,1)S(1)}, bf16[384,512]{1,0:T(8,128)(2,1)S(1)}, u32[]{:S(2)}, u32[]{:S(2)}) collective-permute-start(bf16[384,512]{1,0:T(8,128)(2,1)S(1)} %pad_maximum_fusion.2.qd0), channel_id=1, source_target_pairs={{0,16},{8,24},{16,0},{24,8},{1,17},{9,25},{17,1},{25,9},{2,18},{10... | collective-permute-start | bytes 1179656 | tf_op jit(solution)/shard_map/ppermute | solution.py:232
  15.3 17.3 %collective-permute-start.2 = (bf16[384,512]{1,0:T(8,128)(2,1)S(1)}, bf16[384,512]{1,0:T(8,128)(2,1)S(1)}, u32[]{:S(2)}, u32[]{:S(2)}) collective-permute-start(bf16[384,512]{1,0:T(8,128)(2,1)S(1)} %pad_maximum_fusion.2.qd0), channel_id=1, source_target_pairs={{0,24},{8,0},{16,8},{24,16},{1,25},{9,1},{17,9},{25,17},{2,26},{10... | collective-permute-start | bytes 1179656 | tf_op jit(solution)/shard_map/ppermute | solution.py:232
  16.7 54.5 %copy-start.4 = (s32[96,16]{1,0:T(8,128)}, s32[96,16]{1,0:T(8,128)S(1)}, u32[]{:S(2)}) copy-start(s32[96,16]{1,0:T(8,128)S(1)} %copy.28.anc_ref) | copy-start | bytes 18436
  32.5 38.7 %copy-start.2 = (bf16[384,512]{1,0:T(8,128)(2,1)}, bf16[384,512]{1,0:T(8,128)(2,1)S(1)}, u32[]{:S(2)}) copy-start(bf16[384,512]{1,0:T(8,128)(2,1)S(1)} %collective-permute-done.2.qd3) | copy-start | bytes 1179652
  52.8 1.4 copy-start.1
  71.2 5.9 %collective-permute-start.3 = (f32[48,256]{1,0:T(8,128)S(1)}, f32[48,256]{1,0:T(8,128)S(1)}, u32[]{:S(2)}, u32[]{:S(2)}) collective-permute-start(f32[48,256]{1,0:T(8,128)S(1)} %stats.1.st0), channel_id=1, source_target_pairs={{0,8},{8,16},{16,24},{24,0},{1,9},{9,17},{17,25},{25,1},{2,10},{10... | collective-permute-start | bytes 147464 | tf_op jit(solution)/shard_map/ppermute | solution.py:232
  71.3 5.8 %collective-permute-start.4 = (f32[48,256]{1,0:T(8,128)S(1)}, f32[48,256]{1,0:T(8,128)S(1)}, u32[]{:S(2)}, u32[]{:S(2)}) collective-permute-start(f32[48,256]{1,0:T(8,128)S(1)} %stats.1.st0), channel_id=1, source_target_pairs={{0,16},{8,24},{16,0},{24,8},{1,17},{9,25},{17,1},{25,9},{2,18},{10... | collective-permute-start | bytes 147464 | tf_op jit(solution)/shard_map/ppermute | solution.py:232
  71.4 6.6 %collective-permute-start.5 = (f32[48,256]{1,0:T(8,128)S(1)}, f32[48,256]{1,0:T(8,128)S(1)}, u32[]{:S(2)}, u32[]{:S(2)}) collective-permute-start(f32[48,256]{1,0:T(8,128)S(1)} %stats.1.st0), channel_id=1, source_target_pairs={{0,24},{8,0},{16,8},{24,16},{1,25},{9,1},{17,9},{25,17},{2,26},{10... | collective-permute-start | bytes 147464 | tf_op jit(solution)/shard_map/ppermute | solution.py:232
  78.0 1.0 copy-start.3
  79.0 0.8 copy-start.5
  102.2 55.2 %all-to-all-start = ((bf16[8,384,256]{2,1,0:T(8,128)(2,1)}), bf16[8,384,256]{2,1,0:T(8,128)(2,1)}, u32[]{:S(2)}, u32[]{:S(2)}) async-start(bf16[8,384,256]{2,1,0:T(8,128)(2,1)} %bitcast.9), calls=%async_computation | async-start | bytes 3145728 | tf_op jit(solution)/shard_map/all_to_all | solution.py:265
  122.4 16.2 %copy-start.6 = (bf16[384,1024]{1,0:T(8,128)(2,1)S(1)}, bf16[384,1024]{1,0:T(8,128)(2,1)}, u32[]{:S(2)}) copy-start(bf16[384,1024]{1,0:T(8,128)(2,1)} %param.18) | copy-start | bytes 2359300
  122.5 15.3 %collective-permute-start.6 = (bf16[512,384]{1,0:T(8,128)(2,1)S(1)}, bf16[512,384]{1,0:T(8,128)(2,1)S(1)}, u32[]{:S(2)}, u32[]{:S(2)}) collective-permute-start(bf16[512,384]{1,0:T(8,128)(2,1)S(1)} %get-tuple-element.13), channel_id=1, source_target_pairs={{0,8},{8,16},{16,24},{24,0},{1,9},{9,17},{17,25},{25,1},{2,10},{10... | collective-permute-start | bytes 1179656 | tf_op jit(solution)/shard_map/ppermute | solution.py:232
  122.6 15.2 %collective-permute-start.7 = (bf16[512,384]{1,0:T(8,128)(2,1)S(1)}, bf16[512,384]{1,0:T(8,128)(2,1)S(1)}, u32[]{:S(2)}, u32[]{:S(2)}) collective-permute-start(bf16[512,384]{1,0:T(8,128)(2,1)S(1)} %get-tuple-element.15), channel_id=1, source_target_pairs={{0,16},{8,24},{16,0},{24,8},{1,17},{9,25},{17,1},{25,9},{2,18},{10... | collective-permute-start | bytes 1179656 | tf_op jit(solution)/shard_map/ppermute | solution.py:232
  122.7 15.8 %collective-permute-start.8 = (bf16[512,384]{1,0:T(8,128)(2,1)S(1)}, bf16[512,384]{1,0:T(8,128)(2,1)S(1)}, u32[]{:S(2)}, u32[]{:S(2)}) collective-permute-start(bf16[512,384]{1,0:T(8,128)(2,1)S(1)} %get-tuple-element.14), channel_id=1, source_target_pairs={{0,24},{8,0},{16,8},{24,16},{1,25},{9,1},{17,9},{25,17},{2,26},{10... | collective-permute-start | bytes 1179656 | tf_op jit(solution)/shard_map/ppermute | solution.py:232
  138.6 0.8 copy-start.7
  162.0 4.4 %copy-start.12 = (bf16[1024,128]{1,0:T(8,128)(2,1)S(1)}, bf16[1024,128]{1,0:T(8,128)(2,1)}, u32[]{:S(2)}) copy-start(bf16[1024,128]{1,0:T(8,128)(2,1)} %param.21) | copy-start | bytes 786436
  162.0 4.4 %copy-start.13 = (bf16[1024,128]{1,0:T(8,128)(2,1)S(1)}, bf16[1024,128]{1,0:T(8,128)(2,1)}, u32[]{:S(2)}) copy-start(bf16[1024,128]{1,0:T(8,128)(2,1)} %param.20) | copy-start | bytes 786436
  162.0 39.1 %all-to-all-start.1 = ((bf16[32,32,768]{2,1,0:T(8,128)(2,1)}), bf16[32,32,768]{2,1,0:T(8,128)(2,1)S(1)}, u32[]{:S(2)}, u32[]{:S(2)}) async-start(bf16[32,32,768]{2,1,0:T(8,128)(2,1)} %bitcast.48), calls=%async_computation.1 | async-start | bytes 3145728 | tf_op jit(solution)/shard_map/all_to_all | solution.py:289
  166.3 1.0 copy-start.11
  168.0 0.9 copy-start.10
  168.0 1.3 copy-start.8
  176.5 1.9 slice-start
  176.6 1.8 collective-permute-start.9
  178.6 5.7 %collective-permute-start.10 = (bf16[384,128]{1,0:T(8,128)(2,1)S(1)}, bf16[384,128]{1,0:T(8,128)(2,1)S(1)}, u32[]{:S(2)}, u32[]{:S(2)}) collective-permute-start(bf16[384,128]{1,0:T(8,128)(2,1)S(1)} %get-tuple-element.16), channel_id=1, source_target_pairs={{0,2},{2,4},{4,6},{6,0},{1,3},{3,5},{5,7},{7,1},{8,10},{10,12},{12... | collective-permute-start | bytes 294920 | tf_op jit(solution)/shard_map/ppermute | solution.py:232
  179.2 6.5 %collective-permute-start.11 = (bf16[384,128]{1,0:T(8,128)(2,1)S(1)}, bf16[384,128]{1,0:T(8,128)(2,1)S(1)}, u32[]{:S(2)}, u32[]{:S(2)}) collective-permute-start(bf16[384,128]{1,0:T(8,128)(2,1)S(1)} %get-tuple-element.18), channel_id=1, source_target_pairs={{0,4},{2,6},{4,0},{6,2},{1,5},{3,7},{5,1},{7,3},{8,12},{10,14},{12... | collective-permute-start | bytes 294920 | tf_op jit(solution)/shard_map/ppermute | solution.py:232
  181.6 5.9 %collective-permute-start.12 = (bf16[384,128]{1,0:T(8,128)(2,1)S(1)}, bf16[384,128]{1,0:T(8,128)(2,1)S(1)}, u32[]{:S(2)}, u32[]{:S(2)}) collective-permute-start(bf16[384,128]{1,0:T(8,128)(2,1)S(1)} %get-tuple-element.17), channel_id=1, source_target_pairs={{0,6},{2,0},{4,2},{6,4},{1,7},{3,1},{5,3},{7,5},{8,14},{10,8},{12,... | collective-permute-start | bytes 294920 | tf_op jit(solution)/shard_map/ppermute | solution.py:232
  (1 other events, 0.7 us)
Sparse Core Ops, SparseCore 0:
  9.8 42.9 all-gather.1

commit v2 on v1

v2 whole, which is shorter than its diff:
```python
import functools
import math

import jax
import jax.numpy as jnp
from jax import lax
from jax.experimental import pallas as pl
from jax.experimental.pallas import tpu as pltpu
from jax.sharding import Mesh, PartitionSpec as P

HEAD_WIDTH = 128
BLOCK = 128
GROUP = 2
NZ, NY = 8, 4
DEV_BLOCKS = 3
ROW_BLOCKS = NY * DEV_BLOCKS
COL_BLOCKS = NZ * DEV_BLOCKS
PATH = 16
PAIR = GROUP * BLOCK
SCALE = HEAD_WIDTH ** (-0.5)
SCALE2 = SCALE * math.log2(math.e)
NEG = -1e30
STAT_ROWS = 16
SLOTS = 2
UNROLL = 2
GROUPS = 128
AT, SLOT, REACH, COUNT = 0, GROUPS, (1 + SLOTS) * GROUPS, (1 + 2 * SLOTS) * GROUPS
PLAN = COUNT + 128
VMEM_LIMIT = 48 * 1024 * 1024

f32 = jnp.float32
bf16 = jnp.bfloat16


def dot_nt(a, b):
    return lax.dot_general(a, b, (((1,), (1,)), ((), ())), preferred_element_type=f32)


def dot_nn(a, b):
    return jnp.dot(a, b, preferred_element_type=f32)


def prep_kernel(pos_ref, anc_ref, qd0, qd1, qd2, qd3, q_ref, d_ref, plan_ref):
    z, y = pos_ref[0], pos_ref[1]
    for s, qd in enumerate((qd0, qd1, qd2, qd3)):
        for r in range(DEV_BLOCKS):
            at = lax.rem(y - s + NY, NY) * DEV_BLOCKS + r
            rows = slice(r * BLOCK, (r + 1) * BLOCK)
            for h in range(GROUP):
                put = slice(h * BLOCK, (h + 1) * BLOCK)
                q_ref[at, put, :] = qd[rows, h * HEAD_WIDTH : (h + 1) * HEAD_WIDTH]
                d_ref[at, put, :] = qd[rows, PAIR + h * HEAD_WIDTH : PAIR + (h + 1) * HEAD_WIDTH]

    def close(group):
        for k in range(SLOTS):
            plan_ref[SLOT + k * GROUPS + group] = 0
            plan_ref[REACH + k * GROUPS + group] = -BLOCK
        plan_ref[AT + group] = 0

    def one_block(at, first):
        block = z * ROW_BLOCKS + at

        def one_key(j, count):
            c = anc_ref[block, j]
            hit = jnp.logical_and(c >= 0, lax.rem(lax.div(c, DEV_BLOCKS), NY) == y)
            group = first + lax.div(count, SLOTS)
            k = lax.rem(count, SLOTS)

            @pl.when(hit)
            def _():
                @pl.when(k == 0)
                def _():
                    close(group)
                    plan_ref[AT + group] = at

                slot = lax.div(c, ROW_BLOCKS) * DEV_BLOCKS + lax.rem(c, DEV_BLOCKS)
                plan_ref[SLOT + k * GROUPS + group] = slot
                plan_ref[REACH + k * GROUPS + group] = jnp.where(c == block, 0, BLOCK)

            return count + hit.astype(jnp.int32)

        count = lax.fori_loop(0, PATH, one_key, jnp.int32(0))
        return first + lax.div(count + SLOTS - 1, SLOTS)

    groups = lax.fori_loop(0, ROW_BLOCKS, one_block, jnp.int32(0))
    for u in range(UNROLL):
        close(groups + u)
    plan_ref[COUNT] = groups


def group_of(plan_ref, g):
    at = plan_ref[AT + g]
    slots = [plan_ref[SLOT + k * GROUPS + g] for k in range(SLOTS)]
    reach = [plan_ref[REACH + k * GROUPS + g] for k in range(SLOTS)]
    return at, slots, reach


def base2_scores(kv_ref, q, slots, reach):
    keys = jnp.concatenate([kv_ref[s, :, :HEAD_WIDTH] for s in slots], axis=0)
    s = dot_nt(keys, q) * SCALE2
    key_at = lax.broadcasted_iota(jnp.int32, (BLOCK, PAIR), 0)
    query_at = lax.rem(lax.broadcasted_iota(jnp.int32, (BLOCK, PAIR), 1), BLOCK)
    behind = key_at - query_at
    hide = jnp.concatenate([behind > r for r in reach], axis=0)
    return jnp.where(hide, NEG, s)


def value_dot(kv_ref, d, slots):
    return dot_nt(jnp.concatenate([kv_ref[s, :, HEAD_WIDTH:] for s in slots], axis=0), d)


def stats_kernel(plan_ref, kv_ref, q_ref, d_ref, out_ref):
    out_ref[0:STAT_ROWS, :] = jnp.full((STAT_ROWS, PAIR), NEG, f32)
    out_ref[STAT_ROWS:, :] = jnp.zeros((2 * STAT_ROWS, PAIR), f32)

    def step(i, _):
        done = []
        for u in range(UNROLL):
            at, slots, reach = group_of(plan_ref, i * UNROLL + u)
            s = base2_scores(kv_ref, q_ref[at], slots, reach)
            g = value_dot(kv_ref, d_ref[at], slots)
            m = jnp.max(s, axis=0, keepdims=True)
            p = jnp.exp2(s - m)
            done.append((at, m, jnp.sum(p, axis=0, keepdims=True), jnp.sum(p * g, axis=0, keepdims=True)))
        for at, m, total, dsum in done:
            rows = [pl.ds(n * STAT_ROWS + at, 1) for n in range(3)]
            before = out_ref[rows[0], :]
            top = jnp.maximum(before, m)
            old, new = jnp.exp2(before - top), jnp.exp2(m - top)
            out_ref[rows[0], :] = top
            out_ref[rows[1], :] = out_ref[rows[1], :] * old + total * new
            out_ref[rows[2], :] = out_ref[rows[2], :] * old + dsum * new
        return 0

    lax.fori_loop(0, lax.div(plan_ref[COUNT] + UNROLL - 1, UNROLL), step, 0)


def grads_kernel(
    pos_ref, plan_ref, kv_ref, kvt_ref, q_ref, d_ref, st0, st1, st2, st3,
    row_ref, col_ref,
    o_scr, dq_scr, dk_scr, dv_scr, lse_scr, delta_scr,
):
    y = pos_ref[1]
    for scr in (o_scr, dq_scr, dk_scr, dv_scr):
        def clear(i, _, scr=scr):
            scr[i] = jnp.zeros(scr.shape[1:], f32)
            return 0

        lax.fori_loop(0, scr.shape[0], clear, 0)

    tops = [st[0:STAT_ROWS, :] for st in (st0, st1, st2, st3)]
    m = functools.reduce(jnp.maximum, tops)
    factors = [jnp.exp2(t - m) for t in tops]
    total, dsum = (
        sum(st[n * STAT_ROWS : (n + 1) * STAT_ROWS, :] * f for st, f in zip((st0, st1, st2, st3), factors))
        for n in (1, 2)
    )
    lse_scr[...] = m + jnp.log2(total)
    delta_scr[...] = dsum / total

    def step(i, _):
        done = []
        for u in range(UNROLL):
            at, slots, reach = group_of(plan_ref, i * UNROLL + u)
            q, d = q_ref[at], d_ref[at]
            w = jnp.exp2(base2_scores(kv_ref, q, slots, reach) - lse_scr[pl.ds(at, 1), :])
            g = value_dot(kv_ref, d, slots)
            p = w.astype(bf16)
            ds = (w * (g - delta_scr[pl.ds(at, 1), :]) * SCALE).astype(bf16)
            kt = jnp.concatenate([kvt_ref[s, :HEAD_WIDTH, :] for s in slots], axis=1)
            vt = jnp.concatenate([kvt_ref[s, HEAD_WIDTH:, :] for s in slots], axis=1)
            done.append((at, slots, dot_nn(vt, p), dot_nn(kt, ds), dot_nn(ds, q), dot_nn(p, d)))
        for at, slots, o, dq, dk, dv in done:
            o_scr[at] += o
            dq_scr[at] += dq
            for k, slot in enumerate(slots):
                dk_scr[slot] += dk[k * BLOCK : (k + 1) * BLOCK]
                dv_scr[slot] += dv[k * BLOCK : (k + 1) * BLOCK]
        return 0

    lax.fori_loop(0, lax.div(plan_ref[COUNT] + UNROLL - 1, UNROLL), step, 0)

    def finish_row(t, _):
        for r in range(DEV_BLOCKS):
            at = lax.rem(y + t, NY) * DEV_BLOCKS + r
            cols = slice(r * BLOCK, (r + 1) * BLOCK)
            for h in range(GROUP):
                heads = slice(h * BLOCK, (h + 1) * BLOCK)
                rows = slice(h * HEAD_WIDTH, (h + 1) * HEAD_WIDTH)
                drows = slice(PAIR + h * HEAD_WIDTH, PAIR + (h + 1) * HEAD_WIDTH)
                row_ref[t, rows, cols] = o_scr[at, :, heads].astype(bf16)
                row_ref[t, drows, cols] = dq_scr[at, :, heads].astype(bf16)
        return 0

    lax.fori_loop(0, NY, finish_row, 0)

    def finish_col(c, _):
        col_ref[c, :, :HEAD_WIDTH] = dk_scr[c].astype(bf16)
        col_ref[c, :, HEAD_WIDTH:] = dv_scr[c].astype(bf16)
        return 0

    lax.fori_loop(0, COL_BLOCKS, finish_col, 0)


SMEM_SPEC = pl.BlockSpec(memory_space=pltpu.SMEM)
VMEM_SPEC = pl.BlockSpec(memory_space=pltpu.VMEM)
PARAMS = pltpu.CompilerParams(vmem_limit_bytes=VMEM_LIMIT)
STACK = jax.ShapeDtypeStruct((ROW_BLOCKS, PAIR, HEAD_WIDTH), bf16)


def prep_call(pos, anc, qds):
    return pl.pallas_call(
        prep_kernel,
        out_shape=(STACK, STACK, jax.ShapeDtypeStruct((PLAN,), jnp.int32)),
        in_specs=[SMEM_SPEC] * 2 + [VMEM_SPEC] * NY,
        out_specs=(VMEM_SPEC, VMEM_SPEC, SMEM_SPEC),
        compiler_params=PARAMS,
        name="prep",
    )(pos, anc, *qds)


def stats_call(plan, kv, q, d):
    return pl.pallas_call(
        stats_kernel,
        out_shape=jax.ShapeDtypeStruct((3 * STAT_ROWS, PAIR), f32),
        in_specs=[SMEM_SPEC] + [VMEM_SPEC] * 3,
        out_specs=VMEM_SPEC,
        compiler_params=PARAMS,
        name="stats",
    )(plan, kv, q, d)


def grads_call(pos, plan, kv, kvt, q, d, stats):
    return pl.pallas_call(
        grads_kernel,
        out_shape=(
            jax.ShapeDtypeStruct((NY, 2 * PAIR, DEV_BLOCKS * BLOCK), bf16),
            jax.ShapeDtypeStruct((COL_BLOCKS, BLOCK, 2 * HEAD_WIDTH), bf16),
        ),
        in_specs=[SMEM_SPEC] * 2 + [VMEM_SPEC] * 8,
        out_specs=(VMEM_SPEC, VMEM_SPEC),
        scratch_shapes=[
            pltpu.VMEM((ROW_BLOCKS, HEAD_WIDTH, PAIR), f32),
            pltpu.VMEM((ROW_BLOCKS, HEAD_WIDTH, PAIR), f32),
            pltpu.VMEM((COL_BLOCKS, BLOCK, HEAD_WIDTH), f32),
            pltpu.VMEM((COL_BLOCKS, BLOCK, HEAD_WIDTH), f32),
            pltpu.VMEM((STAT_ROWS, PAIR), f32),
            pltpu.VMEM((STAT_ROWS, PAIR), f32),
        ],
        compiler_params=PARAMS,
        name="grads",
    )(pos, plan, kv, kvt, q, d, *stats)


def shift(x, axis, size, by):
    return lax.ppermute(x, axis, [(i, (i + by) % size) for i in range(size)])


def per_device(
    nx, nc, normed_input, queries, keys, values, grad_out, query_weight, key_weight, value_weight, output_weight, ancestors
):
    z, y = lax.axis_index("z"), lax.axis_index("y")
    x, c = lax.axis_index("x"), lax.axis_index("c")
    rows = queries.shape[0]
    model = grad_out.shape[1]
    pos = jnp.stack([z, y]).astype(jnp.int32)

    kv = jnp.concatenate([keys, values], axis=1)
    kv = lax.all_to_all(jnp.broadcast_to(kv, (NZ,) + kv.shape), "z", 0, 0, tiled=True)
    kv = kv.reshape(COL_BLOCKS, BLOCK, 2 * HEAD_WIDTH)
    attn_grad = dot_nt(grad_out, output_weight).astype(bf16)
    mine = jnp.concatenate([queries, attn_grad], axis=1)
    qds = [mine] + [shift(mine, "y", NY, s) for s in range(1, NY)]

    heads = nx * nc
    width = model // heads

    def laid_out(w):
        w = w.reshape(nx, nc, width, w.shape[1])
        w = jnp.roll(jnp.roll(w, -x, axis=0), -c, axis=1)
        return w.transpose(1, 0, 2, 3).reshape(model, w.shape[3])

    wq = laid_out(query_weight)
    wkv = laid_out(jnp.concatenate([key_weight, value_weight], axis=1))

    part_rows = model // (NZ * NY)

    def from_y(t):
        t = t.reshape(NZ, NY, part_rows, t.shape[1])
        return jnp.roll(t, -y, axis=1).transpose(1, 0, 2, 3).reshape(model, t.shape[3])

    input_t = normed_input.T
    input_y, grad_y = from_y(input_t), from_y(grad_out.T)

    q_stack, d_stack, plan = prep_call(pos, ancestors, qds)
    own = stats_call(plan, kv, q_stack, d_stack)
    stats = [own] + [shift(own, "y", NY, s) for s in range(1, NY)]
    row_part, col_part = grads_call(pos, plan, kv, jnp.swapaxes(kv, 1, 2), q_stack, d_stack, stats)

    got = [shift(row_part[s], "y", NY, s) for s in range(1, NY)]
    col_got = lax.all_to_all(col_part.reshape(NZ, rows, 2 * HEAD_WIDTH), "z", 0, 0, tiled=True)
    row_sum = sum((g.astype(f32) for g in got), row_part[0].astype(f32)).astype(bf16)
    attn_t, dq_t = row_sum[:PAIR], row_sum[PAIR:]

    qo_part = jnp.concatenate([dot_nt(input_y, dq_t).astype(bf16), dot_nt(grad_y, attn_t).astype(bf16)], axis=1)
    qo_part = qo_part.reshape(NY, model // NY, 2 * PAIR)
    qo = qo_part[0].astype(f32)
    for s in range(1, NY):
        qo = qo + shift(qo_part[s], "y", NY, s).astype(f32)
    qo = lax.all_to_all(qo.astype(bf16).reshape(NZ, part_rows, 2 * PAIR), "z", 0, 0, tiled=True)
    qo = jnp.sum(qo.astype(f32), axis=0)

    dkv = jnp.sum(col_got.astype(f32), axis=0).astype(bf16)
    kv_part = dot_nn(input_t, dkv).astype(bf16).reshape(NZ * NY, part_rows, 2 * HEAD_WIDTH)
    kv_grad = jnp.sum(lax.all_to_all(kv_part, ("z", "y"), 0, 0, tiled=True).astype(f32), axis=0)

    part = lax.dot_general(dq_t, wq, (((0,), (1,)), ((), ())), preferred_element_type=f32)
    part = part + dot_nt(dkv, wkv)
    side = nx * width
    keep = part[:, :side]
    for s in range(1, nc):
        keep = keep + shift(part[:, s * side : (s + 1) * side].astype(bf16), "c", nc, s).astype(f32)
    input_grad = keep[:, :width]
    for s in range(1, nx):
        piece = keep[:, s * width : (s + 1) * width].astype(bf16)
        input_grad = input_grad + shift(piece, "x", nx, s).astype(f32)
    input_grad = input_grad.astype(bf16)
    return (
        input_grad,
        qo[:, :PAIR],
        kv_grad[:, :HEAD_WIDTH],
        kv_grad[:, HEAD_WIDTH:],
        qo[:, PAIR:].T,
    )


def solution(mesh):
    heads = mesh.shape["head"]
    nc = 2 if heads % 2 == 0 else 1
    nx = heads // nc
    grid = Mesh(mesh.devices.reshape(NZ, NY, nx, nc), ("z", "y", "x", "c"))
    leaf, head = ("z", "y"), ("x", "c")
    return jax.shard_map(
        functools.partial(per_device, nx, nc),
        mesh=grid,
        in_specs=(
            P(leaf, None),
            P(leaf, head),
            P(leaf, head),
            P(leaf, head),
            P(leaf, None),
            P(None, head),
            P(None, head),
            P(None, head),
            P(head, None),
            P(),
        ),
        out_specs=(
            P(leaf, head),
            P(leaf, head),
            P(leaf, head),
            P(leaf, head),
            P(head, leaf),
        ),
        check_vma=False,
    )
```

time: 212 us -> 170 us (0.80)
  waiting for transfers between devices: 90.3 us -> 64.3 us
  Pallas kernels: 39.4 us -> 24.5 us
  between operations: 14.4 us -> 0.93 us
  starting transfers between devices: 40 us -> 49.1 us
  local copies, waits for them, and re-layouts: 14.6 us -> 19.9 us
  matrix products: 4.98 us -> 2.61 us
  other arithmetic: 5.7 us -> 7.85 us
    all_gather x1 -> x0, waiting for transfers between devices: 20.3 us -> none  [per_device(): lax.all_gather(jnp.concatenate([keys, values], axis=1), 'z', axis=0, tile...]
    all_to_all x1, waiting for transfers between devices: 17.6 us -> 0.01 us  [per_device(): lax.all_to_all(col_part.reshape(NZ, rows, 2 * HEAD_WIDTH), 'z', 0, 0, til...]
    all_to_all x1 -> x3, starting transfers between devices: 4.28 us -> 20.4 us  [the longest x1 8.6 us: per_device(): lax.all_to_all(jnp.broadcast_to(kv, (NZ,) + kv.shape), 'z', 0, 0, tiled=T...]
    pallas_call x1, Pallas kernels: 16.9 us -> 5.01 us  [stats_call(): pl.pallas_call(stats_kernel, out_shape=jax.ShapeDtypeStruct((3 * STAT_ROW...]
    all_to_all x1, starting transfers between devices: 20.1 us -> 9.23 us  [per_device(): lax.all_to_all(col_part.reshape(NZ, rows, 2 * HEAD_WIDTH), 'z', 0, 0, til...]
    pallas_call x1, Pallas kernels: 22.5 us -> 13 us  [grads_call(): pl.pallas_call(grads_kernel, out_shape=(jax.ShapeDtypeStruct((NY, 2 * PAI...]
    all_to_all x1 -> x3, waiting for transfers between devices: 13 us -> 20.8 us  [the longest x1 7.78 us: per_device(): lax.all_to_all(jnp.broadcast_to(kv, (NZ,) + kv.shape), 'z', 0, 0, tiled=T...]
    pallas_call x0 -> x1, Pallas kernels: none -> 6.47 us  [prep_call(): pl.pallas_call(prep_kernel, out_shape=(STACK, STACK, jax.ShapeDtypeStruct...]
  transfers between devices with their start and end apart: 16 -> 20, of which waited for: 13 -> 15; matrix products, arithmetic and copies ran while one was open for 6% -> 12% of each run, Pallas kernels for 0% -> 4%
where the time goes in v2:
time: 170 us; the launch traced here: 169 us
  waiting for transfers between devices  64.3 us (38%)
  starting transfers between devices  49.1 us (29%)
  Pallas kernels  24.5 us (14%)
  local copies, waits for them, and re-layouts  19.9 us (12%)
  other arithmetic  7.85 us (5%)
  matrix products  2.61 us (2%)
    ppermute x16, waiting for transfers between devices, shift(): return lax.ppermute(x, axis, [(i, (i + by) % size) for i in range(size)])  43.4 us
    ppermute x16, starting transfers between devices, shift(): return lax.ppermute(x, axis, [(i, (i + by) % size) for i in range(size)])  19.5 us
    pallas_call x1, Pallas kernels, grads_call(): pl.pallas_call(grads_kernel, out_shape=(jax.ShapeDtypeStruct((NY, 2 * PAI...  13 us
    unnamed x41, local copies, waits for them, and re-layouts  10.8 us
    all_to_all x1, starting transfers between devices, per_device(): lax.all_to_all(col_part.reshape(NZ, rows, 2 * HEAD_WIDTH), 'z', 0, 0, til...  9.23 us
    all_to_all x1, starting transfers between devices, per_device(): lax.all_to_all(jnp.broadcast_to(kv, (NZ,) + kv.shape), 'z', 0, 0, tiled=T...  8.6 us
    all_to_all x1, waiting for transfers between devices, per_device(): lax.all_to_all(jnp.broadcast_to(kv, (NZ,) + kv.shape), 'z', 0, 0, tiled=T...  7.78 us
    all_to_all x1, waiting for transfers between devices, per_device(): lax.all_to_all(kv_part, ('z', 'y'), 0, 0, tiled=True).astype(f32)  7.38 us
  transfers between devices with their start and end apart: 20, of which 15 were waited for; matrix products, arithmetic and copies ran while one was open for 12% of the time, Pallas kernels for 4%

profile of v2, /device:TPU:6, one launch (start us, length us, event | category | flops | bytes accessed | tf_op | source)
XLA Modules:
  0.0 169.1 jit_solution(14672456317036851208)
XLA Ops:
  1.7 1.3 broadcast_in_dim.3
  3.0 8.6 %all-to-all-start = ((bf16[8,384,256]{2,1,0:T(8,128)(2,1)}), bf16[8,384,256]{2,1,0:T(8,128)(2,1)S(1)}, u32[]{:S(2)}, u32[]{:S(2)}) async-start(bf16[8,384,256]{2,1,0:T(8,128)(2,1)} %broadcast_in_dim.3), calls=%async_computation | async-start | bytes 3145728 | tf_op jit(solution)/shard_map/all_to_all | solution.py:269
  12.0 1.7 collective-permute-start
  13.7 2.9 %collective-permute-start.1 = (bf16[384,512]{1,0:T(8,128)(2,1)S(1)}, bf16[384,512]{1,0:T(8,128)(2,1)S(1)}, u32[]{:S(2)}, u32[]{:S(2)}) collective-permute-start(bf16[384,512]{1,0:T(8,128)(2,1)S(1)} %pad_maximum_fusion.1.qd0), channel_id=1, source_target_pairs={{0,16},{8,24},{16,0},{24,8},{1,17},{9,25},{17,1},{25,9},{2,18},{10... | collective-permute-start | bytes 1179656 | tf_op jit(solution)/shard_map/ppermute | solution.py:256
  16.6 1.3 collective-permute-start.2
  18.1 6.1 %collective-permute-done.qd1 = bf16[384,512]{1,0:T(8,128)(2,1)S(1)} collective-permute-done((bf16[384,512]{1,0:T(8,128)(2,1)S(1)}, bf16[384,512]{1,0:T(8,128)(2,1)S(1)}, u32[]{:S(2)}, u32[]{:S(2)}) %collective-permute-start) | collective-permute-done | bytes 393248 | tf_op jit(solution)/shard_map/ppermute | solution.py:256
  25.0 8.6 %collective-permute-done.1.qd2 = bf16[384,512]{1,0:T(8,128)(2,1)S(1)} collective-permute-done((bf16[384,512]{1,0:T(8,128)(2,1)S(1)}, bf16[384,512]{1,0:T(8,128)(2,1)S(1)}, u32[]{:S(2)}, u32[]{:S(2)}) %collective-permute-start.1) | collective-permute-done | bytes 393248 | tf_op jit(solution)/shard_map/ppermute | solution.py:256
  36.3 6.5 %prep.1 = (bf16[12,256,128]{2,1,0:T(8,128)(2,1)S(1)}, bf16[12,256,128]{2,1,0:T(8,128)(2,1)S(1)}, s32[768]{0:T(1024)S(1)}) custom-call(s32[2]{0:T(128)S(1)} %pad_add_fusion.pos_ref, s32[96,16]{1,0:T(8,128)S(1)} %copy.29.anc_ref, bf16[384,512]{1,0:T(8,128)(2,1)S(1)} %pad_maximum_fusion.1.qd0, bf16[384,512]{1,0:T(8,128)(2,1)S(1)} %copy-done.6, ...), custom_call_target="tpu_custom_call" | custom-call | tf_op jit(solution)/shard_map/prep/pallas_call | solution.py:212
  43.7 7.8 %all-to-all-done = bf16[8,384,256]{2,1,0:T(8,128)(2,1)S(1)} async-done(((bf16[8,384,256]{2,1,0:T(8,128)(2,1)}), bf16[8,384,256]{2,1,0:T(8,128)(2,1)S(1)}, u32[]{:S(2)}, u32[]{:S(2)}) %all-to-all-start) | async-done | bytes 1572896 | tf_op jit(solution)/shard_map/all_to_all | solution.py:269
  51.5 1.7 copy-done.3
  53.2 5.0 %stats.1.st0 = f32[48,256]{1,0:T(8,128)S(1)} custom-call(s32[768]{0:T(1024)S(1)} %get-tuple-element.13.plan_ref, bf16[24,128,256]{2,1,0:T(8,128)(2,1)S(1)} %bitcast.49, bf16[12,256,128]{2,1,0:T(8,128)(2,1)S(1)} %get-tuple-element.14.q_ref, bf16[12,256,128]{2,1,0:T(8,128)(2,1)S(1)} %copy-done.3), custom_call_target="tpu_custom_call" | custom-call | tf_op jit(solution)/shard_map/stats/pallas_call | solution.py:223
  59.2 2.5 %collective-permute-start.5 = (f32[48,256]{1,0:T(8,128)S(1)}, f32[48,256]{1,0:T(8,128)S(1)}, u32[]{:S(2)}, u32[]{:S(2)}) collective-permute-start(f32[48,256]{1,0:T(8,128)S(1)} %stats.1.st0), channel_id=1, source_target_pairs={{0,24},{8,0},{16,8},{24,16},{1,25},{9,1},{17,9},{25,17},{2,26},{10... | collective-permute-start | bytes 147464 | tf_op jit(solution)/shard_map/ppermute | solution.py:256
  61.7 1.6 copy.30
  65.0 1.1 copy-done.4
  66.1 13.0 %grads.1 = (bf16[4,512,384]{2,1,0:T(8,128)(2,1)S(1)}, bf16[24,128,256]{2,1,0:T(8,128)(2,1)}) custom-call(s32[2]{0:T(128)S(1)} %pad_add_fusion.pos_ref, s32[768]{0:T(1024)S(1)} %get-tuple-element.13.plan_ref, bf16[24,128,256]{2,1,0:T(8,128)(2,1)} %bitcast.51, bf16[24,256,128]{2,1,0:T(8,128)(2,1)} %bitcast.52, ...), custom_call_target="tpu_custom_call" | custom-call | tf_op jit(solution)/shard_map/grads/pallas_call | solution.py:234
  79.2 9.2 %all-to-all-start.1 = ((bf16[8,384,256]{2,1,0:T(8,128)(2,1)}), bf16[8,384,256]{2,1,0:T(8,128)(2,1)}, u32[]{:S(2)}, u32[]{:S(2)}) async-start(bf16[8,384,256]{2,1,0:T(8,128)(2,1)} %bitcast.11), calls=%async_computation.1 | async-start | bytes 3145728 | tf_op jit(solution)/shard_map/all_to_all | solution.py:301
  88.4 1.1 copy.35
  89.5 2.3 %copy.33 = bf16[384,1024]{0,1:T(8,128)(2,1)} copy(bf16[384,1024]{1,0:T(8,128)(2,1)} %param.16) | data formatting | bytes 1572864 | tf_op args[0]
  92.9 3.2 %collective-permute-start.8 = (bf16[512,384]{1,0:T(8,128)(2,1)S(1)}, bf16[512,384]{1,0:T(8,128)(2,1)}, u32[]{:S(2)}, u32[]{:S(2)}) collective-permute-start(bf16[512,384]{1,0:T(8,128)(2,1)S(1)} %get-tuple-element.21), channel_id=1, source_target_pairs={{0,24},{8,0},{16,8},{24,16},{1,25},{9,1},{17,9},{25,17},{2,26},{10... | collective-permute-start | bytes 1179656 | tf_op jit(solution)/shard_map/ppermute | solution.py:256
  99.1 10.9 %collective-permute-done.6 = bf16[512,384]{1,0:T(8,128)(2,1)} collective-permute-done((bf16[512,384]{1,0:T(8,128)(2,1)}, bf16[512,384]{1,0:T(8,128)(2,1)}, u32[]{:S(2)}, u32[]{:S(2)}) %collective-permute-start.6) | collective-permute-done | bytes 393248 | tf_op jit(solution)/shard_map/ppermute | solution.py:256
  110.7 1.4 fusion.7
  113.6 3.3 %collective-permute-start.14 = (bf16[256,512]{0,1:T(8,128)(2,1)S(1)}, bf16[256,512]{0,1:T(8,128)(2,1)S(1)}, u32[]{:S(2)}, u32[]{:S(2)}) collective-permute-start(bf16[256,512]{0,1:T(8,128)(2,1)S(1)} %get-tuple-element.25), channel_id=1, source_target_pairs={{0,16},{8,24},{16,0},{24,8},{1,17},{9,25},{17,1},{25,9},{2,18},{10... | collective-permute-start | bytes 786440 | tf_op jit(solution)/shard_map/ppermute | solution.py:256
  117.6 4.2 %collective-permute-done.13 = bf16[256,512]{0,1:T(8,128)(2,1)S(1)} collective-permute-done((bf16[256,512]{0,1:T(8,128)(2,1)S(1)}, bf16[256,512]{0,1:T(8,128)(2,1)S(1)}, u32[]{:S(2)}, u32[]{:S(2)}) %collective-permute-start.13) | collective-permute-done | bytes 262176 | tf_op jit(solution)/shard_map/ppermute | solution.py:256
  121.8 6.1 %collective-permute-done.14 = bf16[256,512]{0,1:T(8,128)(2,1)S(1)} collective-permute-done((bf16[256,512]{0,1:T(8,128)(2,1)S(1)}, bf16[256,512]{0,1:T(8,128)(2,1)S(1)}, u32[]{:S(2)}, u32[]{:S(2)}) %collective-permute-start.14) | collective-permute-done | bytes 262176 | tf_op jit(solution)/shard_map/ppermute | solution.py:256
  129.0 6.6 %all-to-all-start.2 = ((bf16[8,32,512]{2,1,0:T(8,128)(2,1)}), bf16[8,32,512]{2,1,0:T(8,128)(2,1)S(1)}, u32[]{:S(2)}, u32[]{:S(2)}) async-start(bf16[8,32,512]{2,1,0:T(8,128)(2,1)} %bitcast.23), calls=%async_computation.2 | async-start | bytes 524288 | tf_op jit(solution)/shard_map/all_to_all | solution.py:310
  135.6 1.7 reduce_sum.30
  140.4 5.7 %all-to-all-done.2 = bf16[8,32,512]{2,1,0:T(8,128)(2,1)S(1)} async-done(((bf16[8,32,512]{2,1,0:T(8,128)(2,1)}), bf16[8,32,512]{2,1,0:T(8,128)(2,1)S(1)}, u32[]{:S(2)}, u32[]{:S(2)}) %all-to-all-start.2) | async-done | bytes 262176 | tf_op jit(solution)/shard_map/all_to_all | solution.py:310
  146.1 5.2 %all-to-all-start.3 = ((bf16[32,32,256]{2,1,0:T(8,128)(2,1)}), bf16[32,32,256]{2,1,0:T(8,128)(2,1)S(1)}, u32[]{:S(2)}, u32[]{:S(2)}) async-start(bf16[32,32,256]{2,1,0:T(8,128)(2,1)} %bitcast.25), calls=%async_computation.3 | async-start | bytes 1048576 | tf_op jit(solution)/shard_map/all_to_all | solution.py:315
  152.1 2.4 %collective-permute-start.11 = (bf16[384,128]{1,0:T(8,128)(2,1)S(1)}, bf16[384,128]{1,0:T(8,128)(2,1)S(1)}, u32[]{:S(2)}, u32[]{:S(2)}) collective-permute-start(bf16[384,128]{1,0:T(8,128)(2,1)S(1)} %get-tuple-element.28), channel_id=1, source_target_pairs={{0,4},{2,6},{4,0},{6,2},{1,5},{3,7},{5,1},{7,3},{8,12},{10,14},{12... | collective-permute-start | bytes 294920 | tf_op jit(solution)/shard_map/ppermute | solution.py:256
  156.3 2.5 %collective-permute-done.11 = bf16[384,128]{1,0:T(8,128)(2,1)S(1)} collective-permute-done((bf16[384,128]{1,0:T(8,128)(2,1)S(1)}, bf16[384,128]{1,0:T(8,128)(2,1)S(1)}, u32[]{:S(2)}, u32[]{:S(2)}) %collective-permute-start.11) | collective-permute-done | bytes 98336 | tf_op jit(solution)/shard_map/ppermute | solution.py:256
  158.8 1.6 collective-permute-done.12
  161.1 7.4 %all-to-all-done.3 = bf16[32,32,256]{2,1,0:T(8,128)(2,1)S(1)} async-done(((bf16[32,32,256]{2,1,0:T(8,128)(2,1)}), bf16[32,32,256]{2,1,0:T(8,128)(2,1)S(1)}, u32[]{:S(2)}, u32[]{:S(2)}) %all-to-all-start.3) | async-done | bytes 524320 | tf_op jit(solution)/shard_map/all_to_all | solution.py:315
  (87 shorter events, 23.6 us)
Async XLA Ops:
  0.6 10.9 %copy-start = (bf16[256,1024]{1,0:T(8,128)(2,1)S(1)}, bf16[256,1024]{1,0:T(8,128)(2,1)}, u32[]{:S(2)}) copy-start(bf16[256,1024]{1,0:T(8,128)(2,1)} %param.24) | copy-start | bytes 1572868
  2.9 8.6 %copy-start.9 = (bf16[384,1024]{1,0:T(8,128)(2,1)S(1)}, bf16[384,1024]{1,0:T(8,128)(2,1)}, u32[]{:S(2)}) copy-start(bf16[384,1024]{1,0:T(8,128)(2,1)} %param.20) | copy-start | bytes 2359300
  3.0 9.0 %copy-start.17 = (bf16[384,256]{1,0:T(8,128)(2,1)S(1)}, bf16[384,256]{1,0:T(8,128)(2,1)}, u32[]{:S(2)}) copy-start(bf16[384,256]{1,0:T(8,128)(2,1)} %param.17) | copy-start | bytes 589828
  3.0 48.6 %all-to-all-start = ((bf16[8,384,256]{2,1,0:T(8,128)(2,1)}), bf16[8,384,256]{2,1,0:T(8,128)(2,1)S(1)}, u32[]{:S(2)}, u32[]{:S(2)}) async-start(bf16[8,384,256]{2,1,0:T(8,128)(2,1)} %broadcast_in_dim.3), calls=%async_computation | async-start | bytes 3145728 | tf_op jit(solution)/shard_map/all_to_all | solution.py:269
  11.6 6.4 %copy-start.18 = (s32[96,16]{0,1:T(8,128)S(1)}, s32[96,16]{0,1:T(8,128)}, u32[]{:S(2)}) copy-start(s32[96,16]{0,1:T(8,128)} %param.25) | copy-start | bytes 18436
  12.0 12.2 %collective-permute-start = (bf16[384,512]{1,0:T(8,128)(2,1)S(1)}, bf16[384,512]{1,0:T(8,128)(2,1)S(1)}, u32[]{:S(2)}, u32[]{:S(2)}) collective-permute-start(bf16[384,512]{1,0:T(8,128)(2,1)S(1)} %pad_maximum_fusion.1.qd0), channel_id=1, source_target_pairs={{0,8},{8,16},{16,24},{24,0},{1,9},{9,17},{17,25},{25,1},{2,10},{10... | collective-permute-start | bytes 1179656 | tf_op jit(solution)/shard_map/ppermute | solution.py:256
  13.7 19.9 %collective-permute-start.1 = (bf16[384,512]{1,0:T(8,128)(2,1)S(1)}, bf16[384,512]{1,0:T(8,128)(2,1)S(1)}, u32[]{:S(2)}, u32[]{:S(2)}) collective-permute-start(bf16[384,512]{1,0:T(8,128)(2,1)S(1)} %pad_maximum_fusion.1.qd0), channel_id=1, source_target_pairs={{0,16},{8,24},{16,0},{24,8},{1,17},{9,25},{17,1},{25,9},{2,18},{10... | collective-permute-start | bytes 1179656 | tf_op jit(solution)/shard_map/ppermute | solution.py:256
  16.6 17.7 %collective-permute-start.2 = (bf16[384,512]{1,0:T(8,128)(2,1)S(1)}, bf16[384,512]{1,0:T(8,128)(2,1)}, u32[]{:S(2)}, u32[]{:S(2)}) collective-permute-start(bf16[384,512]{1,0:T(8,128)(2,1)S(1)} %pad_maximum_fusion.1.qd0), channel_id=1, source_target_pairs={{0,24},{8,0},{16,8},{24,16},{1,25},{9,1},{17,9},{25,17},{2,26},{10... | collective-permute-start | bytes 1179656 | tf_op jit(solution)/shard_map/ppermute | solution.py:256
  51.5 10.2 %copy-start.1 = (bf16[8,384,256]{2,1,0:T(8,128)(2,1)}, bf16[8,384,256]{2,1,0:T(8,128)(2,1)S(1)}, u32[]{:S(2)}) copy-start(bf16[8,384,256]{2,1,0:T(8,128)(2,1)S(1)} %all-to-all-done) | copy-start | bytes 4718596
  51.5 1.7 copy-start.3
  58.2 5.4 %collective-permute-start.3 = (f32[48,256]{1,0:T(8,128)S(1)}, f32[48,256]{1,0:T(8,128)S(1)}, u32[]{:S(2)}, u32[]{:S(2)}) collective-permute-start(f32[48,256]{1,0:T(8,128)S(1)} %stats.1.st0), channel_id=1, source_target_pairs={{0,8},{8,16},{16,24},{24,0},{1,9},{9,17},{17,25},{25,1},{2,10},{10... | collective-permute-start | bytes 147464 | tf_op jit(solution)/shard_map/ppermute | solution.py:256
  58.7 5.6 %collective-permute-start.4 = (f32[48,256]{1,0:T(8,128)S(1)}, f32[48,256]{1,0:T(8,128)S(1)}, u32[]{:S(2)}, u32[]{:S(2)}) collective-permute-start(f32[48,256]{1,0:T(8,128)S(1)} %stats.1.st0), channel_id=1, source_target_pairs={{0,16},{8,24},{16,0},{24,8},{1,17},{9,25},{17,1},{25,9},{2,18},{10... | collective-permute-start | bytes 147464 | tf_op jit(solution)/shard_map/ppermute | solution.py:256
  59.2 5.8 %collective-permute-start.5 = (f32[48,256]{1,0:T(8,128)S(1)}, f32[48,256]{1,0:T(8,128)S(1)}, u32[]{:S(2)}, u32[]{:S(2)}) collective-permute-start(f32[48,256]{1,0:T(8,128)S(1)} %stats.1.st0), channel_id=1, source_target_pairs={{0,24},{8,0},{16,8},{24,16},{1,25},{9,1},{17,9},{25,17},{2,26},{10... | collective-permute-start | bytes 147464 | tf_op jit(solution)/shard_map/ppermute | solution.py:256
  79.2 9.2 %copy-start.10 = (bf16[384,1024]{1,0:T(8,128)(2,1)S(1)}, bf16[384,1024]{1,0:T(8,128)(2,1)}, u32[]{:S(2)}) copy-start(bf16[384,1024]{1,0:T(8,128)(2,1)} %param.20) | copy-start | bytes 2359300
  79.2 49.8 %all-to-all-start.1 = ((bf16[8,384,256]{2,1,0:T(8,128)(2,1)}), bf16[8,384,256]{2,1,0:T(8,128)(2,1)}, u32[]{:S(2)}, u32[]{:S(2)}) async-start(bf16[8,384,256]{2,1,0:T(8,128)(2,1)} %bitcast.11), calls=%async_computation.1 | async-start | bytes 3145728 | tf_op jit(solution)/shard_map/all_to_all | solution.py:301
  91.8 4.3 %copy-start.13 = (bf16[384,1024]{0,1:T(8,128)(2,1)S(1)}, bf16[384,1024]{0,1:T(8,128)(2,1)}, u32[]{:S(2)}) copy-start(bf16[384,1024]{0,1:T(8,128)(2,1)} %copy.35) | copy-start | bytes 2359300
  91.8 4.3 %copy-start.14 = (bf16[384,1024]{0,1:T(8,128)(2,1)S(1)}, bf16[384,1024]{0,1:T(8,128)(2,1)}, u32[]{:S(2)}) copy-start(bf16[384,1024]{0,1:T(8,128)(2,1)} %copy.33) | copy-start | bytes 2359300
  92.9 17.1 %collective-permute-start.6 = (bf16[512,384]{1,0:T(8,128)(2,1)}, bf16[512,384]{1,0:T(8,128)(2,1)}, u32[]{:S(2)}, u32[]{:S(2)}) collective-permute-start(bf16[512,384]{1,0:T(8,128)(2,1)} %get-tuple-element.20), channel_id=1, source_target_pairs={{0,8},{8,16},{16,24},{24,0},{1,9},{9,17},{17,25},{25,1},{2,10},{10... | collective-permute-start | bytes 1179656 | tf_op jit(solution)/shard_map/ppermute | solution.py:256
  92.9 17.1 %collective-permute-start.7 = (bf16[512,384]{1,0:T(8,128)(2,1)}, bf16[512,384]{1,0:T(8,128)(2,1)}, u32[]{:S(2)}, u32[]{:S(2)}) collective-permute-start(bf16[512,384]{1,0:T(8,128)(2,1)} %get-tuple-element.22), channel_id=1, source_target_pairs={{0,16},{8,24},{16,0},{24,8},{1,17},{9,25},{17,1},{25,9},{2,18},{10... | collective-permute-start | bytes 1179656 | tf_op jit(solution)/shard_map/ppermute | solution.py:256
  92.9 17.8 %collective-permute-start.8 = (bf16[512,384]{1,0:T(8,128)(2,1)S(1)}, bf16[512,384]{1,0:T(8,128)(2,1)}, u32[]{:S(2)}, u32[]{:S(2)}) collective-permute-start(bf16[512,384]{1,0:T(8,128)(2,1)S(1)} %get-tuple-element.21), channel_id=1, source_target_pairs={{0,24},{8,0},{16,8},{24,16},{1,25},{9,1},{17,9},{25,17},{2,26},{10... | collective-permute-start | bytes 1179656 | tf_op jit(solution)/shard_map/ppermute | solution.py:256
  99.1 13.5 %copy-start.12 = (bf16[4,8,32,384]{3,2,1,0:T(8,128)(2,1)S(1)}, bf16[4,8,32,384]{3,2,1,0:T(8,128)(2,1)}, u32[]{:S(2)}) copy-start(bf16[4,8,32,384]{3,2,1,0:T(8,128)(2,1)} %copy.34) | copy-start | bytes 2359300
  112.6 4.4 %copy-start.15 = (bf16[1024,256]{1,0:T(8,128)(2,1)S(1)}, bf16[1024,256]{1,0:T(8,128)(2,1)}, u32[]{:S(2)}) copy-start(bf16[1024,256]{1,0:T(8,128)(2,1)} %param.21) | copy-start | bytes 1572868
  113.1 8.7 %collective-permute-start.13 = (bf16[256,512]{0,1:T(8,128)(2,1)S(1)}, bf16[256,512]{0,1:T(8,128)(2,1)S(1)}, u32[]{:S(2)}, u32[]{:S(2)}) collective-permute-start(bf16[256,512]{0,1:T(8,128)(2,1)S(1)} %get-tuple-element.23), channel_id=1, source_target_pairs={{0,8},{8,16},{16,24},{24,0},{1,9},{9,17},{17,25},{25,1},{2,10},{10... | collective-permute-start | bytes 786440 | tf_op jit(solution)/shard_map/ppermute | solution.py:256
  113.6 14.3 %collective-permute-start.14 = (bf16[256,512]{0,1:T(8,128)(2,1)S(1)}, bf16[256,512]{0,1:T(8,128)(2,1)S(1)}, u32[]{:S(2)}, u32[]{:S(2)}) collective-permute-start(bf16[256,512]{0,1:T(8,128)(2,1)S(1)} %get-tuple-element.25), channel_id=1, source_target_pairs={{0,16},{8,24},{16,0},{24,8},{1,17},{9,25},{17,1},{25,9},{2,18},{10... | collective-permute-start | bytes 786440 | tf_op jit(solution)/shard_map/ppermute | solution.py:256
  117.0 11.0 %collective-permute-start.15 = (bf16[256,512]{0,1:T(8,128)(2,1)S(1)}, bf16[256,512]{0,1:T(8,128)(2,1)S(1)}, u32[]{:S(2)}, u32[]{:S(2)}) collective-permute-start(bf16[256,512]{0,1:T(8,128)(2,1)S(1)} %get-tuple-element.24), channel_id=1, source_target_pairs={{0,24},{8,0},{16,8},{24,16},{1,25},{9,1},{17,9},{25,17},{2,26},{10... | collective-permute-start | bytes 786440 | tf_op jit(solution)/shard_map/ppermute | solution.py:256
  129.0 17.1 %all-to-all-start.2 = ((bf16[8,32,512]{2,1,0:T(8,128)(2,1)}), bf16[8,32,512]{2,1,0:T(8,128)(2,1)S(1)}, u32[]{:S(2)}, u32[]{:S(2)}) async-start(bf16[8,32,512]{2,1,0:T(8,128)(2,1)} %bitcast.23), calls=%async_computation.2 | async-start | bytes 524288 | tf_op jit(solution)/shard_map/all_to_all | solution.py:310
  137.7 1.3 copy-start.11
  139.0 12.4 %collective-permute-start.9 = (bf16[384,512]{1,0:T(8,128)(2,1)}, bf16[384,512]{1,0:T(8,128)(2,1)S(1)}, u32[]{:S(2)}, u32[]{:S(2)}) collective-permute-start(bf16[384,512]{1,0:T(8,128)(2,1)} %slice.146), channel_id=1, source_target_pairs={{0,1},{1,0},{2,3},{3,2},{4,5},{5,4},{6,7},{7,6},{8,9},{9,8},{10,11... | collective-permute-start | bytes 1179656 | tf_op jit(solution)/shard_map/ppermute | solution.py:256
  146.1 22.3 %all-to-all-start.3 = ((bf16[32,32,256]{2,1,0:T(8,128)(2,1)}), bf16[32,32,256]{2,1,0:T(8,128)(2,1)S(1)}, u32[]{:S(2)}, u32[]{:S(2)}) async-start(bf16[32,32,256]{2,1,0:T(8,128)(2,1)} %bitcast.25), calls=%async_computation.3 | async-start | bytes 1048576 | tf_op jit(solution)/shard_map/all_to_all | solution.py:315
  151.6 4.7 %collective-permute-start.10 = (bf16[384,128]{1,0:T(8,128)(2,1)S(1)}, bf16[384,128]{1,0:T(8,128)(2,1)S(1)}, u32[]{:S(2)}, u32[]{:S(2)}) collective-permute-start(bf16[384,128]{1,0:T(8,128)(2,1)S(1)} %get-tuple-element.26), channel_id=1, source_target_pairs={{0,2},{2,4},{4,6},{6,0},{1,3},{3,5},{5,7},{7,1},{8,10},{10,12},{12... | collective-permute-start | bytes 294920 | tf_op jit(solution)/shard_map/ppermute | solution.py:256
  152.1 6.6 %collective-permute-start.11 = (bf16[384,128]{1,0:T(8,128)(2,1)S(1)}, bf16[384,128]{1,0:T(8,128)(2,1)S(1)}, u32[]{:S(2)}, u32[]{:S(2)}) collective-permute-start(bf16[384,128]{1,0:T(8,128)(2,1)S(1)} %get-tuple-element.28), channel_id=1, source_target_pairs={{0,4},{2,6},{4,0},{6,2},{1,5},{3,7},{5,1},{7,3},{8,12},{10,14},{12... | collective-permute-start | bytes 294920 | tf_op jit(solution)/shard_map/ppermute | solution.py:256
  154.5 5.8 %collective-permute-start.12 = (bf16[384,128]{1,0:T(8,128)(2,1)S(1)}, bf16[384,128]{1,0:T(8,128)(2,1)S(1)}, u32[]{:S(2)}, u32[]{:S(2)}) collective-permute-start(bf16[384,128]{1,0:T(8,128)(2,1)S(1)} %get-tuple-element.27), channel_id=1, source_target_pairs={{0,6},{2,0},{4,2},{6,4},{1,7},{3,1},{5,3},{7,5},{8,14},{10,8},{12,... | collective-permute-start | bytes 294920 | tf_op jit(solution)/shard_map/ppermute | solution.py:256
  (7 other events, 6.7 us)

commit v3 on v2

v3 whole, which is shorter than its diff:
```python
import functools
import math

import jax
import jax.numpy as jnp
from jax import lax
from jax.experimental import pallas as pl
from jax.experimental.pallas import tpu as pltpu
from jax.sharding import Mesh, PartitionSpec as P

HEAD_WIDTH = 128
BLOCK = 128
GROUP = 2
NZ, NY = 8, 4
DEV_BLOCKS = 3
ROW_BLOCKS = NY * DEV_BLOCKS
COL_BLOCKS = NZ * DEV_BLOCKS
PATH = 16
PAIR = GROUP * BLOCK
SCALE = HEAD_WIDTH ** (-0.5)
SCALE2 = SCALE * math.log2(math.e)
NEG = -1e30
STAT_ROWS = 16
SLOTS = 2
UNROLL = 4
ENTRIES = 256
AT, SLOT, REACH, COUNT = 0, ENTRIES, 2 * ENTRIES, 3 * ENTRIES
PLAN = COUNT + 128

f32 = jnp.float32
bf16 = jnp.bfloat16


def dot_nt(a, b):
    return lax.dot_general(a, b, (((1,), (1,)), ((), ())), preferred_element_type=f32)


def dot_nn(a, b):
    return jnp.dot(a, b, preferred_element_type=f32)


def start_copies(pairs, sems, first=0):
    copies = [pltpu.make_async_copy(src, dst, sems.at[first + i]) for i, (src, dst) in enumerate(pairs)]
    for copy in copies:
        copy.start()
    return copies


def copy_all(pairs, sems):
    for copy in start_copies(pairs, sems):
        copy.wait()


def start_kernel(query_any, key_any, value_any, grad_any, weight_any, qd_ref, kv_ref, grad_ref, weight_ref, sems):
    copies = start_copies(
        (
            (grad_any, grad_ref),
            (weight_any, weight_ref),
            (key_any, kv_ref.at[:, pl.ds(0, HEAD_WIDTH)]),
            (value_any, kv_ref.at[:, pl.ds(HEAD_WIDTH, HEAD_WIDTH)]),
            (query_any, qd_ref.at[:, pl.ds(0, PAIR)]),
        ),
        sems,
    )
    copies[0].wait()
    copies[1].wait()
    qd_ref[:, PAIR:] = dot_nt(grad_ref[...], weight_ref[...]).astype(bf16)
    for copy in copies[2:]:
        copy.wait()


def stack_kernel(own, before, after, top, bottom, out_ref, sems):
    y = lax.axis_index("y")
    pairs = []

    def put(src, src_row, back, row, count):
        at = lax.rem(y - back + NY, NY) * DEV_BLOCKS + row // BLOCK
        for k in range(2):
            for h in range(GROUP):
                src_cols = pl.ds(k * PAIR + h * HEAD_WIDTH, HEAD_WIDTH)
                dst = out_ref.at[at, pl.ds(h * BLOCK + row % BLOCK, count), pl.ds(k * HEAD_WIDTH, HEAD_WIDTH)]
                pairs.append((src.at[pl.ds(src_row, count), src_cols], dst))

    half = BLOCK // 2
    for src, back in ((own, 0), (before, 1), (after, 3)):
        for r in range(DEV_BLOCKS):
            put(src, r * BLOCK, back, r * BLOCK, BLOCK)
    put(top, 0, 2, 0, BLOCK)
    put(top, BLOCK, 2, BLOCK, half)
    put(bottom, 0, 2, BLOCK + half, half)
    put(bottom, half, 2, 2 * BLOCK, BLOCK)
    copy_all(pairs, sems)


def plan_kernel(anc_ref, plan_ref):
    z, y = lax.axis_index("z"), lax.axis_index("y")

    def put(e, at, slot, reach):
        plan_ref[AT + e] = at
        plan_ref[SLOT + e] = slot
        plan_ref[REACH + e] = reach

    def one_block(at, first):
        block = z * ROW_BLOCKS + at

        def one_key(j, e):
            c = anc_ref[j, block]
            device = lax.div(c, DEV_BLOCKS)
            row = lax.div(device, NY)
            hit = jnp.logical_and(c >= 0, device - row * NY == y)
            slot = row * DEV_BLOCKS + c - device * DEV_BLOCKS
            put(e, at, slot, jnp.where(c == block, 0, BLOCK))
            return e + hit.astype(jnp.int32)

        e = lax.fori_loop(0, PATH, one_key, first, unroll=True)
        put(e, at, 0, -BLOCK)
        return e + lax.rem(e, SLOTS)

    end = lax.fori_loop(0, ROW_BLOCKS, one_block, jnp.int32(0))
    for u in range(SLOTS * UNROLL):
        put(end + u, 0, 0, -BLOCK)
    plan_ref[COUNT] = lax.div(end, SLOTS)


def group_of(plan_ref, g):
    slots = [plan_ref[SLOT + SLOTS * g + k] for k in range(SLOTS)]
    reach = [plan_ref[REACH + SLOTS * g + k] for k in range(SLOTS)]
    return plan_ref[AT + SLOTS * g], slots, reach


def base2_scores(kv_ref, q, slots, reach):
    keys = jnp.concatenate([kv_ref[s, :, :HEAD_WIDTH] for s in slots], axis=0)
    s = dot_nt(keys, q) * SCALE2
    key_at = lax.broadcasted_iota(jnp.int32, (BLOCK, PAIR), 0)
    query_at = lax.rem(lax.broadcasted_iota(jnp.int32, (BLOCK, PAIR), 1), BLOCK)
    behind = key_at - query_at
    hide = jnp.concatenate([behind > r for r in reach], axis=0)
    return jnp.where(hide, NEG, s)


def value_dot(kv_ref, d, slots):
    return dot_nt(jnp.concatenate([kv_ref[s, :, HEAD_WIDTH:] for s in slots], axis=0), d)


def stats_kernel(plan_any, *refs):
    pieces, (qd_any, out_ref, kv_ref, qd_ref, plan_ref, sems) = refs[:9], refs[9:]
    z = lax.axis_index("z")

    def slots_of(back):
        return pl.ds(lax.rem(z - back + NZ, NZ) * DEV_BLOCKS, DEV_BLOCKS)

    pairs = [(qd_any, qd_ref), (plan_any, plan_ref)]
    for piece, back in zip(pieces[:7], (0, 1, 2, 3, 5, 6, 7)):
        pairs.append((piece, kv_ref.at[slots_of(back)]))
    far = lax.rem(z + NZ // 2, NZ) * DEV_BLOCKS
    half = BLOCK // 2
    pairs.append((pieces[7].at[0:1], kv_ref.at[pl.ds(far, 1)]))
    pairs.append((pieces[7].at[1, pl.ds(0, half)], kv_ref.at[far + 1, pl.ds(0, half)]))
    pairs.append((pieces[8].at[0, pl.ds(half, half)], kv_ref.at[far + 1, pl.ds(half, half)]))
    pairs.append((pieces[8].at[1:2], kv_ref.at[pl.ds(far + 2, 1)]))
    copy_all(pairs, sems)
    out_ref[0:STAT_ROWS, :] = jnp.full((STAT_ROWS, PAIR), NEG, f32)
    out_ref[STAT_ROWS:, :] = jnp.zeros((2 * STAT_ROWS, PAIR), f32)

    def step(i, _):
        done = []
        for u in range(UNROLL):
            at, slots, reach = group_of(plan_ref, i * UNROLL + u)
            s = base2_scores(kv_ref, qd_ref[at, :, :HEAD_WIDTH], slots, reach)
            g = value_dot(kv_ref, qd_ref[at, :, HEAD_WIDTH:], slots)
            m = jnp.max(s, axis=0, keepdims=True)
            p = jnp.exp2(s - m)
            done.append((at, m, jnp.sum(p, axis=0, keepdims=True), jnp.sum(p * g, axis=0, keepdims=True)))
        for at, m, total, dsum in done:
            rows = [pl.ds(n * STAT_ROWS + at, 1) for n in range(3)]
            before = out_ref[rows[0], :]
            top = jnp.maximum(before, m)
            old, new = jnp.exp2(before - top), jnp.exp2(m - top)
            out_ref[rows[0], :] = top
            out_ref[rows[1], :] = out_ref[rows[1], :] * old + total * new
            out_ref[rows[2], :] = out_ref[rows[2], :] * old + dsum * new
        return 0

    lax.fori_loop(0, lax.div(plan_ref[COUNT] + UNROLL - 1, UNROLL), step, 0)


def grads_kernel(
    plan_any, kv_any, kvt_any, qd_any, st0, st1, st2, st3,
    row0, row1, row2, row3, col_any,
    o_scr, dq_scr, dk_scr, dv_scr, lse_scr, delta_scr,
    kv_ref, kvt_ref, qd_ref, plan_ref, row_scr, col_scr, sems,
):
    y = lax.axis_index("y")
    pairs = ((kv_any, kv_ref), (kvt_any, kvt_ref), (qd_any, qd_ref), (plan_any, plan_ref))
    copies = start_copies(pairs, sems)
    for scr in (o_scr, dq_scr, dk_scr, dv_scr):
        def clear(i, _, scr=scr):
            scr[i] = jnp.zeros(scr.shape[1:], f32)
            return 0

        lax.fori_loop(0, scr.shape[0], clear, 0)

    tops = [st[0:STAT_ROWS, :] for st in (st0, st1, st2, st3)]
    m = functools.reduce(jnp.maximum, tops)
    factors = [jnp.exp2(t - m) for t in tops]
    total, dsum = (
        sum(st[n * STAT_ROWS : (n + 1) * STAT_ROWS, :] * f for st, f in zip((st0, st1, st2, st3), factors))
        for n in (1, 2)
    )
    lse_scr[...] = m + jnp.log2(total)
    delta_scr[...] = dsum / total
    for copy in copies:
        copy.wait()

    def step(i, _):
        done = []
        for u in range(UNROLL):
            at, slots, reach = group_of(plan_ref, i * UNROLL + u)
            q, d = qd_ref[at, :, :HEAD_WIDTH], qd_ref[at, :, HEAD_WIDTH:]
            w = jnp.exp2(base2_scores(kv_ref, q, slots, reach) - lse_scr[pl.ds(at, 1), :])
            g = value_dot(kv_ref, d, slots)
            p = w.astype(bf16)
            ds = (w * (g - delta_scr[pl.ds(at, 1), :]) * SCALE).astype(bf16)
            kt = jnp.concatenate([kvt_ref[s, :HEAD_WIDTH, :] for s in slots], axis=1)
            vt = jnp.concatenate([kvt_ref[s, HEAD_WIDTH:, :] for s in slots], axis=1)
            done.append((at, slots, dot_nn(vt, p), dot_nn(kt, ds), dot_nn(ds, q), dot_nn(p, d)))
        for at, slots, o, dq, dk, dv in done:
            o_scr[at] += o
            dq_scr[at] += dq
            for k, slot in enumerate(slots):
                dk_scr[slot] += dk[k * BLOCK : (k + 1) * BLOCK]
                dv_scr[slot] += dv[k * BLOCK : (k + 1) * BLOCK]
        return 0

    lax.fori_loop(0, lax.div(plan_ref[COUNT] + UNROLL - 1, UNROLL), step, 0)

    copies = []
    for n in range(NZ):
        for c in range(n * DEV_BLOCKS, (n + 1) * DEV_BLOCKS):
            col_scr[c, :, :HEAD_WIDTH] = dk_scr[c].astype(bf16)
            col_scr[c, :, HEAD_WIDTH:] = dv_scr[c].astype(bf16)
        part = pl.ds(n * DEV_BLOCKS, DEV_BLOCKS)
        copies += start_copies([(col_scr.at[part], col_any.at[part])], sems, 4 + n)
    for t, row_ref in enumerate((row0, row1, row2, row3)):
        for r in range(DEV_BLOCKS):
            at = lax.rem(y + t, NY) * DEV_BLOCKS + r
            cols = slice(r * BLOCK, (r + 1) * BLOCK)
            for h in range(GROUP):
                heads = slice(h * BLOCK, (h + 1) * BLOCK)
                rows = slice(h * HEAD_WIDTH, (h + 1) * HEAD_WIDTH)
                drows = slice(PAIR + h * HEAD_WIDTH, PAIR + (h + 1) * HEAD_WIDTH)
                row_scr[t, rows, cols] = o_scr[at, :, heads].astype(bf16)
                row_scr[t, drows, cols] = dq_scr[at, :, heads].astype(bf16)
        copies += start_copies([(row_scr.at[t], row_ref)], sems, 4 + NZ + t)
    for copy in copies:
        copy.wait()


def turn_kernel(kv_ref, out_ref):
    def one(c, _):
        for k in range(2):
            cols = slice(k * HEAD_WIDTH, (k + 1) * HEAD_WIDTH)
            out_ref[c, cols, :] = kv_ref[c, :, cols].T
        return 0

    lax.fori_loop(0, COL_BLOCKS, one, 0, unroll=4)


def scatter_rows(part_ref, cols, value):
    y = lax.axis_index("y")
    step = value.shape[0] // (NZ * NY)
    value = value.astype(bf16)
    for i in range(NZ * NY):
        n, t = divmod(i, NY)
        part_ref[lax.rem(t - y + NY, NY), n * step : (n + 1) * step, cols] = value[i * step : (i + 1) * step]


def model_rows(i, nx, nc, width):
    head = lax.rem(lax.axis_index("x") + i % nx, nx) * nc + lax.rem(lax.axis_index("c") + i // nx, nc)
    return pl.ds(pl.multiple_of(head * width, width), width)


def rows_kernel(
    nx, nc, row0, row1, row2, row3, input_any, grad_any, wq_any, part_any, back_any, turned_any,
    got, input_ref, grad_ref, wq_ref, part_ref, back_ref, turned_ref, sems,
):
    pairs = [(row, got.at[t]) for t, row in enumerate((row0, row1, row2, row3))]
    pairs += [(input_any, input_ref), (grad_any, grad_ref), (wq_any, wq_ref)]
    copies = start_copies(pairs, sems)
    for copy in copies:
        copy.wait()
    turned_ref[...] = input_ref[...].T
    copies = start_copies([(turned_ref, turned_any)], sems, 7)
    o = sum(got[t, :PAIR, :].astype(f32) for t in range(NY)).astype(bf16)
    dq = sum(got[t, PAIR:, :].astype(f32) for t in range(NY)).astype(bf16)
    scatter_rows(part_ref, slice(0, PAIR), dot_nt(turned_ref[...], dq))
    scatter_rows(part_ref, slice(PAIR, 2 * PAIR), dot_nt(grad_ref[...].T, o))
    copies += start_copies([(part_ref, part_any)], sems, 8)
    width = wq_ref.shape[0] // (nx * nc)
    for i in range(nx * nc):
        back_ref[i * width : (i + 1) * width, :] = dot_nn(wq_ref[model_rows(i, nx, nc, width), :], dq)
    copies += start_copies([(back_ref, back_any)], sems, 9)
    for copy in copies:
        copy.wait()


def cols_kernel(
    nx, nc, got_any, turned_any, wk_any, wv_any, back_any, part_ref, send_ref, keep_ref,
    got_ref, turned_ref, wk_ref, wv_ref, back_ref, sems,
):
    pairs = [(got_any, got_ref), (turned_any, turned_ref), (wk_any, wk_ref), (wv_any, wv_ref), (back_any, back_ref)]
    copies = start_copies(pairs, sems)
    copies[0].wait()
    d = sum(got_ref[t].astype(f32) for t in range(NZ)).astype(bf16)
    copies[1].wait()
    scatter_rows(part_ref, slice(0, 2 * HEAD_WIDTH), dot_nn(turned_ref[...], d))
    for copy in copies[2:]:
        copy.wait()
    width = wk_ref.shape[0] // (nx * nc)
    for i in range(nx * nc):
        rows = model_rows(i, nx, nc, width)
        w = jnp.concatenate([wk_ref[rows, :], wv_ref[rows, :]], axis=1)
        part = back_ref[i * width : (i + 1) * width, :] + dot_nt(w, d)
        if i < nx:
            keep_ref[i * width : (i + 1) * width, :] = part
        else:
            send_ref[(i - nx) * width : (i - nx + 1) * width, :] = part.astype(bf16)


SMEM_SPEC = pl.BlockSpec(memory_space=pltpu.SMEM)
VMEM_SPEC = pl.BlockSpec(memory_space=pltpu.VMEM)
HBM_SPEC = pl.BlockSpec(memory_space=pltpu.HBM)


def vmem(mib):
    return pltpu.CompilerParams(vmem_limit_bytes=mib * 1024 * 1024)


STACK = jax.ShapeDtypeStruct((ROW_BLOCKS, PAIR, 2 * HEAD_WIDTH), bf16)


def start_call(queries, keys, values, grad_out, output_weight):
    tokens = queries.shape[0]
    return pl.pallas_call(
        start_kernel,
        out_shape=(
            jax.ShapeDtypeStruct((tokens, 2 * PAIR), bf16),
            jax.ShapeDtypeStruct((tokens, 2 * HEAD_WIDTH), bf16),
        ),
        in_specs=[HBM_SPEC] * 5,
        out_specs=(VMEM_SPEC,) * 2,
        scratch_shapes=[
            pltpu.VMEM(grad_out.shape, bf16),
            pltpu.VMEM(output_weight.shape, bf16),
            pltpu.SemaphoreType.DMA((5,)),
        ],
        compiler_params=vmem(54),
        name="start",
    )(queries, keys, values, grad_out, output_weight)


def plan_call(anc):
    return pl.pallas_call(
        plan_kernel,
        out_shape=jax.ShapeDtypeStruct((PLAN,), jnp.int32),
        in_specs=[SMEM_SPEC],
        out_specs=SMEM_SPEC,
        name="plan",
    )(anc)


def stack_call(qds):
    return pl.pallas_call(
        stack_kernel,
        out_shape=STACK,
        in_specs=[HBM_SPEC] * 5,
        out_specs=HBM_SPEC,
        scratch_shapes=[pltpu.SemaphoreType.DMA((2 * GROUP * (3 * DEV_BLOCKS + 4),))],
        compiler_params=vmem(4),
        name="stack",
    )(*qds)


def stats_call(plan, pieces, qd):
    return pl.pallas_call(
        stats_kernel,
        out_shape=(
            jax.ShapeDtypeStruct((3 * STAT_ROWS, PAIR), f32),
            jax.ShapeDtypeStruct((COL_BLOCKS, BLOCK, 2 * HEAD_WIDTH), bf16),
        ),
        in_specs=[HBM_SPEC] * 11,
        out_specs=(VMEM_SPEC, VMEM_SPEC),
        scratch_shapes=[
            pltpu.VMEM(STACK.shape, bf16),
            pltpu.SMEM((PLAN,), jnp.int32),
            pltpu.SemaphoreType.DMA((13,)),
        ],
        compiler_params=vmem(12),
        name="stats",
    )(plan, *pieces, qd)


def grads_call(plan, kv, kvt, qd, stats):
    return pl.pallas_call(
        grads_kernel,
        out_shape=(
            *[jax.ShapeDtypeStruct((2 * PAIR, DEV_BLOCKS * BLOCK), bf16)] * NY,
            jax.ShapeDtypeStruct((COL_BLOCKS, BLOCK, 2 * HEAD_WIDTH), bf16),
        ),
        in_specs=[HBM_SPEC] * 4 + [VMEM_SPEC] * 4,
        out_specs=(HBM_SPEC,) * 5,
        scratch_shapes=[
            pltpu.VMEM((ROW_BLOCKS, HEAD_WIDTH, PAIR), f32),
            pltpu.VMEM((ROW_BLOCKS, HEAD_WIDTH, PAIR), f32),
            pltpu.VMEM((COL_BLOCKS, BLOCK, HEAD_WIDTH), f32),
            pltpu.VMEM((COL_BLOCKS, BLOCK, HEAD_WIDTH), f32),
            pltpu.VMEM((STAT_ROWS, PAIR), f32),
            pltpu.VMEM((STAT_ROWS, PAIR), f32),
            pltpu.VMEM((COL_BLOCKS, BLOCK, 2 * HEAD_WIDTH), bf16),
            pltpu.VMEM((COL_BLOCKS, 2 * HEAD_WIDTH, BLOCK), bf16),
            pltpu.VMEM(STACK.shape, bf16),
            pltpu.SMEM((PLAN,), jnp.int32),
            pltpu.VMEM((NY, 2 * PAIR, DEV_BLOCKS * BLOCK), bf16),
            pltpu.VMEM((COL_BLOCKS, BLOCK, 2 * HEAD_WIDTH), bf16),
            pltpu.SemaphoreType.DMA((4 + NZ + NY,)),
        ],
        compiler_params=vmem(54),
        name="grads",
    )(plan, kv, kvt, qd, *stats)


def turn_call(kv):
    return pl.pallas_call(
        turn_kernel,
        out_shape=jax.ShapeDtypeStruct((COL_BLOCKS, 2 * HEAD_WIDTH, BLOCK), bf16),
        in_specs=[VMEM_SPEC],
        out_specs=VMEM_SPEC,
        compiler_params=vmem(8),
        name="turn",
    )(kv)


def shift(x, axis, size, by):
    return lax.ppermute(x, axis, [(i, (i + by) % size) for i in range(size)])


def rows_call(nx, nc, got, normed_input, grad_out, query_weight):
    tokens, model = normed_input.shape
    return pl.pallas_call(
        functools.partial(rows_kernel, nx, nc),
        out_shape=(
            jax.ShapeDtypeStruct((NY, model // NY, 2 * PAIR), bf16),
            jax.ShapeDtypeStruct((model, tokens), f32),
            jax.ShapeDtypeStruct((model, tokens), bf16),
        ),
        in_specs=[HBM_SPEC] * 7,
        out_specs=(HBM_SPEC,) * 3,
        scratch_shapes=[
            pltpu.VMEM((NY, 2 * PAIR, tokens), bf16),
            pltpu.VMEM(normed_input.shape, bf16),
            pltpu.VMEM(normed_input.shape, bf16),
            pltpu.VMEM(query_weight.shape, bf16),
            pltpu.VMEM((NY, model // NY, 2 * PAIR), bf16),
            pltpu.VMEM((model, tokens), f32),
            pltpu.VMEM((model, tokens), bf16),
            pltpu.SemaphoreType.DMA((10,)),
        ],
        compiler_params=vmem(54),
        name="rows",
    )(*got, normed_input, grad_out, query_weight)


def cols_call(nx, nc, got, turned, key_weight, value_weight, back):
    model, tokens = turned.shape
    side = model // nc
    return pl.pallas_call(
        functools.partial(cols_kernel, nx, nc),
        out_shape=(
            jax.ShapeDtypeStruct((NY, model // NY, 2 * HEAD_WIDTH), bf16),
            jax.ShapeDtypeStruct((max(model - side, side), tokens), bf16),
            jax.ShapeDtypeStruct((side, tokens), f32),
        ),
        in_specs=[HBM_SPEC] * 5,
        out_specs=(VMEM_SPEC,) * 3,
        scratch_shapes=[
            pltpu.VMEM(got.shape, bf16),
            pltpu.VMEM(turned.shape, bf16),
            pltpu.VMEM(key_weight.shape, bf16),
            pltpu.VMEM(value_weight.shape, bf16),
            pltpu.VMEM(back.shape, f32),
            pltpu.SemaphoreType.DMA((5,)),
        ],
        compiler_params=vmem(20),
        name="cols",
    )(got, turned, key_weight, value_weight, back)


def ring_gather(own):
    up, down = [own], [own]
    for _ in range(3):
        up.append(shift(up[-1], "z", NZ, 1))
        down.append(shift(down[-1], "z", NZ, -1))
    pieces = [p.reshape(DEV_BLOCKS, BLOCK, 2 * HEAD_WIDTH) for p in up + down[:0:-1]]
    top = shift(up[-1][: 2 * BLOCK], "z", NZ, 1)
    bottom = shift(down[-1][BLOCK:], "z", NZ, -1)
    return pieces + [top.reshape(2, BLOCK, 2 * HEAD_WIDTH), bottom.reshape(2, BLOCK, 2 * HEAD_WIDTH)]


def per_device(
    nx, nc, normed_input, queries, keys, values, grad_out, query_weight, key_weight, value_weight, output_weight, ancestors
):
    model = grad_out.shape[1]

    mine, kv = start_call(queries, keys, values, grad_out, output_weight)
    pieces = ring_gather(kv)
    before, after = shift(mine, "y", NY, 1), shift(mine, "y", NY, -1)
    half = mine.shape[0] // 2
    qds = [mine, before, after, shift(before[:half], "y", NY, 1), shift(after[half:], "y", NY, -1)]

    plan = plan_call(ancestors.T)
    qd = stack_call(qds)
    own, kv = stats_call(plan, pieces, qd)
    stats = [own] + [shift(own, "y", NY, s) for s in range(1, NY)]
    *row_part, col_part = grads_call(plan, kv, turn_call(kv), qd, stats)

    col_got = lax.all_to_all(col_part.reshape(NZ, DEV_BLOCKS * BLOCK, 2 * HEAD_WIDTH), "z", 0, 0, tiled=True)
    row_got = [row_part[0]] + [shift(row_part[s], "y", NY, s) for s in range(1, NY)]

    part_rows = model // (NZ * NY)
    qo_part, back, turned = rows_call(nx, nc, row_got, normed_input, grad_out, query_weight)
    qo_got = [qo_part[0]] + [shift(qo_part[s], "y", NY, s) for s in range(1, NY)]

    kv_part, send, keep = cols_call(nx, nc, col_got, turned, key_weight, value_weight, back)
    kv_got = [kv_part[0]] + [shift(kv_part[s], "y", NY, s) for s in range(1, NY)]
    sums = [sum(g.astype(f32) for g in got).astype(bf16) for got in (qo_got, kv_got)]
    sums = jnp.concatenate(sums, axis=1).reshape(NZ, part_rows, 2 * PAIR + 2 * HEAD_WIDTH)
    sums = jnp.sum(lax.all_to_all(sums, "z", 0, 0, tiled=True).astype(f32), axis=0)

    width = model // (nx * nc)
    side = nx * width
    for s in range(1, nc):
        keep = keep + shift(send[(s - 1) * side : s * side], "c", nc, s).astype(f32)
    input_grad = keep[:width]
    for s in range(1, nx):
        piece = keep[s * width : (s + 1) * width].astype(bf16)
        input_grad = input_grad + shift(piece, "x", nx, s).astype(f32)
    return (
        input_grad.astype(bf16).T,
        sums[:, :PAIR],
        sums[:, 2 * PAIR : 2 * PAIR + HEAD_WIDTH],
        sums[:, 2 * PAIR + HEAD_WIDTH :],
        sums[:, PAIR : 2 * PAIR].T,
    )


def solution(mesh):
    heads = mesh.shape["head"]
    nc = 2 if heads % 2 == 0 else 1
    nx = heads // nc
    grid = Mesh(mesh.devices.reshape(NZ, NY, nx, nc), ("z", "y", "x", "c"))
    leaf, head = ("z", "y"), ("x", "c")
    return jax.shard_map(
        functools.partial(per_device, nx, nc),
        mesh=grid,
        in_specs=(
            P(leaf, None),
            P(leaf, head),
            P(leaf, head),
            P(leaf, head),
            P(leaf, None),
            P(None, head),
            P(None, head),
            P(None, head),
            P(head, None),
            P(),
        ),
        out_specs=(
            P(leaf, head),
            P(leaf, head),
            P(leaf, head),
            P(leaf, head),
            P(head, leaf),
        ),
        check_vma=False,
    )
```

time: 170 us -> 142 us (0.84)
  waiting for transfers between devices: 64.3 us -> 40.7 us
  Pallas kernels: 24.5 us -> 35 us
  local copies, waits for them, and re-layouts: 19.9 us -> 9.57 us
  other arithmetic: 7.85 us -> 3.5 us
  starting transfers between devices: 49.1 us -> 52.7 us
  matrix products: 2.61 us -> 0 us
    ppermute x16 -> x28, starting transfers between devices: 19.5 us -> 40.4 us  [shift(): return lax.ppermute(x, axis, [(i, (i + by) % size) for i in range(size)])]
    all_to_all x4 -> x2, starting transfers between devices: 29.6 us -> 12.3 us  [the longest x1 8.81 us: per_device(): lax.all_to_all(col_part.reshape(NZ, DEV_BLOCKS * BLOCK, 2 * HEAD_WIDTH),...]
    ppermute x16 -> x28, waiting for transfers between devices: 43.4 us -> 31.7 us  [shift(): return lax.ppermute(x, axis, [(i, (i + by) % size) for i in range(size)])]
    all_to_all x4 -> x2, waiting for transfers between devices: 20.8 us -> 9.09 us  [the longest x1 7.61 us: per_device(): lax.all_to_all(col_part.reshape(NZ, DEV_BLOCKS * BLOCK, 2 * HEAD_WIDTH),...]
    pallas_call x3 -> x8, Pallas kernels: 24.5 us -> 35 us  [the longest x1 13.8 us: grads_call(): pl.pallas_call(grads_kernel, out_shape=(*[jax.ShapeDtypeStruct((2 * PAIR,...]
    unnamed x41 -> x43, local copies, waits for them, and re-layouts: 10.8 us -> 5.44 us
    dot_general x6 -> x0, matrix products: 2.61 us -> none  [the longest x4 1.73 us: dot_nt(): lax.dot_general(a, b, (((1,), (1,)), ((), ())), preferred_element_type=f32)]
    convert_element_type x2 -> x0, local copies, waits for them, and re-layouts: 1.87 us -> none  [the longest x1 1 us: per_device(): dot_nn(input_t, dkv).astype(bf16)]
  transfers between devices with their start and end apart: 20 -> 30, of which waited for: 15 -> 15; matrix products, arithmetic and copies ran while one was open for 12% -> 5% of each run, Pallas kernels for 4% -> 9%
where the time goes in v3:
time: 142 us; the launch traced here: 143 us
  starting transfers between devices  52.7 us (37%)
  waiting for transfers between devices  40.7 us (29%)
  Pallas kernels  35 us (25%)
  local copies, waits for them, and re-layouts  9.57 us (7%)
  other arithmetic  3.5 us (2%)
    ppermute x28, starting transfers between devices, shift(): return lax.ppermute(x, axis, [(i, (i + by) % size) for i in range(size)])  40.4 us
    ppermute x28, waiting for transfers between devices, shift(): return lax.ppermute(x, axis, [(i, (i + by) % size) for i in range(size)])  31.7 us
    pallas_call x1, Pallas kernels, grads_call(): pl.pallas_call(grads_kernel, out_shape=(*[jax.ShapeDtypeStruct((2 * PAIR,...  13.8 us
    all_to_all x1, starting transfers between devices, per_device(): lax.all_to_all(col_part.reshape(NZ, DEV_BLOCKS * BLOCK, 2 * HEAD_WIDTH),...  8.81 us
    all_to_all x1, waiting for transfers between devices, per_device(): lax.all_to_all(col_part.reshape(NZ, DEV_BLOCKS * BLOCK, 2 * HEAD_WIDTH),...  7.61 us
    pallas_call x1, Pallas kernels, stats_call(): pl.pallas_call(stats_kernel, out_shape=(jax.ShapeDtypeStruct((3 * STAT_RO...  5.95 us
    unnamed x43, local copies, waits for them, and re-layouts  5.44 us
    pallas_call x1, Pallas kernels, rows_call(): pl.pallas_call(functools.partial(rows_kernel, nx, nc), out_shape=(jax.Sha...  4.75 us
  transfers between devices with their start and end apart: 30, of which 15 were waited for; matrix products, arithmetic and copies ran while one was open for 5% of the time, Pallas kernels for 9%

profile of v3, /device:TPU:6, one launch (start us, length us, event | category | flops | bytes accessed | tf_op | source)
XLA Modules:
  0.0 142.5 jit_solution(14471529437663438522)
XLA Ops:
  0.6 2.6 %start.1 = (bf16[384,512]{1,0:T(8,128)(2,1)}, bf16[384,256]{1,0:T(8,128)(2,1)}) custom-call(bf16[384,256]{1,0:T(8,128)(2,1)} %query_any.1, bf16[384,128]{1,0:T(8,128)(2,1)} %key_any.1, bf16[384,128]{1,0:T(8,128)(2,1)} %value_any.1, bf16[384,1024]{1,0:T(8,128)(2,1)} %grad_any.3, bf16[256,1024]{1,0:T(8,128)(2,1)} %weight_any.1), custom_call_target="tpu_custom_call" | custom-call | tf_op jit(solution)/shard_map/start/pallas_call | solution.py:344
  3.2 5.9 %collective-permute-start.3 = (bf16[384,256]{1,0:T(8,128)(2,1)}, bf16[384,256]{1,0:T(8,128)(2,1)S(1)}, u32[]{:S(2)}, u32[]{:S(2)}) collective-permute-start(bf16[384,256]{1,0:T(8,128)(2,1)} %get-tuple-element.20), channel_id=1, source_target_pairs={{0,224},{32,0},{64,32},{96,64},{128,96},{160,128},{192,160},{224,1... | collective-permute-start | bytes 589832 | tf_op jit(solution)/shard_map/ppermute | solution.py:444
  9.2 3.0 %collective-permute-start.9 = (bf16[384,512]{1,0:T(8,128)(2,1)}, bf16[384,512]{1,0:T(8,128)(2,1)S(1)}, u32[]{:S(2)}, u32[]{:S(2)}) collective-permute-start(bf16[384,512]{1,0:T(8,128)(2,1)} %get-tuple-element.21.own), channel_id=1, source_target_pairs={{0,24},{8,0},{16,8},{24,16},{1,25},{9,1},{17,9},{25,17},{2,26},{10... | collective-permute-start | bytes 1179656 | tf_op jit(solution)/shard_map/ppermute | solution.py:444
  12.2 1.5 %collective-permute-done.3 = bf16[384,256]{1,0:T(8,128)(2,1)S(1)} collective-permute-done((bf16[384,256]{1,0:T(8,128)(2,1)}, bf16[384,256]{1,0:T(8,128)(2,1)S(1)}, u32[]{:S(2)}, u32[]{:S(2)}) %collective-permute-start.3) | collective-permute-done | bytes 196640 | tf_op jit(solution)/shard_map/ppermute | solution.py:444
  13.6 3.6 %collective-permute-start.4 = (bf16[384,256]{1,0:T(8,128)(2,1)S(1)}, bf16[384,256]{1,0:T(8,128)(2,1)S(1)}, u32[]{:S(2)}, u32[]{:S(2)}) collective-permute-start(bf16[384,256]{1,0:T(8,128)(2,1)S(1)} %collective-permute-done.3), channel_id=1, source_target_pairs={{0,224},{32,0},{64,32},{96,64},{128,96},{160,128},{192,160},{224,1... | collective-permute-start | bytes 589832 | tf_op jit(solution)/shard_map/ppermute | solution.py:444
  17.2 3.3 %collective-permute-done.4 = bf16[384,256]{1,0:T(8,128)(2,1)S(1)} collective-permute-done((bf16[384,256]{1,0:T(8,128)(2,1)S(1)}, bf16[384,256]{1,0:T(8,128)(2,1)S(1)}, u32[]{:S(2)}, u32[]{:S(2)}) %collective-permute-start.4) | collective-permute-done | bytes 196640 | tf_op jit(solution)/shard_map/ppermute | solution.py:444
  20.5 3.7 %collective-permute-start.5 = (bf16[384,256]{1,0:T(8,128)(2,1)S(1)}, bf16[384,256]{1,0:T(8,128)(2,1)S(1)}, u32[]{:S(2)}, u32[]{:S(2)}) collective-permute-start(bf16[384,256]{1,0:T(8,128)(2,1)S(1)} %collective-permute-done.4), channel_id=1, source_target_pairs={{0,224},{32,0},{64,32},{96,64},{128,96},{160,128},{192,160},{224,1... | collective-permute-start | bytes 589832 | tf_op jit(solution)/shard_map/ppermute | solution.py:444
  24.2 3.1 %collective-permute-start.11 = (bf16[192,512]{1,0:T(8,128)(2,1)S(1)}, bf16[192,512]{1,0:T(8,128)(2,1)S(1)}, u32[]{:S(2)}, u32[]{:S(2)}) collective-permute-start(bf16[192,512]{1,0:T(8,128)(2,1)S(1)} %slice.86), channel_id=1, source_target_pairs={{0,24},{8,0},{16,8},{24,16},{1,25},{9,1},{17,9},{25,17},{2,26},{10... | collective-permute-start | bytes 589832 | tf_op jit(solution)/shard_map/ppermute | solution.py:444
  27.5 3.7 %collective-permute-start.7 = (bf16[256,256]{1,0:T(8,128)(2,1)S(1)}, bf16[256,256]{1,0:T(8,128)(2,1)S(1)}, u32[]{:S(2)}, u32[]{:S(2)}) collective-permute-start(bf16[256,256]{1,0:T(8,128)(2,1)S(1)} %slice.84), channel_id=1, source_target_pairs={{0,224},{32,0},{64,32},{96,64},{128,96},{160,128},{192,160},{224,1... | collective-permute-start | bytes 393224 | tf_op jit(solution)/shard_map/ppermute | solution.py:444
  31.8 3.4 %plan.1.plan_any = s32[896]{0:T(1024)} custom-call(s32[16,96]{1,0:T(8,128)} %bitcast.44), custom_call_target="tpu_custom_call" | custom-call | tf_op jit(solution)/shard_map/plan/pallas_call | solution.py:363
  36.2 2.0 %collective-permute-done.6 = bf16[256,256]{1,0:T(8,128)(2,1)S(1)} collective-permute-done((bf16[256,256]{1,0:T(8,128)(2,1)}, bf16[256,256]{1,0:T(8,128)(2,1)S(1)}, u32[]{:S(2)}, u32[]{:S(2)}) %collective-permute-start.6) | collective-permute-done | bytes 131104 | tf_op jit(solution)/shard_map/ppermute | solution.py:444
  38.2 5.9 %stats.1 = (f32[48,256]{1,0:T(8,128)S(1)}, bf16[24,128,256]{2,1,0:T(8,128)(2,1)S(1)}) custom-call(s32[896]{0:T(1024)S(1)} %copy-done.11, bf16[3,128,256]{2,1,0:T(8,128)(2,1)S(1)} %bitcast.36, bf16[3,128,256]{2,1,0:T(8,128)(2,1)S(1)} %bitcast.38, bf16[3,128,256]{2,1,0:T(8,128)(2,1)S(1)} %bitcast.40, bf16[3,128,256]{2,1,0:T(8,128)(2,1)S(1)} %bitcast.35, ...), custom_call_target="tpu_custom_call" | custom-call | tf_op jit(solution)/shard_map/stats/pallas_call | solution.py:385
  44.3 2.4 %collective-permute-start.13 = (f32[48,256]{1,0:T(8,128)S(1)}, f32[48,256]{1,0:T(8,128)S(1)}, u32[]{:S(2)}, u32[]{:S(2)}) collective-permute-start(f32[48,256]{1,0:T(8,128)S(1)} %get-tuple-element.23.st0), channel_id=1, source_target_pairs={{0,16},{8,24},{16,0},{24,8},{1,17},{9,25},{17,1},{25,9},{2,18},{10... | collective-permute-start | bytes 147464 | tf_op jit(solution)/shard_map/ppermute | solution.py:444
  50.2 1.9 %collective-permute-done.12.st1 = f32[48,256]{1,0:T(8,128)S(1)} collective-permute-done((f32[48,256]{1,0:T(8,128)S(1)}, f32[48,256]{1,0:T(8,128)S(1)}, u32[]{:S(2)}, u32[]{:S(2)}) %collective-permute-start.12) | collective-permute-done | bytes 49184 | tf_op jit(solution)/shard_map/ppermute | solution.py:444
  52.7 13.8 %grads.1 = (bf16[512,384]{1,0:T(8,128)(2,1)}, bf16[512,384]{1,0:T(8,128)(2,1)}, bf16[512,384]{1,0:T(8,128)(2,1)}, bf16[512,384]{1,0:T(8,128)(2,1)}, bf16[24,128,256]{2,1,0:T(8,128)(2,1)}) custom-call(s32[896]{0:T(1024)} %plan.1.plan_any, bf16[24,128,256]{2,1,0:T(8,128)(2,1)} %copy-done.1, bf16[24,256,128]{2,1,0:T(8,128)(2,1)} %copy-done.2, ...), custom_call_target="tpu_custom_call" | custom-call | tf_op jit(solution)/shard_map/grads/pallas_call | solution.py:404
  66.5 8.8 %all-to-all-start = ((bf16[8,384,256]{2,1,0:T(8,128)(2,1)}), bf16[8,384,256]{2,1,0:T(8,128)(2,1)S(1)}, u32[]{:S(2)}, u32[]{:S(2)}) async-start(bf16[8,384,256]{2,1,0:T(8,128)(2,1)} %bitcast.43), calls=%async_computation | async-start | bytes 3145728 | tf_op jit(solution)/shard_map/all_to_all | solution.py:526
  75.6 3.2 %collective-permute-start.17 = (bf16[512,384]{1,0:T(8,128)(2,1)S(1)}, bf16[512,384]{1,0:T(8,128)(2,1)S(1)}, u32[]{:S(2)}, u32[]{:S(2)}) collective-permute-start(bf16[512,384]{1,0:T(8,128)(2,1)S(1)} %copy-done.18), channel_id=1, source_target_pairs={{0,24},{8,0},{16,8},{24,16},{1,25},{9,1},{17,9},{25,17},{2,26},{10... | collective-permute-start | bytes 1179656 | tf_op jit(solution)/shard_map/ppermute | solution.py:444
  78.7 11.7 %collective-permute-done.15.row1 = bf16[512,384]{1,0:T(8,128)(2,1)S(1)} collective-permute-done((bf16[512,384]{1,0:T(8,128)(2,1)S(1)}, bf16[512,384]{1,0:T(8,128)(2,1)S(1)}, u32[]{:S(2)}, u32[]{:S(2)}) %collective-permute-start.15) | collective-permute-done | bytes 393248 | tf_op jit(solution)/shard_map/ppermute | solution.py:444
  91.9 4.7 %rows.1 = (bf16[4,256,512]{2,1,0:T(8,128)(2,1)}, f32[1024,384]{1,0:T(8,128)}, bf16[1024,384]{1,0:T(8,128)(2,1)}) custom-call(bf16[512,384]{1,0:T(8,128)(2,1)} %get-tuple-element.25.row0, bf16[512,384]{1,0:T(8,128)(2,1)} %copy-done.12, bf16[512,384]{1,0:T(8,128)(2,1)} %copy-done.13, bf16[512,384]{1,0:T(8,128)(2,1)} %copy-done.14, ...), custom_call_target="tpu_custom_call" | custom-call | tf_op jit(solution)/shard_map/rows/pallas_call | solution.py:449
  96.7 2.1 %slice_bitcast_fusion.2 = (bf16[256,512]{1,0:T(8,128)(2,1)}, bf16[256,512]{1,0:T(8,128)(2,1)}, bf16[256,512]{1,0:T(8,128)(2,1)}) fusion(bf16[4,256,512]{2,1,0:T(8,128)(2,1)} %get-tuple-element.33), kind=kLoop, calls=%fused_computation.13 | loop fusion | bytes 1572864 | tf_op jit(solution)/shard_map/squeeze | solution.py:531
  99.0 3.0 %collective-permute-start.24 = (bf16[256,512]{1,0:T(8,128)(2,1)}, bf16[256,512]{1,0:T(8,128)(2,1)}, u32[]{:S(2)}, u32[]{:S(2)}) collective-permute-start(bf16[256,512]{1,0:T(8,128)(2,1)} %get-tuple-element.43), channel_id=1, source_target_pairs={{0,24},{8,0},{16,8},{24,16},{1,25},{9,1},{17,9},{25,17},{2,26},{10... | collective-permute-start | bytes 786440 | tf_op jit(solution)/shard_map/ppermute | solution.py:444
  102.6 7.6 %all-to-all-done.got_any = bf16[8,384,256]{2,1,0:T(8,128)(2,1)S(1)} async-done(((bf16[8,384,256]{2,1,0:T(8,128)(2,1)}), bf16[8,384,256]{2,1,0:T(8,128)(2,1)S(1)}, u32[]{:S(2)}, u32[]{:S(2)}) %all-to-all-start) | async-done | bytes 1572896 | tf_op jit(solution)/shard_map/all_to_all | solution.py:526
  112.3 2.9 %cols.1 = (bf16[4,256,256]{2,1,0:T(8,128)(2,1)S(1)}, bf16[512,384]{1,0:T(8,128)(2,1)}, f32[512,384]{1,0:T(8,128)S(1)}) custom-call(bf16[8,384,256]{2,1,0:T(8,128)(2,1)S(1)} %all-to-all-done.got_any, bf16[1024,384]{1,0:T(8,128)(2,1)S(1)} %copy-done.5, bf16[1024,128]{1,0:T(8,128)(2,1)S(1)} %copy-done.7, bf16[1024,128]{1,0:T(8,128)(2,1)S(1)} %copy-done.8, ...), custom_call_target="tpu_custom_call" | custom-call | tf_op jit(solution)/shard_map/cols/pallas_call | solution.py:476
  115.4 3.2 %collective-permute-start.27 = (bf16[256,256]{1,0:T(8,128)(2,1)S(1)}, bf16[256,256]{1,0:T(8,128)(2,1)S(1)}, u32[]{:S(2)}, u32[]{:S(2)}) collective-permute-start(bf16[256,256]{1,0:T(8,128)(2,1)S(1)} %get-tuple-element.46), channel_id=1, source_target_pairs={{0,24},{8,0},{16,8},{24,16},{1,25},{9,1},{17,9},{25,17},{2,26},{10... | collective-permute-start | bytes 393224 | tf_op jit(solution)/shard_map/ppermute | solution.py:444
  119.0 1.3 fusion.2
  122.6 2.6 %collective-permute-done.26 = bf16[256,256]{1,0:T(8,128)(2,1)S(1)} collective-permute-done((bf16[256,256]{1,0:T(8,128)(2,1)S(1)}, bf16[256,256]{1,0:T(8,128)(2,1)S(1)}, u32[]{:S(2)}, u32[]{:S(2)}) %collective-permute-start.26) | collective-permute-done | bytes 131104 | tf_op jit(solution)/shard_map/ppermute | solution.py:444
  126.0 3.5 %all-to-all-start.1 = ((bf16[8,32,768]{2,1,0:T(8,128)(2,1)}), bf16[8,32,768]{2,1,0:T(8,128)(2,1)S(1)}, u32[]{:S(2)}, u32[]{:S(2)}) async-start(bf16[8,32,768]{2,1,0:T(8,128)(2,1)} %bitcast.20), calls=%async_computation.1 | async-start | bytes 786432 | tf_op jit(solution)/shard_map/all_to_all | solution.py:537
  131.3 1.5 %collective-permute-start.21 = (bf16[128,384]{1,0:T(8,128)(2,1)S(1)}, bf16[128,384]{1,0:T(8,128)(2,1)S(1)}, u32[]{:S(2)}, u32[]{:S(2)}) collective-permute-start(bf16[128,384]{1,0:T(8,128)(2,1)S(1)} %get-tuple-element.49), channel_id=1, source_target_pairs={{0,6},{2,0},{4,2},{6,4},{1,7},{3,1},{5,3},{7,5},{8,14},{10,8},{12,... | collective-permute-start | bytes 294920 | tf_op jit(solution)/shard_map/ppermute | solution.py:444
  132.8 1.5 %collective-permute-start.20 = (bf16[128,384]{1,0:T(8,128)(2,1)S(1)}, bf16[128,384]{1,0:T(8,128)(2,1)S(1)}, u32[]{:S(2)}, u32[]{:S(2)}) collective-permute-start(bf16[128,384]{1,0:T(8,128)(2,1)S(1)} %get-tuple-element.50), channel_id=1, source_target_pairs={{0,4},{2,6},{4,0},{6,2},{1,5},{3,7},{5,1},{7,3},{8,12},{10,14},{12... | collective-permute-start | bytes 294920 | tf_op jit(solution)/shard_map/ppermute | solution.py:444
  135.4 1.7 %collective-permute-done.21 = bf16[128,384]{1,0:T(8,128)(2,1)S(1)} collective-permute-done((bf16[128,384]{1,0:T(8,128)(2,1)S(1)}, bf16[128,384]{1,0:T(8,128)(2,1)S(1)}, u32[]{:S(2)}, u32[]{:S(2)}) %collective-permute-start.21) | collective-permute-done | bytes 98336 | tf_op jit(solution)/shard_map/ppermute | solution.py:444
  137.1 1.8 %collective-permute-done.20 = bf16[128,384]{1,0:T(8,128)(2,1)S(1)} collective-permute-done((bf16[128,384]{1,0:T(8,128)(2,1)S(1)}, bf16[128,384]{1,0:T(8,128)(2,1)S(1)}, u32[]{:S(2)}, u32[]{:S(2)}) %collective-permute-start.20) | collective-permute-done | bytes 98336 | tf_op jit(solution)/shard_map/ppermute | solution.py:444
  139.7 1.5 %all-to-all-done.1 = bf16[8,32,768]{2,1,0:T(8,128)(2,1)S(1)} async-done(((bf16[8,32,768]{2,1,0:T(8,128)(2,1)}), bf16[8,32,768]{2,1,0:T(8,128)(2,1)S(1)}, u32[]{:S(2)}, u32[]{:S(2)}) %all-to-all-start.1) | async-done | bytes 393248 | tf_op jit(solution)/shard_map/all_to_all | solution.py:537
  (94 shorter events, 18.9 us)
Async XLA Ops:
  3.2 32.1 %copy-start.6 = (bf16[384,512]{1,0:T(8,128)(2,1)S(1)}, bf16[384,512]{1,0:T(8,128)(2,1)}, u32[]{:S(2)}) copy-start(bf16[384,512]{1,0:T(8,128)(2,1)} %get-tuple-element.21.own) | copy-start | bytes 1179652
  3.2 10.4 %collective-permute-start.3 = (bf16[384,256]{1,0:T(8,128)(2,1)}, bf16[384,256]{1,0:T(8,128)(2,1)S(1)}, u32[]{:S(2)}, u32[]{:S(2)}) collective-permute-start(bf16[384,256]{1,0:T(8,128)(2,1)} %get-tuple-element.20), channel_id=1, source_target_pairs={{0,224},{32,0},{64,32},{96,64},{128,96},{160,128},{192,160},{224,1... | collective-permute-start | bytes 589832 | tf_op jit(solution)/shard_map/ppermute | solution.py:444
  9.1 8.1 %collective-permute-start = (bf16[384,256]{1,0:T(8,128)(2,1)}, bf16[384,256]{1,0:T(8,128)(2,1)S(1)}, u32[]{:S(2)}, u32[]{:S(2)}) collective-permute-start(bf16[384,256]{1,0:T(8,128)(2,1)} %get-tuple-element.20), channel_id=1, source_target_pairs={{0,32},{32,64},{64,96},{96,128},{128,160},{160,192},{192,224},{224... | collective-permute-start | bytes 589832 | tf_op jit(solution)/shard_map/ppermute | solution.py:444
  9.2 15.1 %collective-permute-start.9 = (bf16[384,512]{1,0:T(8,128)(2,1)}, bf16[384,512]{1,0:T(8,128)(2,1)S(1)}, u32[]{:S(2)}, u32[]{:S(2)}) collective-permute-start(bf16[384,512]{1,0:T(8,128)(2,1)} %get-tuple-element.21.own), channel_id=1, source_target_pairs={{0,24},{8,0},{16,8},{24,16},{1,25},{9,1},{17,9},{25,17},{2,26},{10... | collective-permute-start | bytes 1179656 | tf_op jit(solution)/shard_map/ppermute | solution.py:444
  12.2 15.1 %collective-permute-start.8 = (bf16[384,512]{1,0:T(8,128)(2,1)}, bf16[384,512]{1,0:T(8,128)(2,1)S(1)}, u32[]{:S(2)}, u32[]{:S(2)}) collective-permute-start(bf16[384,512]{1,0:T(8,128)(2,1)} %get-tuple-element.21.own), channel_id=1, source_target_pairs={{0,8},{8,16},{16,24},{24,0},{1,9},{9,17},{17,25},{25,1},{2,10},{10... | collective-permute-start | bytes 1179656 | tf_op jit(solution)/shard_map/ppermute | solution.py:444
  13.6 6.9 %collective-permute-start.4 = (bf16[384,256]{1,0:T(8,128)(2,1)S(1)}, bf16[384,256]{1,0:T(8,128)(2,1)S(1)}, u32[]{:S(2)}, u32[]{:S(2)}) collective-permute-start(bf16[384,256]{1,0:T(8,128)(2,1)S(1)} %collective-permute-done.3), channel_id=1, source_target_pairs={{0,224},{32,0},{64,32},{96,64},{128,96},{160,128},{192,160},{224,1... | collective-permute-start | bytes 589832 | tf_op jit(solution)/shard_map/ppermute | solution.py:444
  17.2 7.0 %collective-permute-start.1 = (bf16[384,256]{1,0:T(8,128)(2,1)S(1)}, bf16[384,256]{1,0:T(8,128)(2,1)S(1)}, u32[]{:S(2)}, u32[]{:S(2)}) collective-permute-start(bf16[384,256]{1,0:T(8,128)(2,1)S(1)} %collective-permute-done), channel_id=1, source_target_pairs={{0,32},{32,64},{64,96},{96,128},{128,160},{160,192},{192,224},{224... | collective-permute-start | bytes 589832 | tf_op jit(solution)/shard_map/ppermute | solution.py:444
  20.5 6.9 %collective-permute-start.5 = (bf16[384,256]{1,0:T(8,128)(2,1)S(1)}, bf16[384,256]{1,0:T(8,128)(2,1)S(1)}, u32[]{:S(2)}, u32[]{:S(2)}) collective-permute-start(bf16[384,256]{1,0:T(8,128)(2,1)S(1)} %collective-permute-done.4), channel_id=1, source_target_pairs={{0,224},{32,0},{64,32},{96,64},{128,96},{160,128},{192,160},{224,1... | collective-permute-start | bytes 589832 | tf_op jit(solution)/shard_map/ppermute | solution.py:444
  24.2 7.0 %collective-permute-start.2 = (bf16[384,256]{1,0:T(8,128)(2,1)S(1)}, bf16[384,256]{1,0:T(8,128)(2,1)S(1)}, u32[]{:S(2)}, u32[]{:S(2)}) collective-permute-start(bf16[384,256]{1,0:T(8,128)(2,1)S(1)} %collective-permute-done.1), channel_id=1, source_target_pairs={{0,32},{32,64},{64,96},{96,128},{128,160},{160,192},{192,224},{224... | collective-permute-start | bytes 589832 | tf_op jit(solution)/shard_map/ppermute | solution.py:444
  24.2 11.0 %collective-permute-start.11 = (bf16[192,512]{1,0:T(8,128)(2,1)S(1)}, bf16[192,512]{1,0:T(8,128)(2,1)S(1)}, u32[]{:S(2)}, u32[]{:S(2)}) collective-permute-start(bf16[192,512]{1,0:T(8,128)(2,1)S(1)} %slice.86), channel_id=1, source_target_pairs={{0,24},{8,0},{16,8},{24,16},{1,25},{9,1},{17,9},{25,17},{2,26},{10... | collective-permute-start | bytes 589832 | tf_op jit(solution)/shard_map/ppermute | solution.py:444
  27.3 7.9 %collective-permute-start.10 = (bf16[192,512]{1,0:T(8,128)(2,1)S(1)}, bf16[192,512]{1,0:T(8,128)(2,1)S(1)}, u32[]{:S(2)}, u32[]{:S(2)}) collective-permute-start(bf16[192,512]{1,0:T(8,128)(2,1)S(1)} %slice.85), channel_id=1, source_target_pairs={{0,8},{8,16},{16,24},{24,0},{1,9},{9,17},{17,25},{25,1},{2,10},{10... | collective-permute-start | bytes 589832 | tf_op jit(solution)/shard_map/ppermute | solution.py:444
  27.5 8.7 %collective-permute-start.7 = (bf16[256,256]{1,0:T(8,128)(2,1)S(1)}, bf16[256,256]{1,0:T(8,128)(2,1)S(1)}, u32[]{:S(2)}, u32[]{:S(2)}) collective-permute-start(bf16[256,256]{1,0:T(8,128)(2,1)S(1)} %slice.84), channel_id=1, source_target_pairs={{0,224},{32,0},{64,32},{96,64},{128,96},{160,128},{192,160},{224,1... | collective-permute-start | bytes 393224 | tf_op jit(solution)/shard_map/ppermute | solution.py:444
  31.8 6.4 %collective-permute-start.6 = (bf16[256,256]{1,0:T(8,128)(2,1)}, bf16[256,256]{1,0:T(8,128)(2,1)S(1)}, u32[]{:S(2)}, u32[]{:S(2)}) collective-permute-start(bf16[256,256]{1,0:T(8,128)(2,1)} %slice.83), channel_id=1, source_target_pairs={{0,32},{32,64},{64,96},{96,128},{128,160},{160,192},{192,224},{224... | collective-permute-start | bytes 393224 | tf_op jit(solution)/shard_map/ppermute | solution.py:444
  44.2 4.8 %collective-permute-start.14 = (f32[48,256]{1,0:T(8,128)S(1)}, f32[48,256]{1,0:T(8,128)S(1)}, u32[]{:S(2)}, u32[]{:S(2)}) collective-permute-start(f32[48,256]{1,0:T(8,128)S(1)} %get-tuple-element.23.st0), channel_id=1, source_target_pairs={{0,24},{8,0},{16,8},{24,16},{1,25},{9,1},{17,9},{25,17},{2,26},{10... | collective-permute-start | bytes 147464 | tf_op jit(solution)/shard_map/ppermute | solution.py:444
  44.3 5.8 %collective-permute-start.13 = (f32[48,256]{1,0:T(8,128)S(1)}, f32[48,256]{1,0:T(8,128)S(1)}, u32[]{:S(2)}, u32[]{:S(2)}) collective-permute-start(f32[48,256]{1,0:T(8,128)S(1)} %get-tuple-element.23.st0), channel_id=1, source_target_pairs={{0,16},{8,24},{16,0},{24,8},{1,17},{9,25},{17,1},{25,9},{2,18},{10... | collective-permute-start | bytes 147464 | tf_op jit(solution)/shard_map/ppermute | solution.py:444
  46.8 5.3 %collective-permute-start.12 = (f32[48,256]{1,0:T(8,128)S(1)}, f32[48,256]{1,0:T(8,128)S(1)}, u32[]{:S(2)}, u32[]{:S(2)}) collective-permute-start(f32[48,256]{1,0:T(8,128)S(1)} %get-tuple-element.23.st0), channel_id=1, source_target_pairs={{0,8},{8,16},{16,24},{24,0},{1,9},{9,17},{17,25},{25,1},{2,10},{10... | collective-permute-start | bytes 147464 | tf_op jit(solution)/shard_map/ppermute | solution.py:444
  66.5 43.7 %all-to-all-start = ((bf16[8,384,256]{2,1,0:T(8,128)(2,1)}), bf16[8,384,256]{2,1,0:T(8,128)(2,1)S(1)}, u32[]{:S(2)}, u32[]{:S(2)}) async-start(bf16[8,384,256]{2,1,0:T(8,128)(2,1)} %bitcast.43), calls=%async_computation | async-start | bytes 3145728 | tf_op jit(solution)/shard_map/all_to_all | solution.py:526
  75.3 15.1 %collective-permute-start.15 = (bf16[512,384]{1,0:T(8,128)(2,1)S(1)}, bf16[512,384]{1,0:T(8,128)(2,1)S(1)}, u32[]{:S(2)}, u32[]{:S(2)}) collective-permute-start(bf16[512,384]{1,0:T(8,128)(2,1)S(1)} %copy-done.20), channel_id=1, source_target_pairs={{0,8},{8,16},{16,24},{24,0},{1,9},{9,17},{17,25},{25,1},{2,10},{10... | collective-permute-start | bytes 1179656 | tf_op jit(solution)/shard_map/ppermute | solution.py:444
  75.4 15.0 %collective-permute-start.16 = (bf16[512,384]{1,0:T(8,128)(2,1)S(1)}, bf16[512,384]{1,0:T(8,128)(2,1)S(1)}, u32[]{:S(2)}, u32[]{:S(2)}) collective-permute-start(bf16[512,384]{1,0:T(8,128)(2,1)S(1)} %copy-done.19), channel_id=1, source_target_pairs={{0,16},{8,24},{16,0},{24,8},{1,17},{9,25},{17,1},{25,9},{2,18},{10... | collective-permute-start | bytes 1179656 | tf_op jit(solution)/shard_map/ppermute | solution.py:444
  75.6 15.6 %collective-permute-start.17 = (bf16[512,384]{1,0:T(8,128)(2,1)S(1)}, bf16[512,384]{1,0:T(8,128)(2,1)S(1)}, u32[]{:S(2)}, u32[]{:S(2)}) collective-permute-start(bf16[512,384]{1,0:T(8,128)(2,1)S(1)} %copy-done.18), channel_id=1, source_target_pairs={{0,24},{8,0},{16,8},{24,16},{1,25},{9,1},{17,9},{25,17},{2,26},{10... | collective-permute-start | bytes 1179656 | tf_op jit(solution)/shard_map/ppermute | solution.py:444
  91.9 18.4 %copy-start.7 = (bf16[1024,128]{1,0:T(8,128)(2,1)S(1)}, bf16[1024,128]{1,0:T(8,128)(2,1)}, u32[]{:S(2)}) copy-start(bf16[1024,128]{1,0:T(8,128)(2,1)} %wk_any.1) | copy-start | bytes 786436
  98.8 19.9 %collective-permute-start.22 = (bf16[256,512]{1,0:T(8,128)(2,1)}, bf16[256,512]{1,0:T(8,128)(2,1)}, u32[]{:S(2)}, u32[]{:S(2)}) collective-permute-start(bf16[256,512]{1,0:T(8,128)(2,1)} %get-tuple-element.42), channel_id=1, source_target_pairs={{0,8},{8,16},{16,24},{24,0},{1,9},{9,17},{17,25},{25,1},{2,10},{10... | collective-permute-start | bytes 786440 | tf_op jit(solution)/shard_map/ppermute | solution.py:444
  99.0 19.7 %collective-permute-start.24 = (bf16[256,512]{1,0:T(8,128)(2,1)}, bf16[256,512]{1,0:T(8,128)(2,1)}, u32[]{:S(2)}, u32[]{:S(2)}) collective-permute-start(bf16[256,512]{1,0:T(8,128)(2,1)} %get-tuple-element.43), channel_id=1, source_target_pairs={{0,24},{8,0},{16,8},{24,16},{1,25},{9,1},{17,9},{25,17},{2,26},{10... | collective-permute-start | bytes 786440 | tf_op jit(solution)/shard_map/ppermute | solution.py:444
  102.0 17.0 %collective-permute-start.23 = (bf16[256,512]{1,0:T(8,128)(2,1)}, bf16[256,512]{1,0:T(8,128)(2,1)}, u32[]{:S(2)}, u32[]{:S(2)}) collective-permute-start(bf16[256,512]{1,0:T(8,128)(2,1)} %get-tuple-element.44), channel_id=1, source_target_pairs={{0,16},{8,24},{16,0},{24,8},{1,17},{9,25},{17,1},{25,9},{2,18},{10... | collective-permute-start | bytes 786440 | tf_op jit(solution)/shard_map/ppermute | solution.py:444
  115.3 6.3 %collective-permute-start.25 = (bf16[256,256]{1,0:T(8,128)(2,1)S(1)}, bf16[256,256]{1,0:T(8,128)(2,1)S(1)}, u32[]{:S(2)}, u32[]{:S(2)}) collective-permute-start(bf16[256,256]{1,0:T(8,128)(2,1)S(1)} %get-tuple-element.45), channel_id=1, source_target_pairs={{0,8},{8,16},{16,24},{24,0},{1,9},{9,17},{17,25},{25,1},{2,10},{10... | collective-permute-start | bytes 393224 | tf_op jit(solution)/shard_map/ppermute | solution.py:444
  115.4 7.1 %collective-permute-start.27 = (bf16[256,256]{1,0:T(8,128)(2,1)S(1)}, bf16[256,256]{1,0:T(8,128)(2,1)S(1)}, u32[]{:S(2)}, u32[]{:S(2)}) collective-permute-start(bf16[256,256]{1,0:T(8,128)(2,1)S(1)} %get-tuple-element.46), channel_id=1, source_target_pairs={{0,24},{8,0},{16,8},{24,16},{1,25},{9,1},{17,9},{25,17},{2,26},{10... | collective-permute-start | bytes 393224 | tf_op jit(solution)/shard_map/ppermute | solution.py:444
  118.6 6.5 %collective-permute-start.26 = (bf16[256,256]{1,0:T(8,128)(2,1)S(1)}, bf16[256,256]{1,0:T(8,128)(2,1)S(1)}, u32[]{:S(2)}, u32[]{:S(2)}) collective-permute-start(bf16[256,256]{1,0:T(8,128)(2,1)S(1)} %get-tuple-element.47), channel_id=1, source_target_pairs={{0,16},{8,24},{16,0},{24,8},{1,17},{9,25},{17,1},{25,9},{2,18},{10... | collective-permute-start | bytes 393224 | tf_op jit(solution)/shard_map/ppermute | solution.py:444
  118.7 10.8 %collective-permute-start.18 = (bf16[512,384]{1,0:T(8,128)(2,1)}, bf16[512,384]{1,0:T(8,128)(2,1)S(1)}, u32[]{:S(2)}, u32[]{:S(2)}) collective-permute-start(bf16[512,384]{1,0:T(8,128)(2,1)} %get-tuple-element.32), channel_id=1, source_target_pairs={{0,1},{1,0},{2,3},{3,2},{4,5},{5,4},{6,7},{7,6},{8,9},{9,8},{10,11... | collective-permute-start | bytes 1179656 | tf_op jit(solution)/shard_map/ppermute | solution.py:444
  126.0 15.3 %all-to-all-start.1 = ((bf16[8,32,768]{2,1,0:T(8,128)(2,1)}), bf16[8,32,768]{2,1,0:T(8,128)(2,1)S(1)}, u32[]{:S(2)}, u32[]{:S(2)}) async-start(bf16[8,32,768]{2,1,0:T(8,128)(2,1)} %bitcast.20), calls=%async_computation.1 | async-start | bytes 786432 | tf_op jit(solution)/shard_map/all_to_all | solution.py:537
  130.7 4.7 %collective-permute-start.19 = (bf16[128,384]{1,0:T(8,128)(2,1)S(1)}, bf16[128,384]{1,0:T(8,128)(2,1)S(1)}, u32[]{:S(2)}, u32[]{:S(2)}) collective-permute-start(bf16[128,384]{1,0:T(8,128)(2,1)S(1)} %get-tuple-element.48), channel_id=1, source_target_pairs={{0,2},{2,4},{4,6},{6,0},{1,3},{3,5},{5,7},{7,1},{8,10},{10,12},{12... | collective-permute-start | bytes 294920 | tf_op jit(solution)/shard_map/ppermute | solution.py:444
  131.3 5.8 %collective-permute-start.21 = (bf16[128,384]{1,0:T(8,128)(2,1)S(1)}, bf16[128,384]{1,0:T(8,128)(2,1)S(1)}, u32[]{:S(2)}, u32[]{:S(2)}) collective-permute-start(bf16[128,384]{1,0:T(8,128)(2,1)S(1)} %get-tuple-element.49), channel_id=1, source_target_pairs={{0,6},{2,0},{4,2},{6,4},{1,7},{3,1},{5,3},{7,5},{8,14},{10,8},{12,... | collective-permute-start | bytes 294920 | tf_op jit(solution)/shard_map/ppermute | solution.py:444
  132.8 6.1 %collective-permute-start.20 = (bf16[128,384]{1,0:T(8,128)(2,1)S(1)}, bf16[128,384]{1,0:T(8,128)(2,1)S(1)}, u32[]{:S(2)}, u32[]{:S(2)}) collective-permute-start(bf16[128,384]{1,0:T(8,128)(2,1)S(1)} %get-tuple-element.50), channel_id=1, source_target_pairs={{0,4},{2,6},{4,0},{6,2},{1,5},{3,7},{5,1},{7,3},{8,12},{10,14},{12... | collective-permute-start | bytes 294920 | tf_op jit(solution)/shard_map/ppermute | solution.py:444
  (19 other events, 83.6 us)

commit v4 on v3

--- a/solution.py
+++ b/solution.py
@@ -51,22 +51,23 @@
         copy.wait()
 
 
-def start_kernel(query_any, key_any, value_any, grad_any, weight_any, qd_ref, kv_ref, grad_ref, weight_ref, sems):
-    copies = start_copies(
+def join_kernel(key_any, value_any, kv_ref, sems):
+    copy_all(
         (
-            (grad_any, grad_ref),
-            (weight_any, weight_ref),
             (key_any, kv_ref.at[:, pl.ds(0, HEAD_WIDTH)]),
             (value_any, kv_ref.at[:, pl.ds(HEAD_WIDTH, HEAD_WIDTH)]),
-            (query_any, qd_ref.at[:, pl.ds(0, PAIR)]),
         ),
         sems,
     )
+
+
+def start_kernel(query_any, grad_any, weight_any, qd_ref, grad_ref, weight_ref, sems):
+    pairs = ((grad_any, grad_ref), (weight_any, weight_ref), (query_any, qd_ref.at[:, pl.ds(0, PAIR)]))
+    copies = start_copies(pairs, sems)
     copies[0].wait()
     copies[1].wait()
     qd_ref[:, PAIR:] = dot_nt(grad_ref[...], weight_ref[...]).astype(bf16)
-    for copy in copies[2:]:
-        copy.wait()
+    copies[2].wait()
 
 
 def stack_kernel(own, before, after, top, bottom, out_ref, sems):
@@ -143,13 +144,13 @@
 
 
 def stats_kernel(plan_any, *refs):
-    pieces, (qd_any, out_ref, kv_ref, qd_ref, plan_ref, sems) = refs[:9], refs[9:]
+    pieces, (qd_ref, out_ref, kv_ref, plan_ref, sems) = refs[:9], refs[9:]
     z = lax.axis_index("z")
 
     def slots_of(back):
         return pl.ds(lax.rem(z - back + NZ, NZ) * DEV_BLOCKS, DEV_BLOCKS)
 
-    pairs = [(qd_any, qd_ref), (plan_any, plan_ref)]
+    pairs = [(plan_any, plan_ref)]
     for piece, back in zip(pieces[:7], (0, 1, 2, 3, 5, 6, 7)):
         pairs.append((piece, kv_ref.at[slots_of(back)]))
     far = lax.rem(z + NZ // 2, NZ) * DEV_BLOCKS
@@ -185,13 +186,13 @@
 
 
 def grads_kernel(
-    plan_any, kv_any, kvt_any, qd_any, st0, st1, st2, st3,
+    plan_any, kv_any, qd_any, st0, st1, st2, st3,
     row0, row1, row2, row3, col_any,
     o_scr, dq_scr, dk_scr, dv_scr, lse_scr, delta_scr,
     kv_ref, kvt_ref, qd_ref, plan_ref, row_scr, col_scr, sems,
 ):
     y = lax.axis_index("y")
-    pairs = ((kv_any, kv_ref), (kvt_any, kvt_ref), (qd_any, qd_ref), (plan_any, plan_ref))
+    pairs = ((kv_any, kv_ref), (qd_any, qd_ref), (plan_any, plan_ref))
     copies = start_copies(pairs, sems)
     for scr in (o_scr, dq_scr, dk_scr, dv_scr):
         def clear(i, _, scr=scr):
@@ -209,7 +210,16 @@
     )
     lse_scr[...] = m + jnp.log2(total)
     delta_scr[...] = dsum / total
-    for copy in copies:
+    copies[0].wait()
+
+    def turn(c, _):
+        for k in range(2):
+            cols = slice(k * HEAD_WIDTH, (k + 1) * HEAD_WIDTH)
+            kvt_ref[c, cols, :] = kv_ref[c, :, cols].T
+        return 0
+
+    lax.fori_loop(0, COL_BLOCKS, turn, 0, unroll=4)
+    for copy in copies[1:]:
         copy.wait()
 
     def step(i, _):
@@ -254,16 +264,6 @@
         copies += start_copies([(row_scr.at[t], row_ref)], sems, 4 + NZ + t)
     for copy in copies:
         copy.wait()
-
-
-def turn_kernel(kv_ref, out_ref):
-    def one(c, _):
-        for k in range(2):
-            cols = slice(k * HEAD_WIDTH, (k + 1) * HEAD_WIDTH)
-            out_ref[c, cols, :] = kv_ref[c, :, cols].T
-        return 0
-
-    lax.fori_loop(0, COL_BLOCKS, one, 0, unroll=4)
 
 
 def scatter_rows(part_ref, cols, value):
@@ -304,18 +304,17 @@
         copy.wait()
 
 
-def cols_kernel(
-    nx, nc, got_any, turned_any, wk_any, wv_any, back_any, part_ref, send_ref, keep_ref,
-    got_ref, turned_ref, wk_ref, wv_ref, back_ref, sems,
-):
-    pairs = [(got_any, got_ref), (turned_any, turned_ref), (wk_any, wk_ref), (wv_any, wv_ref), (back_any, back_ref)]
-    copies = start_copies(pairs, sems)
+def cols_kernel(got_any, turned_any, part_ref, d_ref, got_ref, turned_ref, sems):
+    copies = start_copies(((got_any, got_ref), (turned_any, turned_ref)), sems)
     copies[0].wait()
-    d = sum(got_ref[t].astype(f32) for t in range(NZ)).astype(bf16)
+    d_ref[...] = sum(got_ref[t].astype(f32) for t in range(NZ)).astype(bf16)
     copies[1].wait()
-    scatter_rows(part_ref, slice(0, 2 * HEAD_WIDTH), dot_nn(turned_ref[...], d))
-    for copy in copies[2:]:
-        copy.wait()
+    scatter_rows(part_ref, slice(0, 2 * HEAD_WIDTH), dot_nn(turned_ref[...], d_ref[...]))
+
+
+def back_kernel(nx, nc, d_ref, wk_any, wv_any, back_any, send_ref, keep_ref, wk_ref, wv_ref, back_ref, sems):
+    copy_all(((wk_any, wk_ref), (wv_any, wv_ref), (back_any, back_ref)), sems)
+    d = d_ref[...]
     width = wk_ref.shape[0] // (nx * nc)
     for i in range(nx * nc):
         rows = model_rows(i, nx, nc, width)
@@ -339,24 +338,32 @@
 STACK = jax.ShapeDtypeStruct((ROW_BLOCKS, PAIR, 2 * HEAD_WIDTH), bf16)
 
 
-def start_call(queries, keys, values, grad_out, output_weight):
-    tokens = queries.shape[0]
+def join_call(keys, values):
+    return pl.pallas_call(
+        join_kernel,
+        out_shape=jax.ShapeDtypeStruct((keys.shape[0], 2 * HEAD_WIDTH), bf16),
+        in_specs=[HBM_SPEC] * 2,
+        out_specs=VMEM_SPEC,
+        scratch_shapes=[pltpu.SemaphoreType.DMA((2,))],
+        compiler_params=vmem(54),
+        name="join",
+    )(keys, values)
+
+
+def start_call(queries, grad_out, output_weight):
     return pl.pallas_call(
         start_kernel,
-        out_shape=(
-            jax.ShapeDtypeStruct((tokens, 2 * PAIR), bf16),
-            jax.ShapeDtypeStruct((tokens, 2 * HEAD_WIDTH), bf16),
-        ),
-        in_specs=[HBM_SPEC] * 5,
-        out_specs=(VMEM_SPEC,) * 2,
+        out_shape=jax.ShapeDtypeStruct((queries.shape[0], 2 * PAIR), bf16),
+        in_specs=[HBM_SPEC] * 3,
+        out_specs=VMEM_SPEC,
         scratch_shapes=[
             pltpu.VMEM(grad_out.shape, bf16),
             pltpu.VMEM(output_weight.shape, bf16),
-            pltpu.SemaphoreType.DMA((5,)),
+            pltpu.SemaphoreType.DMA((3,)),
         ],
         compiler_params=vmem(54),
         name="start",
-    )(queries, keys, values, grad_out, output_weight)
+    )(queries, grad_out, output_weight)
 
 
 def plan_call(anc):
@@ -388,26 +395,25 @@
             jax.ShapeDtypeStruct((3 * STAT_ROWS, PAIR), f32),
             jax.ShapeDtypeStruct((COL_BLOCKS, BLOCK, 2 * HEAD_WIDTH), bf16),
         ),
-        in_specs=[HBM_SPEC] * 11,
+        in_specs=[HBM_SPEC] * 10 + [VMEM_SPEC],
         out_specs=(VMEM_SPEC, VMEM_SPEC),
         scratch_shapes=[
-            pltpu.VMEM(STACK.shape, bf16),
             pltpu.SMEM((PLAN,), jnp.int32),
-            pltpu.SemaphoreType.DMA((13,)),
+            pltpu.SemaphoreType.DMA((12,)),
         ],
         compiler_params=vmem(12),
         name="stats",
     )(plan, *pieces, qd)
 
 
-def grads_call(plan, kv, kvt, qd, stats):
+def grads_call(plan, kv, qd, stats):
     return pl.pallas_call(
         grads_kernel,
         out_shape=(
             *[jax.ShapeDtypeStruct((2 * PAIR, DEV_BLOCKS * BLOCK), bf16)] * NY,
             jax.ShapeDtypeStruct((COL_BLOCKS, BLOCK, 2 * HEAD_WIDTH), bf16),
         ),
-        in_specs=[HBM_SPEC] * 4 + [VMEM_SPEC] * 4,
+        in_specs=[HBM_SPEC] * 3 + [VMEM_SPEC] * 4,
         out_specs=(HBM_SPEC,) * 5,
         scratch_shapes=[
             pltpu.VMEM((ROW_BLOCKS, HEAD_WIDTH, PAIR), f32),
@@ -424,20 +430,9 @@
             pltpu.VMEM((COL_BLOCKS, BLOCK, 2 * HEAD_WIDTH), bf16),
             pltpu.SemaphoreType.DMA((4 + NZ + NY,)),
         ],
-        compiler_params=vmem(54),
+        compiler_params=vmem(40),
         name="grads",
-    )(plan, kv, kvt, qd, *stats)
-
-
-def turn_call(kv):
-    return pl.pallas_call(
-        turn_kernel,
-        out_shape=jax.ShapeDtypeStruct((COL_BLOCKS, 2 * HEAD_WIDTH, BLOCK), bf16),
-        in_specs=[VMEM_SPEC],
-        out_specs=VMEM_SPEC,
-        compiler_params=vmem(8),
-        name="turn",
-    )(kv)
+    )(plan, kv, qd, *stats)
 
 
 def shift(x, axis, size, by):
@@ -470,29 +465,46 @@
     )(*got, normed_input, grad_out, query_weight)
 
 
-def cols_call(nx, nc, got, turned, key_weight, value_weight, back):
+def cols_call(got, turned):
     model, tokens = turned.shape
-    side = model // nc
-    return pl.pallas_call(
-        functools.partial(cols_kernel, nx, nc),
+    return pl.pallas_call(
+        cols_kernel,
         out_shape=(
             jax.ShapeDtypeStruct((NY, model // NY, 2 * HEAD_WIDTH), bf16),
-            jax.ShapeDtypeStruct((max(model - side, side), tokens), bf16),
-            jax.ShapeDtypeStruct((side, tokens), f32),
-        ),
-        in_specs=[HBM_SPEC] * 5,
-        out_specs=(VMEM_SPEC,) * 3,
+            jax.ShapeDtypeStruct((tokens, 2 * HEAD_WIDTH), bf16),
+        ),
+        in_specs=[HBM_SPEC] * 2,
+        out_specs=(VMEM_SPEC,) * 2,
         scratch_shapes=[
             pltpu.VMEM(got.shape, bf16),
             pltpu.VMEM(turned.shape, bf16),
+            pltpu.SemaphoreType.DMA((2,)),
+        ],
+        compiler_params=vmem(20),
+        name="cols",
+    )(got, turned)
+
+
+def back_call(nx, nc, d, key_weight, value_weight, back):
+    model, tokens = back.shape
+    side = model // nc
+    return pl.pallas_call(
+        functools.partial(back_kernel, nx, nc),
+        out_shape=(
+            jax.ShapeDtypeStruct((max(model - side, side), tokens), bf16),
+            jax.ShapeDtypeStruct((side, tokens), f32),
+        ),
+        in_specs=[VMEM_SPEC] + [HBM_SPEC] * 3,
+        out_specs=(VMEM_SPEC,) * 2,
+        scratch_shapes=[
             pltpu.VMEM(key_weight.shape, bf16),
             pltpu.VMEM(value_weight.shape, bf16),
             pltpu.VMEM(back.shape, f32),
-            pltpu.SemaphoreType.DMA((5,)),
+            pltpu.SemaphoreType.DMA((3,)),
         ],
         compiler_params=vmem(20),
-        name="cols",
-    )(got, turned, key_weight, value_weight, back)
+        name="back",
+    )(d, key_weight, value_weight, back)
 
 
 def ring_gather(own):
@@ -511,8 +523,8 @@
 ):
     model = grad_out.shape[1]
 
-    mine, kv = start_call(queries, keys, values, grad_out, output_weight)
-    pieces = ring_gather(kv)
+    pieces = ring_gather(join_call(keys, values))
+    mine = start_call(queries, grad_out, output_weight)
     before, after = shift(mine, "y", NY, 1), shift(mine, "y", NY, -1)
     half = mine.shape[0] // 2
     qds = [mine, before, after, shift(before[:half], "y", NY, 1), shift(after[half:], "y", NY, -1)]
@@ -521,7 +533,7 @@
     qd = stack_call(qds)
     own, kv = stats_call(plan, pieces, qd)
     stats = [own] + [shift(own, "y", NY, s) for s in range(1, NY)]
-    *row_part, col_part = grads_call(plan, kv, turn_call(kv), qd, stats)
+    *row_part, col_part = grads_call(plan, kv, qd, stats)
 
     col_got = lax.all_to_all(col_part.reshape(NZ, DEV_BLOCKS * BLOCK, 2 * HEAD_WIDTH), "z", 0, 0, tiled=True)
     row_got = [row_part[0]] + [shift(row_part[s], "y", NY, s) for s in range(1, NY)]
@@ -530,7 +542,8 @@
     qo_part, back, turned = rows_call(nx, nc, row_got, normed_input, grad_out, query_weight)
     qo_got = [qo_part[0]] + [shift(qo_part[s], "y", NY, s) for s in range(1, NY)]
 
-    kv_part, send, keep = cols_call(nx, nc, col_got, turned, key_weight, value_weight, back)
+    kv_part, dkv = cols_call(col_got, turned)
+    send, keep = back_call(nx, nc, dkv, key_weight, value_weight, back)
     kv_got = [kv_part[0]] + [shift(kv_part[s], "y", NY, s) for s in range(1, NY)]
     sums = [sum(g.astype(f32) for g in got).astype(bf16) for got in (qo_got, kv_got)]
     sums = jnp.concatenate(sums, axis=1).reshape(NZ, part_rows, 2 * PAIR + 2 * HEAD_WIDTH)

time: 142 us -> 135 us (0.951)
  local copies, waits for them, and re-layouts: 9.57 us -> 6.32 us
  Pallas kernels: 35 us -> 31.9 us
  waiting for transfers between devices: 40.7 us -> 43.1 us
  starting transfers between devices: 52.7 us -> 50.6 us
    unnamed x43 -> x23, local copies, waits for them, and re-layouts: 5.44 us -> 2.3 us
    pallas_call x1, Pallas kernels: 13.8 us -> 11.5 us  [grads_call(): pl.pallas_call(grads_kernel, out_shape=(*[jax.ShapeDtypeStruct((2 * PAIR,...]
    pallas_call x3 -> x4, Pallas kernels: 6.25 us -> 5.63 us  [the longest x1 2.45 us: start_call(): pl.pallas_call(start_kernel, out_shape=jax.ShapeDtypeStruct((queries.shap...]
  transfers between devices with their start and end apart: 30 -> 30, of which waited for: 15 -> 14; matrix products, arithmetic and copies ran while one was open for 5% -> 4% of each run, Pallas kernels for 9% -> 10%
where the time goes in v4:
time: 135 us
  starting transfers between devices  50.6 us (37%)
  waiting for transfers between devices  43.1 us (32%)
  Pallas kernels  31.9 us (24%)
  local copies, waits for them, and re-layouts  6.32 us (5%)
  other arithmetic  2.12 us (2%)
    ppermute x28, starting transfers between devices, shift(): return lax.ppermute(x, axis, [(i, (i + by) % size) for i in range(size)])  39.2 us
    ppermute x28, waiting for transfers between devices, shift(): return lax.ppermute(x, axis, [(i, (i + by) % size) for i in range(size)])  32.6 us
    pallas_call x1, Pallas kernels, grads_call(): pl.pallas_call(grads_kernel, out_shape=(*[jax.ShapeDtypeStruct((2 * PAIR,...  11.5 us
    all_to_all x1, starting transfers between devices, per_device(): lax.all_to_all(col_part.reshape(NZ, DEV_BLOCKS * BLOCK, 2 * HEAD_WIDTH),...  7.95 us
    all_to_all x1, waiting for transfers between devices, per_device(): lax.all_to_all(col_part.reshape(NZ, DEV_BLOCKS * BLOCK, 2 * HEAD_WIDTH),...  7.88 us
    pallas_call x1, Pallas kernels, stats_call(): pl.pallas_call(stats_kernel, out_shape=(jax.ShapeDtypeStruct((3 * STAT_RO...  5.8 us
    pallas_call x1, Pallas kernels, rows_call(): pl.pallas_call(functools.partial(rows_kernel, nx, nc), out_shape=(jax.Sha...  4.73 us
    all_to_all x1, starting transfers between devices, per_device(): lax.all_to_all(sums, 'z', 0, 0, tiled=True).astype(f32)  3.45 us
  transfers between devices with their start and end apart: 30, of which 14 were waited for; matrix products, arithmetic and copies ran while one was open for 4% of the time, Pallas kernels for 10%

profile of v4, /device:TPU:6, one launch (start us, length us, event | category | flops | bytes accessed | tf_op | source)
XLA Modules:
  0.0 135.0 jit_solution(15539561584170742100)
XLA Ops:
  0.6 1.6 %join.1 = bf16[384,256]{1,0:T(8,128)(2,1)} custom-call(bf16[384,128]{1,0:T(8,128)(2,1)} %key_any.1, bf16[384,128]{1,0:T(8,128)(2,1)} %value_any.1), custom_call_target="tpu_custom_call" | custom-call | tf_op jit(solution)/shard_map/join/pallas_call | solution.py:342
  2.3 5.9 %collective-permute-start.3 = (bf16[384,256]{1,0:T(8,128)(2,1)}, bf16[384,256]{1,0:T(8,128)(2,1)S(1)}, u32[]{:S(2)}, u32[]{:S(2)}) collective-permute-start(bf16[384,256]{1,0:T(8,128)(2,1)} %join.1), channel_id=1, source_target_pairs={{0,224},{32,0},{64,32},{96,64},{128,96},{160,128},{192,160},{224,1... | collective-permute-start | bytes 589832 | tf_op jit(solution)/shard_map/ppermute | solution.py:439
  8.2 2.4 %start.1.own = bf16[384,512]{1,0:T(8,128)(2,1)} custom-call(bf16[384,256]{1,0:T(8,128)(2,1)} %query_any.1, bf16[384,1024]{1,0:T(8,128)(2,1)} %grad_any.3, bf16[256,1024]{1,0:T(8,128)(2,1)} %weight_any.1), custom_call_target="tpu_custom_call" | custom-call | tf_op jit(solution)/shard_map/start/pallas_call | solution.py:354
  10.7 3.1 %collective-permute-start.9 = (bf16[384,512]{1,0:T(8,128)(2,1)}, bf16[384,512]{1,0:T(8,128)(2,1)S(1)}, u32[]{:S(2)}, u32[]{:S(2)}) collective-permute-start(bf16[384,512]{1,0:T(8,128)(2,1)} %start.1.own), channel_id=1, source_target_pairs={{0,24},{8,0},{16,8},{24,16},{1,25},{9,1},{17,9},{25,17},{2,26},{10... | collective-permute-start | bytes 1179656 | tf_op jit(solution)/shard_map/ppermute | solution.py:439
  13.8 3.2 %collective-permute-start.4 = (bf16[384,256]{1,0:T(8,128)(2,1)S(1)}, bf16[384,256]{1,0:T(8,128)(2,1)S(1)}, u32[]{:S(2)}, u32[]{:S(2)}) collective-permute-start(bf16[384,256]{1,0:T(8,128)(2,1)S(1)} %collective-permute-done.3), channel_id=1, source_target_pairs={{0,224},{32,0},{64,32},{96,64},{128,96},{160,128},{192,160},{224,1... | collective-permute-start | bytes 589832 | tf_op jit(solution)/shard_map/ppermute | solution.py:439
  17.0 3.3 %collective-permute-done.4 = bf16[384,256]{1,0:T(8,128)(2,1)S(1)} collective-permute-done((bf16[384,256]{1,0:T(8,128)(2,1)S(1)}, bf16[384,256]{1,0:T(8,128)(2,1)S(1)}, u32[]{:S(2)}, u32[]{:S(2)}) %collective-permute-start.4) | collective-permute-done | bytes 196640 | tf_op jit(solution)/shard_map/ppermute | solution.py:439
  20.3 3.7 %collective-permute-start.5 = (bf16[384,256]{1,0:T(8,128)(2,1)S(1)}, bf16[384,256]{1,0:T(8,128)(2,1)S(1)}, u32[]{:S(2)}, u32[]{:S(2)}) collective-permute-start(bf16[384,256]{1,0:T(8,128)(2,1)S(1)} %collective-permute-done.4), channel_id=1, source_target_pairs={{0,224},{32,0},{64,32},{96,64},{128,96},{160,128},{192,160},{224,1... | collective-permute-start | bytes 589832 | tf_op jit(solution)/shard_map/ppermute | solution.py:439
  24.0 3.2 %collective-permute-start.11 = (bf16[192,512]{1,0:T(8,128)(2,1)S(1)}, bf16[192,512]{1,0:T(8,128)(2,1)S(1)}, u32[]{:S(2)}, u32[]{:S(2)}) collective-permute-start(bf16[192,512]{1,0:T(8,128)(2,1)S(1)} %slice.86), channel_id=1, source_target_pairs={{0,24},{8,0},{16,8},{24,16},{1,25},{9,1},{17,9},{25,17},{2,26},{10... | collective-permute-start | bytes 589832 | tf_op jit(solution)/shard_map/ppermute | solution.py:439
  27.4 3.6 %collective-permute-start.7 = (bf16[256,256]{1,0:T(8,128)(2,1)S(1)}, bf16[256,256]{1,0:T(8,128)(2,1)S(1)}, u32[]{:S(2)}, u32[]{:S(2)}) collective-permute-start(bf16[256,256]{1,0:T(8,128)(2,1)S(1)} %slice.84), channel_id=1, source_target_pairs={{0,224},{32,0},{64,32},{96,64},{128,96},{160,128},{192,160},{224,1... | collective-permute-start | bytes 393224 | tf_op jit(solution)/shard_map/ppermute | solution.py:439
  31.7 3.4 %plan.1.plan_any = s32[896]{0:T(1024)} custom-call(s32[16,96]{1,0:T(8,128)} %bitcast.43), custom_call_target="tpu_custom_call" | custom-call | tf_op jit(solution)/shard_map/plan/pallas_call | solution.py:370
  36.0 2.1 %collective-permute-done.6 = bf16[256,256]{1,0:T(8,128)(2,1)S(1)} collective-permute-done((bf16[256,256]{1,0:T(8,128)(2,1)}, bf16[256,256]{1,0:T(8,128)(2,1)S(1)}, u32[]{:S(2)}, u32[]{:S(2)}) %collective-permute-start.6) | collective-permute-done | bytes 131104 | tf_op jit(solution)/shard_map/ppermute | solution.py:439
  38.0 5.8 %stats.1 = (f32[48,256]{1,0:T(8,128)S(1)}, bf16[24,128,256]{2,1,0:T(8,128)(2,1)S(1)}) custom-call(s32[896]{0:T(1024)S(1)} %copy-done.7, bf16[3,128,256]{2,1,0:T(8,128)(2,1)S(1)} %bitcast.34, bf16[3,128,256]{2,1,0:T(8,128)(2,1)S(1)} %bitcast.38, bf16[3,128,256]{2,1,0:T(8,128)(2,1)S(1)} %bitcast.40, bf16[3,128,256]{2,1,0:T(8,128)(2,1)S(1)} %bitcast.36, ...), custom_call_target="tpu_custom_call" | custom-call | tf_op jit(solution)/shard_map/stats/pallas_call | solution.py:392
  44.1 1.5 %collective-permute-start.13 = (f32[48,256]{1,0:T(8,128)S(1)}, f32[48,256]{1,0:T(8,128)S(1)}, u32[]{:S(2)}, u32[]{:S(2)}) collective-permute-start(f32[48,256]{1,0:T(8,128)S(1)} %get-tuple-element.20.st0), channel_id=1, source_target_pairs={{0,16},{8,24},{16,0},{24,8},{1,17},{9,25},{17,1},{25,9},{2,18},{10... | collective-permute-start | bytes 147464 | tf_op jit(solution)/shard_map/ppermute | solution.py:439
  46.0 2.0 %collective-permute-done.14.st3 = f32[48,256]{1,0:T(8,128)S(1)} collective-permute-done((f32[48,256]{1,0:T(8,128)S(1)}, f32[48,256]{1,0:T(8,128)S(1)}, u32[]{:S(2)}, u32[]{:S(2)}) %collective-permute-start.14) | collective-permute-done | bytes 49184 | tf_op jit(solution)/shard_map/ppermute | solution.py:439
  48.0 1.8 %collective-permute-done.13.st2 = f32[48,256]{1,0:T(8,128)S(1)} collective-permute-done((f32[48,256]{1,0:T(8,128)S(1)}, f32[48,256]{1,0:T(8,128)S(1)}, u32[]{:S(2)}, u32[]{:S(2)}) %collective-permute-start.13) | collective-permute-done | bytes 49184 | tf_op jit(solution)/shard_map/ppermute | solution.py:439
  50.9 11.5 %grads.1 = (bf16[512,384]{1,0:T(8,128)(2,1)S(1)}, bf16[512,384]{1,0:T(8,128)(2,1)S(1)}, bf16[512,384]{1,0:T(8,128)(2,1)S(1)}, bf16[512,384]{1,0:T(8,128)(2,1)S(1)}, bf16[24,128,256]{2,1,0:T(8,128)(2,1)}) custom-call(s32[896]{0:T(1024)S(1)} %copy-done.7, bf16[24,128,256]{2,1,0:T(8,128)(2,1)S(1)} %get-tuple-element.19.kv_any, ...), custom_call_target="tpu_custom_call" | custom-call | tf_op jit(solution)/shard_map/grads/pallas_call | solution.py:410
  63.2 7.9 %all-to-all-start = ((bf16[8,384,256]{2,1,0:T(8,128)(2,1)}), bf16[8,384,256]{2,1,0:T(8,128)(2,1)S(1)}, u32[]{:S(2)}, u32[]{:S(2)}) async-start(bf16[8,384,256]{2,1,0:T(8,128)(2,1)} %bitcast.10), calls=%async_computation | async-start | bytes 3145728 | tf_op jit(solution)/shard_map/all_to_all | solution.py:538
  72.0 2.4 %collective-permute-start.17 = (bf16[512,384]{1,0:T(8,128)(2,1)S(1)}, bf16[512,384]{1,0:T(8,128)(2,1)S(1)}, u32[]{:S(2)}, u32[]{:S(2)}) collective-permute-start(bf16[512,384]{1,0:T(8,128)(2,1)S(1)} %get-tuple-element.25), channel_id=1, source_target_pairs={{0,24},{8,0},{16,8},{24,16},{1,25},{9,1},{17,9},{25,17},{2,26},{10... | collective-permute-start | bytes 1179656 | tf_op jit(solution)/shard_map/ppermute | solution.py:439
  74.4 11.9 %collective-permute-done.15.row1 = bf16[512,384]{1,0:T(8,128)(2,1)S(1)} collective-permute-done((bf16[512,384]{1,0:T(8,128)(2,1)S(1)}, bf16[512,384]{1,0:T(8,128)(2,1)S(1)}, u32[]{:S(2)}, u32[]{:S(2)}) %collective-permute-start.15) | collective-permute-done | bytes 393248 | tf_op jit(solution)/shard_map/ppermute | solution.py:439
  87.7 4.7 %rows.1 = (bf16[4,256,512]{2,1,0:T(8,128)(2,1)}, f32[1024,384]{1,0:T(8,128)}, bf16[1024,384]{1,0:T(8,128)(2,1)}) custom-call(bf16[512,384]{1,0:T(8,128)(2,1)} %copy-done.4, bf16[512,384]{1,0:T(8,128)(2,1)} %copy-done.8, bf16[512,384]{1,0:T(8,128)(2,1)} %copy-done.9, bf16[512,384]{1,0:T(8,128)(2,1)} %copy-done.10, bf16[384,1024]{1,0:T(8,128)(2,1)} %input_any.1, ...), custom_call_target="tpu_custom_call" | custom-call | tf_op jit(solution)/shard_map/rows/pallas_call | solution.py:444
  92.4 2.0 %slice_bitcast_fusion.2 = (bf16[256,512]{1,0:T(8,128)(2,1)}, bf16[256,512]{1,0:T(8,128)(2,1)}, bf16[256,512]{1,0:T(8,128)(2,1)S(1)}) fusion(bf16[4,256,512]{2,1,0:T(8,128)(2,1)} %get-tuple-element.31), kind=kLoop, calls=%fused_computation.13 | loop fusion | bytes 1572864 | tf_op jit(solution)/shard_map/squeeze | solution.py:543
  94.6 3.0 %collective-permute-start.24 = (bf16[256,512]{1,0:T(8,128)(2,1)}, bf16[256,512]{1,0:T(8,128)(2,1)S(1)}, u32[]{:S(2)}, u32[]{:S(2)}) collective-permute-start(bf16[256,512]{1,0:T(8,128)(2,1)} %get-tuple-element.41), channel_id=1, source_target_pairs={{0,24},{8,0},{16,8},{24,16},{1,25},{9,1},{17,9},{25,17},{2,26},{10... | collective-permute-start | bytes 786440 | tf_op jit(solution)/shard_map/ppermute | solution.py:439
  98.2 7.9 %all-to-all-done.got_any = bf16[8,384,256]{2,1,0:T(8,128)(2,1)S(1)} async-done(((bf16[8,384,256]{2,1,0:T(8,128)(2,1)}), bf16[8,384,256]{2,1,0:T(8,128)(2,1)S(1)}, u32[]{:S(2)}, u32[]{:S(2)}) %all-to-all-start) | async-done | bytes 1572896 | tf_op jit(solution)/shard_map/all_to_all | solution.py:538
  107.0 3.2 %collective-permute-start.27 = (bf16[256,256]{1,0:T(8,128)(2,1)S(1)}, bf16[256,256]{1,0:T(8,128)(2,1)S(1)}, u32[]{:S(2)}, u32[]{:S(2)}) collective-permute-start(bf16[256,256]{1,0:T(8,128)(2,1)S(1)} %get-tuple-element.44), channel_id=1, source_target_pairs={{0,24},{8,0},{16,8},{24,16},{1,25},{9,1},{17,9},{25,17},{2,26},{10... | collective-permute-start | bytes 393224 | tf_op jit(solution)/shard_map/ppermute | solution.py:439
  113.6 4.0 %collective-permute-done.26 = bf16[256,256]{1,0:T(8,128)(2,1)S(1)} collective-permute-done((bf16[256,256]{1,0:T(8,128)(2,1)S(1)}, bf16[256,256]{1,0:T(8,128)(2,1)S(1)}, u32[]{:S(2)}, u32[]{:S(2)}) %collective-permute-start.26) | collective-permute-done | bytes 131104 | tf_op jit(solution)/shard_map/ppermute | solution.py:439
  118.4 3.5 %all-to-all-start.1 = ((bf16[8,32,768]{2,1,0:T(8,128)(2,1)}), bf16[8,32,768]{2,1,0:T(8,128)(2,1)S(1)}, u32[]{:S(2)}, u32[]{:S(2)}) async-start(bf16[8,32,768]{2,1,0:T(8,128)(2,1)} %bitcast.20), calls=%async_computation.1 | async-start | bytes 786432 | tf_op jit(solution)/shard_map/all_to_all | solution.py:550
  122.6 1.5 %collective-permute-start.21 = (bf16[128,384]{1,0:T(8,128)(2,1)S(1)}, bf16[128,384]{1,0:T(8,128)(2,1)S(1)}, u32[]{:S(2)}, u32[]{:S(2)}) collective-permute-start(bf16[128,384]{1,0:T(8,128)(2,1)S(1)} %get-tuple-element.47), channel_id=1, source_target_pairs={{0,6},{2,0},{4,2},{6,4},{1,7},{3,1},{5,3},{7,5},{8,14},{10,8},{12,... | collective-permute-start | bytes 294920 | tf_op jit(solution)/shard_map/ppermute | solution.py:439
  124.2 1.4 %collective-permute-start.20 = (bf16[128,384]{1,0:T(8,128)(2,1)S(1)}, bf16[128,384]{1,0:T(8,128)(2,1)S(1)}, u32[]{:S(2)}, u32[]{:S(2)}) collective-permute-start(bf16[128,384]{1,0:T(8,128)(2,1)S(1)} %get-tuple-element.48), channel_id=1, source_target_pairs={{0,4},{2,6},{4,0},{6,2},{1,5},{3,7},{5,1},{7,3},{8,12},{10,14},{12... | collective-permute-start | bytes 294920 | tf_op jit(solution)/shard_map/ppermute | solution.py:439
  125.6 1.2 collective-permute-done.19
  126.7 1.7 %collective-permute-done.21 = bf16[128,384]{1,0:T(8,128)(2,1)S(1)} collective-permute-done((bf16[128,384]{1,0:T(8,128)(2,1)S(1)}, bf16[128,384]{1,0:T(8,128)(2,1)S(1)}, u32[]{:S(2)}, u32[]{:S(2)}) %collective-permute-start.21) | collective-permute-done | bytes 98336 | tf_op jit(solution)/shard_map/ppermute | solution.py:439
  128.4 1.8 %collective-permute-done.20 = bf16[128,384]{1,0:T(8,128)(2,1)S(1)} collective-permute-done((bf16[128,384]{1,0:T(8,128)(2,1)S(1)}, bf16[128,384]{1,0:T(8,128)(2,1)S(1)}, u32[]{:S(2)}, u32[]{:S(2)}) %collective-permute-start.20) | collective-permute-done | bytes 98336 | tf_op jit(solution)/shard_map/ppermute | solution.py:439
  131.1 2.6 %all-to-all-done.1 = bf16[8,32,768]{2,1,0:T(8,128)(2,1)S(1)} async-done(((bf16[8,32,768]{2,1,0:T(8,128)(2,1)}), bf16[8,32,768]{2,1,0:T(8,128)(2,1)S(1)}, u32[]{:S(2)}, u32[]{:S(2)}) %all-to-all-start.1) | async-done | bytes 393248 | tf_op jit(solution)/shard_map/all_to_all | solution.py:550
  (75 shorter events, 15.0 us)
Async XLA Ops:
  2.3 11.5 %collective-permute-start.3 = (bf16[384,256]{1,0:T(8,128)(2,1)}, bf16[384,256]{1,0:T(8,128)(2,1)S(1)}, u32[]{:S(2)}, u32[]{:S(2)}) collective-permute-start(bf16[384,256]{1,0:T(8,128)(2,1)} %join.1), channel_id=1, source_target_pairs={{0,224},{32,0},{64,32},{96,64},{128,96},{160,128},{192,160},{224,1... | collective-permute-start | bytes 589832 | tf_op jit(solution)/shard_map/ppermute | solution.py:439
  8.2 8.8 %collective-permute-start = (bf16[384,256]{1,0:T(8,128)(2,1)}, bf16[384,256]{1,0:T(8,128)(2,1)S(1)}, u32[]{:S(2)}, u32[]{:S(2)}) collective-permute-start(bf16[384,256]{1,0:T(8,128)(2,1)} %join.1), channel_id=1, source_target_pairs={{0,32},{32,64},{64,96},{96,128},{128,160},{160,192},{192,224},{224... | collective-permute-start | bytes 589832 | tf_op jit(solution)/shard_map/ppermute | solution.py:439
  10.7 24.4 %copy-start.1 = (bf16[384,512]{1,0:T(8,128)(2,1)S(1)}, bf16[384,512]{1,0:T(8,128)(2,1)}, u32[]{:S(2)}) copy-start(bf16[384,512]{1,0:T(8,128)(2,1)} %start.1.own) | copy-start | bytes 1179652
  10.7 13.4 %collective-permute-start.9 = (bf16[384,512]{1,0:T(8,128)(2,1)}, bf16[384,512]{1,0:T(8,128)(2,1)S(1)}, u32[]{:S(2)}, u32[]{:S(2)}) collective-permute-start(bf16[384,512]{1,0:T(8,128)(2,1)} %start.1.own), channel_id=1, source_target_pairs={{0,24},{8,0},{16,8},{24,16},{1,25},{9,1},{17,9},{25,17},{2,26},{10... | collective-permute-start | bytes 1179656 | tf_op jit(solution)/shard_map/ppermute | solution.py:439
  13.8 13.5 %collective-permute-start.8 = (bf16[384,512]{1,0:T(8,128)(2,1)}, bf16[384,512]{1,0:T(8,128)(2,1)S(1)}, u32[]{:S(2)}, u32[]{:S(2)}) collective-permute-start(bf16[384,512]{1,0:T(8,128)(2,1)} %start.1.own), channel_id=1, source_target_pairs={{0,8},{8,16},{16,24},{24,0},{1,9},{9,17},{17,25},{25,1},{2,10},{10... | collective-permute-start | bytes 1179656 | tf_op jit(solution)/shard_map/ppermute | solution.py:439
  13.8 6.5 %collective-permute-start.4 = (bf16[384,256]{1,0:T(8,128)(2,1)S(1)}, bf16[384,256]{1,0:T(8,128)(2,1)S(1)}, u32[]{:S(2)}, u32[]{:S(2)}) collective-permute-start(bf16[384,256]{1,0:T(8,128)(2,1)S(1)} %collective-permute-done.3), channel_id=1, source_target_pairs={{0,224},{32,0},{64,32},{96,64},{128,96},{160,128},{192,160},{224,1... | collective-permute-start | bytes 589832 | tf_op jit(solution)/shard_map/ppermute | solution.py:439
  17.0 7.0 %collective-permute-start.1 = (bf16[384,256]{1,0:T(8,128)(2,1)S(1)}, bf16[384,256]{1,0:T(8,128)(2,1)S(1)}, u32[]{:S(2)}, u32[]{:S(2)}) collective-permute-start(bf16[384,256]{1,0:T(8,128)(2,1)S(1)} %collective-permute-done), channel_id=1, source_target_pairs={{0,32},{32,64},{64,96},{96,128},{128,160},{160,192},{192,224},{224... | collective-permute-start | bytes 589832 | tf_op jit(solution)/shard_map/ppermute | solution.py:439
  20.3 7.0 %collective-permute-start.5 = (bf16[384,256]{1,0:T(8,128)(2,1)S(1)}, bf16[384,256]{1,0:T(8,128)(2,1)S(1)}, u32[]{:S(2)}, u32[]{:S(2)}) collective-permute-start(bf16[384,256]{1,0:T(8,128)(2,1)S(1)} %collective-permute-done.4), channel_id=1, source_target_pairs={{0,224},{32,0},{64,32},{96,64},{128,96},{160,128},{192,160},{224,1... | collective-permute-start | bytes 589832 | tf_op jit(solution)/shard_map/ppermute | solution.py:439
  24.0 7.0 %collective-permute-start.2 = (bf16[384,256]{1,0:T(8,128)(2,1)S(1)}, bf16[384,256]{1,0:T(8,128)(2,1)S(1)}, u32[]{:S(2)}, u32[]{:S(2)}) collective-permute-start(bf16[384,256]{1,0:T(8,128)(2,1)S(1)} %collective-permute-done.1), channel_id=1, source_target_pairs={{0,32},{32,64},{64,96},{96,128},{128,160},{160,192},{192,224},{224... | collective-permute-start | bytes 589832 | tf_op jit(solution)/shard_map/ppermute | solution.py:439
  24.0 11.0 %collective-permute-start.11 = (bf16[192,512]{1,0:T(8,128)(2,1)S(1)}, bf16[192,512]{1,0:T(8,128)(2,1)S(1)}, u32[]{:S(2)}, u32[]{:S(2)}) collective-permute-start(bf16[192,512]{1,0:T(8,128)(2,1)S(1)} %slice.86), channel_id=1, source_target_pairs={{0,24},{8,0},{16,8},{24,16},{1,25},{9,1},{17,9},{25,17},{2,26},{10... | collective-permute-start | bytes 589832 | tf_op jit(solution)/shard_map/ppermute | solution.py:439
  27.3 7.8 %collective-permute-start.10 = (bf16[192,512]{1,0:T(8,128)(2,1)S(1)}, bf16[192,512]{1,0:T(8,128)(2,1)S(1)}, u32[]{:S(2)}, u32[]{:S(2)}) collective-permute-start(bf16[192,512]{1,0:T(8,128)(2,1)S(1)} %slice.85), channel_id=1, source_target_pairs={{0,8},{8,16},{16,24},{24,0},{1,9},{9,17},{17,25},{25,1},{2,10},{10... | collective-permute-start | bytes 589832 | tf_op jit(solution)/shard_map/ppermute | solution.py:439
  27.4 8.6 %collective-permute-start.7 = (bf16[256,256]{1,0:T(8,128)(2,1)S(1)}, bf16[256,256]{1,0:T(8,128)(2,1)S(1)}, u32[]{:S(2)}, u32[]{:S(2)}) collective-permute-start(bf16[256,256]{1,0:T(8,128)(2,1)S(1)} %slice.84), channel_id=1, source_target_pairs={{0,224},{32,0},{64,32},{96,64},{128,96},{160,128},{192,160},{224,1... | collective-permute-start | bytes 393224 | tf_op jit(solution)/shard_map/ppermute | solution.py:439
  31.7 6.4 %collective-permute-start.6 = (bf16[256,256]{1,0:T(8,128)(2,1)}, bf16[256,256]{1,0:T(8,128)(2,1)S(1)}, u32[]{:S(2)}, u32[]{:S(2)}) collective-permute-start(bf16[256,256]{1,0:T(8,128)(2,1)} %slice.83), channel_id=1, source_target_pairs={{0,32},{32,64},{64,96},{96,128},{128,160},{160,192},{192,224},{224... | collective-permute-start | bytes 393224 | tf_op jit(solution)/shard_map/ppermute | solution.py:439
  43.9 4.2 %collective-permute-start.14 = (f32[48,256]{1,0:T(8,128)S(1)}, f32[48,256]{1,0:T(8,128)S(1)}, u32[]{:S(2)}, u32[]{:S(2)}) collective-permute-start(f32[48,256]{1,0:T(8,128)S(1)} %get-tuple-element.20.st0), channel_id=1, source_target_pairs={{0,24},{8,0},{16,8},{24,16},{1,25},{9,1},{17,9},{25,17},{2,26},{10... | collective-permute-start | bytes 147464 | tf_op jit(solution)/shard_map/ppermute | solution.py:439
  44.1 5.7 %collective-permute-start.13 = (f32[48,256]{1,0:T(8,128)S(1)}, f32[48,256]{1,0:T(8,128)S(1)}, u32[]{:S(2)}, u32[]{:S(2)}) collective-permute-start(f32[48,256]{1,0:T(8,128)S(1)} %get-tuple-element.20.st0), channel_id=1, source_target_pairs={{0,16},{8,24},{16,0},{24,8},{1,17},{9,25},{17,1},{25,9},{2,18},{10... | collective-permute-start | bytes 147464 | tf_op jit(solution)/shard_map/ppermute | solution.py:439
  45.6 5.3 %collective-permute-start.12 = (f32[48,256]{1,0:T(8,128)S(1)}, f32[48,256]{1,0:T(8,128)S(1)}, u32[]{:S(2)}, u32[]{:S(2)}) collective-permute-start(f32[48,256]{1,0:T(8,128)S(1)} %get-tuple-element.20.st0), channel_id=1, source_target_pairs={{0,8},{8,16},{16,24},{24,0},{1,9},{9,17},{17,25},{25,1},{2,10},{10... | collective-permute-start | bytes 147464 | tf_op jit(solution)/shard_map/ppermute | solution.py:439
  63.2 42.9 %all-to-all-start = ((bf16[8,384,256]{2,1,0:T(8,128)(2,1)}), bf16[8,384,256]{2,1,0:T(8,128)(2,1)S(1)}, u32[]{:S(2)}, u32[]{:S(2)}) async-start(bf16[8,384,256]{2,1,0:T(8,128)(2,1)} %bitcast.10), calls=%async_computation | async-start | bytes 3145728 | tf_op jit(solution)/shard_map/all_to_all | solution.py:538
  71.1 15.1 %collective-permute-start.15 = (bf16[512,384]{1,0:T(8,128)(2,1)S(1)}, bf16[512,384]{1,0:T(8,128)(2,1)S(1)}, u32[]{:S(2)}, u32[]{:S(2)}) collective-permute-start(bf16[512,384]{1,0:T(8,128)(2,1)S(1)} %get-tuple-element.23), channel_id=1, source_target_pairs={{0,8},{8,16},{16,24},{24,0},{1,9},{9,17},{17,25},{25,1},{2,10},{10... | collective-permute-start | bytes 1179656 | tf_op jit(solution)/shard_map/ppermute | solution.py:439
  71.2 15.1 %collective-permute-start.16 = (bf16[512,384]{1,0:T(8,128)(2,1)S(1)}, bf16[512,384]{1,0:T(8,128)(2,1)S(1)}, u32[]{:S(2)}, u32[]{:S(2)}) collective-permute-start(bf16[512,384]{1,0:T(8,128)(2,1)S(1)} %get-tuple-element.24), channel_id=1, source_target_pairs={{0,16},{8,24},{16,0},{24,8},{1,17},{9,25},{17,1},{25,9},{2,18},{10... | collective-permute-start | bytes 1179656 | tf_op jit(solution)/shard_map/ppermute | solution.py:439
  72.0 14.9 %collective-permute-start.17 = (bf16[512,384]{1,0:T(8,128)(2,1)S(1)}, bf16[512,384]{1,0:T(8,128)(2,1)S(1)}, u32[]{:S(2)}, u32[]{:S(2)}) collective-permute-start(bf16[512,384]{1,0:T(8,128)(2,1)S(1)} %get-tuple-element.25), channel_id=1, source_target_pairs={{0,24},{8,0},{16,8},{24,16},{1,25},{9,1},{17,9},{25,17},{2,26},{10... | collective-permute-start | bytes 1179656 | tf_op jit(solution)/shard_map/ppermute | solution.py:439
  92.4 13.7 %copy-start.3 = (bf16[1024,384]{1,0:T(8,128)(2,1)S(1)}, bf16[1024,384]{1,0:T(8,128)(2,1)}, u32[]{:S(2)}) copy-start(bf16[1024,384]{1,0:T(8,128)(2,1)} %get-tuple-element.26.turned_any) | copy-start | bytes 2359300
  94.4 16.6 %collective-permute-start.22 = (bf16[256,512]{1,0:T(8,128)(2,1)}, bf16[256,512]{1,0:T(8,128)(2,1)S(1)}, u32[]{:S(2)}, u32[]{:S(2)}) collective-permute-start(bf16[256,512]{1,0:T(8,128)(2,1)} %get-tuple-element.40), channel_id=1, source_target_pairs={{0,8},{8,16},{16,24},{24,0},{1,9},{9,17},{17,25},{25,1},{2,10},{10... | collective-permute-start | bytes 786440 | tf_op jit(solution)/shard_map/ppermute | solution.py:439
  94.6 16.5 %collective-permute-start.24 = (bf16[256,512]{1,0:T(8,128)(2,1)}, bf16[256,512]{1,0:T(8,128)(2,1)S(1)}, u32[]{:S(2)}, u32[]{:S(2)}) collective-permute-start(bf16[256,512]{1,0:T(8,128)(2,1)} %get-tuple-element.41), channel_id=1, source_target_pairs={{0,24},{8,0},{16,8},{24,16},{1,25},{9,1},{17,9},{25,17},{2,26},{10... | collective-permute-start | bytes 786440 | tf_op jit(solution)/shard_map/ppermute | solution.py:439
  97.7 13.8 %collective-permute-start.23 = (bf16[256,512]{1,0:T(8,128)(2,1)S(1)}, bf16[256,512]{1,0:T(8,128)(2,1)S(1)}, u32[]{:S(2)}, u32[]{:S(2)}) collective-permute-start(bf16[256,512]{1,0:T(8,128)(2,1)S(1)} %get-tuple-element.42), channel_id=1, source_target_pairs={{0,16},{8,24},{16,0},{24,8},{1,17},{9,25},{17,1},{25,9},{2,18},{10... | collective-permute-start | bytes 786440 | tf_op jit(solution)/shard_map/ppermute | solution.py:439
  107.0 6.6 %collective-permute-start.25 = (bf16[256,256]{1,0:T(8,128)(2,1)S(1)}, bf16[256,256]{1,0:T(8,128)(2,1)S(1)}, u32[]{:S(2)}, u32[]{:S(2)}) collective-permute-start(bf16[256,256]{1,0:T(8,128)(2,1)S(1)} %get-tuple-element.43), channel_id=1, source_target_pairs={{0,8},{8,16},{16,24},{24,0},{1,9},{9,17},{17,25},{25,1},{2,10},{10... | collective-permute-start | bytes 393224 | tf_op jit(solution)/shard_map/ppermute | solution.py:439
  107.0 6.5 %collective-permute-start.27 = (bf16[256,256]{1,0:T(8,128)(2,1)S(1)}, bf16[256,256]{1,0:T(8,128)(2,1)S(1)}, u32[]{:S(2)}, u32[]{:S(2)}) collective-permute-start(bf16[256,256]{1,0:T(8,128)(2,1)S(1)} %get-tuple-element.44), channel_id=1, source_target_pairs={{0,24},{8,0},{16,8},{24,16},{1,25},{9,1},{17,9},{25,17},{2,26},{10... | collective-permute-start | bytes 393224 | tf_op jit(solution)/shard_map/ppermute | solution.py:439
  111.0 6.6 %collective-permute-start.26 = (bf16[256,256]{1,0:T(8,128)(2,1)S(1)}, bf16[256,256]{1,0:T(8,128)(2,1)S(1)}, u32[]{:S(2)}, u32[]{:S(2)}) collective-permute-start(bf16[256,256]{1,0:T(8,128)(2,1)S(1)} %get-tuple-element.45), channel_id=1, source_target_pairs={{0,16},{8,24},{16,0},{24,8},{1,17},{9,25},{17,1},{25,9},{2,18},{10... | collective-permute-start | bytes 393224 | tf_op jit(solution)/shard_map/ppermute | solution.py:439
  111.1 10.8 %collective-permute-start.18 = (bf16[512,384]{1,0:T(8,128)(2,1)S(1)}, bf16[512,384]{1,0:T(8,128)(2,1)S(1)}, u32[]{:S(2)}, u32[]{:S(2)}) collective-permute-start(bf16[512,384]{1,0:T(8,128)(2,1)S(1)} %get-tuple-element.30), channel_id=1, source_target_pairs={{0,1},{1,0},{2,3},{3,2},{4,5},{5,4},{6,7},{7,6},{8,9},{9,8},{10,11... | collective-permute-start | bytes 1179656 | tf_op jit(solution)/shard_map/ppermute | solution.py:439
  118.4 15.3 %all-to-all-start.1 = ((bf16[8,32,768]{2,1,0:T(8,128)(2,1)}), bf16[8,32,768]{2,1,0:T(8,128)(2,1)S(1)}, u32[]{:S(2)}, u32[]{:S(2)}) async-start(bf16[8,32,768]{2,1,0:T(8,128)(2,1)} %bitcast.20), calls=%async_computation.1 | async-start | bytes 786432 | tf_op jit(solution)/shard_map/all_to_all | solution.py:550
  122.0 4.7 %collective-permute-start.19 = (bf16[128,384]{1,0:T(8,128)(2,1)S(1)}, bf16[128,384]{1,0:T(8,128)(2,1)S(1)}, u32[]{:S(2)}, u32[]{:S(2)}) collective-permute-start(bf16[128,384]{1,0:T(8,128)(2,1)S(1)} %get-tuple-element.46), channel_id=1, source_target_pairs={{0,2},{2,4},{4,6},{6,0},{1,3},{3,5},{5,7},{7,1},{8,10},{10,12},{12... | collective-permute-start | bytes 294920 | tf_op jit(solution)/shard_map/ppermute | solution.py:439
  122.6 5.8 %collective-permute-start.21 = (bf16[128,384]{1,0:T(8,128)(2,1)S(1)}, bf16[128,384]{1,0:T(8,128)(2,1)S(1)}, u32[]{:S(2)}, u32[]{:S(2)}) collective-permute-start(bf16[128,384]{1,0:T(8,128)(2,1)S(1)} %get-tuple-element.47), channel_id=1, source_target_pairs={{0,6},{2,0},{4,2},{6,4},{1,7},{3,1},{5,3},{7,5},{8,14},{10,8},{12,... | collective-permute-start | bytes 294920 | tf_op jit(solution)/shard_map/ppermute | solution.py:439
  124.2 6.1 %collective-permute-start.20 = (bf16[128,384]{1,0:T(8,128)(2,1)S(1)}, bf16[128,384]{1,0:T(8,128)(2,1)S(1)}, u32[]{:S(2)}, u32[]{:S(2)}) collective-permute-start(bf16[128,384]{1,0:T(8,128)(2,1)S(1)} %get-tuple-element.48), channel_id=1, source_target_pairs={{0,4},{2,6},{4,0},{6,2},{1,5},{3,7},{5,1},{7,3},{8,12},{10,14},{12... | collective-permute-start | bytes 294920 | tf_op jit(solution)/shard_map/ppermute | solution.py:439
  (9 other events, 21.7 us)

commit v5 on v4

--- a/solution.py
+++ b/solution.py
@@ -507,15 +507,17 @@
     )(d, key_weight, value_weight, back)
 
 
-def ring_gather(own):
+def ring_gather(own, plan):
     up, down = [own], [own]
-    for _ in range(3):
+    for step in range(3):
         up.append(shift(up[-1], "z", NZ, 1))
         down.append(shift(down[-1], "z", NZ, -1))
+        if step == 1:
+            up[-1], plan = lax.optimization_barrier((up[-1], plan))
     pieces = [p.reshape(DEV_BLOCKS, BLOCK, 2 * HEAD_WIDTH) for p in up + down[:0:-1]]
     top = shift(up[-1][: 2 * BLOCK], "z", NZ, 1)
     bottom = shift(down[-1][BLOCK:], "z", NZ, -1)
-    return pieces + [top.reshape(2, BLOCK, 2 * HEAD_WIDTH), bottom.reshape(2, BLOCK, 2 * HEAD_WIDTH)]
+    return plan, pieces + [top.reshape(2, BLOCK, 2 * HEAD_WIDTH), bottom.reshape(2, BLOCK, 2 * HEAD_WIDTH)]
 
 
 def per_device(
@@ -523,13 +525,12 @@
 ):
     model = grad_out.shape[1]
 
-    pieces = ring_gather(join_call(keys, values))
+    plan, pieces = ring_gather(join_call(keys, values), plan_call(ancestors.T))
     mine = start_call(queries, grad_out, output_weight)
     before, after = shift(mine, "y", NY, 1), shift(mine, "y", NY, -1)
     half = mine.shape[0] // 2
     qds = [mine, before, after, shift(before[:half], "y", NY, 1), shift(after[half:], "y", NY, -1)]
 
-    plan = plan_call(ancestors.T)
     qd = stack_call(qds)
     own, kv = stats_call(plan, pieces, qd)
     stats = [own] + [shift(own, "y", NY, s) for s in range(1, NY)]

time: 135 us -> 135 us (level); the launches traced: 135 us -> 132 us
  starting transfers between devices: 50.6 us -> 49 us
    all_to_all x1, starting transfers between devices: 7.95 us -> 6.34 us  [per_device(): lax.all_to_all(col_part.reshape(NZ, DEV_BLOCKS * BLOCK, 2 * HEAD_WIDTH),...]
where the time goes in v5:
time: 135 us; the launch traced here: 132 us
  starting transfers between devices  49 us (36%)
  waiting for transfers between devices  42.8 us (32%)
  Pallas kernels  31.9 us (24%)
  local copies, waits for them, and re-layouts  5.67 us (4%)
  other arithmetic  2.12 us (2%)
    ppermute x28, starting transfers between devices, shift(): return lax.ppermute(x, axis, [(i, (i + by) % size) for i in range(size)])  39.2 us
    ppermute x28, waiting for transfers between devices, shift(): return lax.ppermute(x, axis, [(i, (i + by) % size) for i in range(size)])  32.3 us
    pallas_call x1, Pallas kernels, grads_call(): pl.pallas_call(grads_kernel, out_shape=(*[jax.ShapeDtypeStruct((2 * PAIR,...  11.5 us
    all_to_all x1, waiting for transfers between devices, per_device(): lax.all_to_all(col_part.reshape(NZ, DEV_BLOCKS * BLOCK, 2 * HEAD_WIDTH),...  7.87 us
    all_to_all x1, starting transfers between devices, per_device(): lax.all_to_all(col_part.reshape(NZ, DEV_BLOCKS * BLOCK, 2 * HEAD_WIDTH),...  6.34 us
    pallas_call x1, Pallas kernels, stats_call(): pl.pallas_call(stats_kernel, out_shape=(jax.ShapeDtypeStruct((3 * STAT_RO...  5.8 us
    pallas_call x1, Pallas kernels, rows_call(): pl.pallas_call(functools.partial(rows_kernel, nx, nc), out_shape=(jax.Sha...  4.73 us
    all_to_all x1, starting transfers between devices, per_device(): lax.all_to_all(sums, 'z', 0, 0, tiled=True).astype(f32)  3.45 us
  transfers between devices with their start and end apart: 30, of which 14 were waited for; matrix products, arithmetic and copies ran while one was open for 4% of the time, Pallas kernels for 10%

profile of v5, /device:TPU:6, one launch (start us, length us, event | category | flops | bytes accessed | tf_op | source)
XLA Modules:
  0.0 132.5 jit_solution(4082448780671385362)
XLA Ops:
  0.6 1.6 %join.1 = bf16[384,256]{1,0:T(8,128)(2,1)} custom-call(bf16[384,128]{1,0:T(8,128)(2,1)} %key_any.1, bf16[384,128]{1,0:T(8,128)(2,1)} %value_any.1), custom_call_target="tpu_custom_call" | custom-call | tf_op jit(solution)/shard_map/join/pallas_call | solution.py:342
  2.3 5.9 %collective-permute-start.3 = (bf16[384,256]{1,0:T(8,128)(2,1)}, bf16[384,256]{1,0:T(8,128)(2,1)S(1)}, u32[]{:S(2)}, u32[]{:S(2)}) collective-permute-start(bf16[384,256]{1,0:T(8,128)(2,1)} %join.1), channel_id=1, source_target_pairs={{0,224},{32,0},{64,32},{96,64},{128,96},{160,128},{192,160},{224,1... | collective-permute-start | bytes 589832 | tf_op jit(solution)/shard_map/ppermute | solution.py:439
  8.2 2.4 %start.1.own = bf16[384,512]{1,0:T(8,128)(2,1)} custom-call(bf16[384,256]{1,0:T(8,128)(2,1)} %query_any.1, bf16[384,1024]{1,0:T(8,128)(2,1)} %grad_any.3, bf16[256,1024]{1,0:T(8,128)(2,1)} %weight_any.1), custom_call_target="tpu_custom_call" | custom-call | tf_op jit(solution)/shard_map/start/pallas_call | solution.py:354
  10.7 3.1 %collective-permute-start.9 = (bf16[384,512]{1,0:T(8,128)(2,1)}, bf16[384,512]{1,0:T(8,128)(2,1)S(1)}, u32[]{:S(2)}, u32[]{:S(2)}) collective-permute-start(bf16[384,512]{1,0:T(8,128)(2,1)} %start.1.own), channel_id=1, source_target_pairs={{0,24},{8,0},{16,8},{24,16},{1,25},{9,1},{17,9},{25,17},{2,26},{10... | collective-permute-start | bytes 1179656 | tf_op jit(solution)/shard_map/ppermute | solution.py:439
  13.8 3.2 %collective-permute-start.4 = (bf16[384,256]{1,0:T(8,128)(2,1)S(1)}, bf16[384,256]{1,0:T(8,128)(2,1)S(1)}, u32[]{:S(2)}, u32[]{:S(2)}) collective-permute-start(bf16[384,256]{1,0:T(8,128)(2,1)S(1)} %collective-permute-done.3), channel_id=1, source_target_pairs={{0,224},{32,0},{64,32},{96,64},{128,96},{160,128},{192,160},{224,1... | collective-permute-start | bytes 589832 | tf_op jit(solution)/shard_map/ppermute | solution.py:439
  17.0 3.4 %plan.1.plan_any = s32[896]{0:T(1024)} custom-call(s32[16,96]{1,0:T(8,128)} %bitcast.43), custom_call_target="tpu_custom_call" | custom-call | tf_op jit(solution)/shard_map/plan/pallas_call | solution.py:370
  20.4 3.6 %collective-permute-start.5 = (bf16[384,256]{1,0:T(8,128)(2,1)S(1)}, bf16[384,256]{1,0:T(8,128)(2,1)S(1)}, u32[]{:S(2)}, u32[]{:S(2)}) collective-permute-start(bf16[384,256]{1,0:T(8,128)(2,1)S(1)} %collective-permute-done.4), channel_id=1, source_target_pairs={{0,224},{32,0},{64,32},{96,64},{128,96},{160,128},{192,160},{224,1... | collective-permute-start | bytes 589832 | tf_op jit(solution)/shard_map/ppermute | solution.py:439
  24.0 3.2 %collective-permute-start.11 = (bf16[192,512]{1,0:T(8,128)(2,1)S(1)}, bf16[192,512]{1,0:T(8,128)(2,1)S(1)}, u32[]{:S(2)}, u32[]{:S(2)}) collective-permute-start(bf16[192,512]{1,0:T(8,128)(2,1)S(1)} %slice.86), channel_id=1, source_target_pairs={{0,24},{8,0},{16,8},{24,16},{1,25},{9,1},{17,9},{25,17},{2,26},{10... | collective-permute-start | bytes 589832 | tf_op jit(solution)/shard_map/ppermute | solution.py:439
  27.4 3.6 %collective-permute-start.7 = (bf16[256,256]{1,0:T(8,128)(2,1)S(1)}, bf16[256,256]{1,0:T(8,128)(2,1)S(1)}, u32[]{:S(2)}, u32[]{:S(2)}) collective-permute-start(bf16[256,256]{1,0:T(8,128)(2,1)S(1)} %slice.84), channel_id=1, source_target_pairs={{0,224},{32,0},{64,32},{96,64},{128,96},{160,128},{192,160},{224,1... | collective-permute-start | bytes 393224 | tf_op jit(solution)/shard_map/ppermute | solution.py:439
  31.1 3.1 %collective-permute-done.10.top = bf16[192,512]{1,0:T(8,128)(2,1)S(1)} collective-permute-done((bf16[192,512]{1,0:T(8,128)(2,1)S(1)}, bf16[192,512]{1,0:T(8,128)(2,1)S(1)}, u32[]{:S(2)}, u32[]{:S(2)}) %collective-permute-start.10) | collective-permute-done | bytes 196640 | tf_op jit(solution)/shard_map/ppermute | solution.py:439
  35.1 2.2 %collective-permute-done.6 = bf16[256,256]{1,0:T(8,128)(2,1)S(1)} collective-permute-done((bf16[256,256]{1,0:T(8,128)(2,1)S(1)}, bf16[256,256]{1,0:T(8,128)(2,1)S(1)}, u32[]{:S(2)}, u32[]{:S(2)}) %collective-permute-start.6) | collective-permute-done | bytes 131104 | tf_op jit(solution)/shard_map/ppermute | solution.py:439
  37.3 5.8 %stats.1 = (f32[48,256]{1,0:T(8,128)S(1)}, bf16[24,128,256]{2,1,0:T(8,128)(2,1)S(1)}) custom-call(s32[896]{0:T(1024)S(1)} %copy-done.7, bf16[3,128,256]{2,1,0:T(8,128)(2,1)S(1)} %bitcast.34, bf16[3,128,256]{2,1,0:T(8,128)(2,1)S(1)} %bitcast.38, bf16[3,128,256]{2,1,0:T(8,128)(2,1)S(1)} %bitcast.40, bf16[3,128,256]{2,1,0:T(8,128)(2,1)S(1)} %bitcast.36, ...), custom_call_target="tpu_custom_call" | custom-call | tf_op jit(solution)/shard_map/stats/pallas_call | solution.py:392
  43.3 1.5 %collective-permute-start.13 = (f32[48,256]{1,0:T(8,128)S(1)}, f32[48,256]{1,0:T(8,128)S(1)}, u32[]{:S(2)}, u32[]{:S(2)}) collective-permute-start(f32[48,256]{1,0:T(8,128)S(1)} %get-tuple-element.24.st0), channel_id=1, source_target_pairs={{0,16},{8,24},{16,0},{24,8},{1,17},{9,25},{17,1},{25,9},{2,18},{10... | collective-permute-start | bytes 147464 | tf_op jit(solution)/shard_map/ppermute | solution.py:439
  45.2 2.0 %collective-permute-done.14.st3 = f32[48,256]{1,0:T(8,128)S(1)} collective-permute-done((f32[48,256]{1,0:T(8,128)S(1)}, f32[48,256]{1,0:T(8,128)S(1)}, u32[]{:S(2)}, u32[]{:S(2)}) %collective-permute-start.14) | collective-permute-done | bytes 49184 | tf_op jit(solution)/shard_map/ppermute | solution.py:439
  47.3 1.8 %collective-permute-done.13.st2 = f32[48,256]{1,0:T(8,128)S(1)} collective-permute-done((f32[48,256]{1,0:T(8,128)S(1)}, f32[48,256]{1,0:T(8,128)S(1)}, u32[]{:S(2)}, u32[]{:S(2)}) %collective-permute-start.13) | collective-permute-done | bytes 49184 | tf_op jit(solution)/shard_map/ppermute | solution.py:439
  50.2 11.5 %grads.1 = (bf16[512,384]{1,0:T(8,128)(2,1)S(1)}, bf16[512,384]{1,0:T(8,128)(2,1)S(1)}, bf16[512,384]{1,0:T(8,128)(2,1)S(1)}, bf16[512,384]{1,0:T(8,128)(2,1)S(1)}, bf16[24,128,256]{2,1,0:T(8,128)(2,1)}) custom-call(s32[896]{0:T(1024)S(1)} %copy-done.7, bf16[24,128,256]{2,1,0:T(8,128)(2,1)S(1)} %get-tuple-element.23.kv_any, ...), custom_call_target="tpu_custom_call" | custom-call | tf_op jit(solution)/shard_map/grads/pallas_call | solution.py:410
  62.4 6.3 %all-to-all-start = ((bf16[8,384,256]{2,1,0:T(8,128)(2,1)}), bf16[8,384,256]{2,1,0:T(8,128)(2,1)S(1)}, u32[]{:S(2)}, u32[]{:S(2)}) async-start(bf16[8,384,256]{2,1,0:T(8,128)(2,1)} %bitcast.10), calls=%async_computation | async-start | bytes 3145728 | tf_op jit(solution)/shard_map/all_to_all | solution.py:539
  69.3 2.7 %collective-permute-start.17 = (bf16[512,384]{1,0:T(8,128)(2,1)S(1)}, bf16[512,384]{1,0:T(8,128)(2,1)S(1)}, u32[]{:S(2)}, u32[]{:S(2)}) collective-permute-start(bf16[512,384]{1,0:T(8,128)(2,1)S(1)} %get-tuple-element.29), channel_id=1, source_target_pairs={{0,24},{8,0},{16,8},{24,16},{1,25},{9,1},{17,9},{25,17},{2,26},{10... | collective-permute-start | bytes 1179656 | tf_op jit(solution)/shard_map/ppermute | solution.py:439
  72.0 11.7 %collective-permute-done.15.row1 = bf16[512,384]{1,0:T(8,128)(2,1)S(1)} collective-permute-done((bf16[512,384]{1,0:T(8,128)(2,1)S(1)}, bf16[512,384]{1,0:T(8,128)(2,1)S(1)}, u32[]{:S(2)}, u32[]{:S(2)}) %collective-permute-start.15) | collective-permute-done | bytes 393248 | tf_op jit(solution)/shard_map/ppermute | solution.py:439
  85.2 4.7 %rows.1 = (bf16[4,256,512]{2,1,0:T(8,128)(2,1)}, f32[1024,384]{1,0:T(8,128)}, bf16[1024,384]{1,0:T(8,128)(2,1)}) custom-call(bf16[512,384]{1,0:T(8,128)(2,1)} %copy-done.4, bf16[512,384]{1,0:T(8,128)(2,1)} %copy-done.8, bf16[512,384]{1,0:T(8,128)(2,1)} %copy-done.9, bf16[512,384]{1,0:T(8,128)(2,1)} %copy-done.10, bf16[384,1024]{1,0:T(8,128)(2,1)} %input_any.1, ...), custom_call_target="tpu_custom_call" | custom-call | tf_op jit(solution)/shard_map/rows/pallas_call | solution.py:444
  89.9 2.0 %slice_bitcast_fusion.2 = (bf16[256,512]{1,0:T(8,128)(2,1)}, bf16[256,512]{1,0:T(8,128)(2,1)}, bf16[256,512]{1,0:T(8,128)(2,1)S(1)}) fusion(bf16[4,256,512]{2,1,0:T(8,128)(2,1)} %get-tuple-element.35), kind=kLoop, calls=%fused_computation.13 | loop fusion | bytes 1572864 | tf_op jit(solution)/shard_map/squeeze | solution.py:544
  92.1 3.0 %collective-permute-start.24 = (bf16[256,512]{1,0:T(8,128)(2,1)}, bf16[256,512]{1,0:T(8,128)(2,1)S(1)}, u32[]{:S(2)}, u32[]{:S(2)}) collective-permute-start(bf16[256,512]{1,0:T(8,128)(2,1)} %get-tuple-element.45), channel_id=1, source_target_pairs={{0,24},{8,0},{16,8},{24,16},{1,25},{9,1},{17,9},{25,17},{2,26},{10... | collective-permute-start | bytes 786440 | tf_op jit(solution)/shard_map/ppermute | solution.py:439
  95.7 7.9 %all-to-all-done.got_any = bf16[8,384,256]{2,1,0:T(8,128)(2,1)S(1)} async-done(((bf16[8,384,256]{2,1,0:T(8,128)(2,1)}), bf16[8,384,256]{2,1,0:T(8,128)(2,1)S(1)}, u32[]{:S(2)}, u32[]{:S(2)}) %all-to-all-start) | async-done | bytes 1572896 | tf_op jit(solution)/shard_map/all_to_all | solution.py:539
  104.5 3.2 %collective-permute-start.27 = (bf16[256,256]{1,0:T(8,128)(2,1)S(1)}, bf16[256,256]{1,0:T(8,128)(2,1)S(1)}, u32[]{:S(2)}, u32[]{:S(2)}) collective-permute-start(bf16[256,256]{1,0:T(8,128)(2,1)S(1)} %get-tuple-element.48), channel_id=1, source_target_pairs={{0,24},{8,0},{16,8},{24,16},{1,25},{9,1},{17,9},{25,17},{2,26},{10... | collective-permute-start | bytes 393224 | tf_op jit(solution)/shard_map/ppermute | solution.py:439
  110.7 4.4 %collective-permute-done.26 = bf16[256,256]{1,0:T(8,128)(2,1)S(1)} collective-permute-done((bf16[256,256]{1,0:T(8,128)(2,1)S(1)}, bf16[256,256]{1,0:T(8,128)(2,1)S(1)}, u32[]{:S(2)}, u32[]{:S(2)}) %collective-permute-start.26) | collective-permute-done | bytes 131104 | tf_op jit(solution)/shard_map/ppermute | solution.py:439
  115.9 3.5 %all-to-all-start.1 = ((bf16[8,32,768]{2,1,0:T(8,128)(2,1)}), bf16[8,32,768]{2,1,0:T(8,128)(2,1)S(1)}, u32[]{:S(2)}, u32[]{:S(2)}) async-start(bf16[8,32,768]{2,1,0:T(8,128)(2,1)} %bitcast.20), calls=%async_computation.1 | async-start | bytes 786432 | tf_op jit(solution)/shard_map/all_to_all | solution.py:551
  120.1 1.6 %collective-permute-start.21 = (bf16[128,384]{1,0:T(8,128)(2,1)S(1)}, bf16[128,384]{1,0:T(8,128)(2,1)S(1)}, u32[]{:S(2)}, u32[]{:S(2)}) collective-permute-start(bf16[128,384]{1,0:T(8,128)(2,1)S(1)} %get-tuple-element.51), channel_id=1, source_target_pairs={{0,6},{2,0},{4,2},{6,4},{1,7},{3,1},{5,3},{7,5},{8,14},{10,8},{12,... | collective-permute-start | bytes 294920 | tf_op jit(solution)/shard_map/ppermute | solution.py:439
  121.6 1.4 %collective-permute-start.20 = (bf16[128,384]{1,0:T(8,128)(2,1)S(1)}, bf16[128,384]{1,0:T(8,128)(2,1)S(1)}, u32[]{:S(2)}, u32[]{:S(2)}) collective-permute-start(bf16[128,384]{1,0:T(8,128)(2,1)S(1)} %get-tuple-element.52), channel_id=1, source_target_pairs={{0,4},{2,6},{4,0},{6,2},{1,5},{3,7},{5,1},{7,3},{8,12},{10,14},{12... | collective-permute-start | bytes 294920 | tf_op jit(solution)/shard_map/ppermute | solution.py:439
  123.0 1.2 collective-permute-done.19
  124.2 1.7 %collective-permute-done.21 = bf16[128,384]{1,0:T(8,128)(2,1)S(1)} collective-permute-done((bf16[128,384]{1,0:T(8,128)(2,1)S(1)}, bf16[128,384]{1,0:T(8,128)(2,1)S(1)}, u32[]{:S(2)}, u32[]{:S(2)}) %collective-permute-start.21) | collective-permute-done | bytes 98336 | tf_op jit(solution)/shard_map/ppermute | solution.py:439
  125.9 1.9 %collective-permute-done.20 = bf16[128,384]{1,0:T(8,128)(2,1)S(1)} collective-permute-done((bf16[128,384]{1,0:T(8,128)(2,1)S(1)}, bf16[128,384]{1,0:T(8,128)(2,1)S(1)}, u32[]{:S(2)}, u32[]{:S(2)}) %collective-permute-start.20) | collective-permute-done | bytes 98336 | tf_op jit(solution)/shard_map/ppermute | solution.py:439
  128.6 2.6 %all-to-all-done.1 = bf16[8,32,768]{2,1,0:T(8,128)(2,1)S(1)} async-done(((bf16[8,32,768]{2,1,0:T(8,128)(2,1)}), bf16[8,32,768]{2,1,0:T(8,128)(2,1)S(1)}, u32[]{:S(2)}, u32[]{:S(2)}) %all-to-all-start.1) | async-done | bytes 393248 | tf_op jit(solution)/shard_map/all_to_all | solution.py:551
  (75 shorter events, 13.7 us)
Async XLA Ops:
  2.3 11.5 %collective-permute-start.3 = (bf16[384,256]{1,0:T(8,128)(2,1)}, bf16[384,256]{1,0:T(8,128)(2,1)S(1)}, u32[]{:S(2)}, u32[]{:S(2)}) collective-permute-start(bf16[384,256]{1,0:T(8,128)(2,1)} %join.1), channel_id=1, source_target_pairs={{0,224},{32,0},{64,32},{96,64},{128,96},{160,128},{192,160},{224,1... | collective-permute-start | bytes 589832 | tf_op jit(solution)/shard_map/ppermute | solution.py:439
  8.2 8.8 %collective-permute-start = (bf16[384,256]{1,0:T(8,128)(2,1)}, bf16[384,256]{1,0:T(8,128)(2,1)S(1)}, u32[]{:S(2)}, u32[]{:S(2)}) collective-permute-start(bf16[384,256]{1,0:T(8,128)(2,1)} %join.1), channel_id=1, source_target_pairs={{0,32},{32,64},{64,96},{96,128},{128,160},{160,192},{192,224},{224... | collective-permute-start | bytes 589832 | tf_op jit(solution)/shard_map/ppermute | solution.py:439
  10.7 23.6 %copy-start.1 = (bf16[384,512]{1,0:T(8,128)(2,1)S(1)}, bf16[384,512]{1,0:T(8,128)(2,1)}, u32[]{:S(2)}) copy-start(bf16[384,512]{1,0:T(8,128)(2,1)} %start.1.own) | copy-start | bytes 1179652
  10.7 13.4 %collective-permute-start.9 = (bf16[384,512]{1,0:T(8,128)(2,1)}, bf16[384,512]{1,0:T(8,128)(2,1)S(1)}, u32[]{:S(2)}, u32[]{:S(2)}) collective-permute-start(bf16[384,512]{1,0:T(8,128)(2,1)} %start.1.own), channel_id=1, source_target_pairs={{0,24},{8,0},{16,8},{24,16},{1,25},{9,1},{17,9},{25,17},{2,26},{10... | collective-permute-start | bytes 1179656 | tf_op jit(solution)/shard_map/ppermute | solution.py:439
  13.8 13.5 %collective-permute-start.8 = (bf16[384,512]{1,0:T(8,128)(2,1)}, bf16[384,512]{1,0:T(8,128)(2,1)S(1)}, u32[]{:S(2)}, u32[]{:S(2)}) collective-permute-start(bf16[384,512]{1,0:T(8,128)(2,1)} %start.1.own), channel_id=1, source_target_pairs={{0,8},{8,16},{16,24},{24,0},{1,9},{9,17},{17,25},{25,1},{2,10},{10... | collective-permute-start | bytes 1179656 | tf_op jit(solution)/shard_map/ppermute | solution.py:439
  13.8 6.6 %collective-permute-start.4 = (bf16[384,256]{1,0:T(8,128)(2,1)S(1)}, bf16[384,256]{1,0:T(8,128)(2,1)S(1)}, u32[]{:S(2)}, u32[]{:S(2)}) collective-permute-start(bf16[384,256]{1,0:T(8,128)(2,1)S(1)} %collective-permute-done.3), channel_id=1, source_target_pairs={{0,224},{32,0},{64,32},{96,64},{128,96},{160,128},{192,160},{224,1... | collective-permute-start | bytes 589832 | tf_op jit(solution)/shard_map/ppermute | solution.py:439
  17.0 7.0 %collective-permute-start.1 = (bf16[384,256]{1,0:T(8,128)(2,1)S(1)}, bf16[384,256]{1,0:T(8,128)(2,1)S(1)}, u32[]{:S(2)}, u32[]{:S(2)}) collective-permute-start(bf16[384,256]{1,0:T(8,128)(2,1)S(1)} %collective-permute-done), channel_id=1, source_target_pairs={{0,32},{32,64},{64,96},{96,128},{128,160},{160,192},{192,224},{224... | collective-permute-start | bytes 589832 | tf_op jit(solution)/shard_map/ppermute | solution.py:439
  20.4 6.9 %collective-permute-start.5 = (bf16[384,256]{1,0:T(8,128)(2,1)S(1)}, bf16[384,256]{1,0:T(8,128)(2,1)S(1)}, u32[]{:S(2)}, u32[]{:S(2)}) collective-permute-start(bf16[384,256]{1,0:T(8,128)(2,1)S(1)} %collective-permute-done.4), channel_id=1, source_target_pairs={{0,224},{32,0},{64,32},{96,64},{128,96},{160,128},{192,160},{224,1... | collective-permute-start | bytes 589832 | tf_op jit(solution)/shard_map/ppermute | solution.py:439
  24.0 7.0 %collective-permute-start.2 = (bf16[384,256]{1,0:T(8,128)(2,1)S(1)}, bf16[384,256]{1,0:T(8,128)(2,1)S(1)}, u32[]{:S(2)}, u32[]{:S(2)}) collective-permute-start(bf16[384,256]{1,0:T(8,128)(2,1)S(1)} %collective-permute-done.1), channel_id=1, source_target_pairs={{0,32},{32,64},{64,96},{96,128},{128,160},{160,192},{192,224},{224... | collective-permute-start | bytes 589832 | tf_op jit(solution)/shard_map/ppermute | solution.py:439
  24.0 7.1 %collective-permute-start.11 = (bf16[192,512]{1,0:T(8,128)(2,1)S(1)}, bf16[192,512]{1,0:T(8,128)(2,1)S(1)}, u32[]{:S(2)}, u32[]{:S(2)}) collective-permute-start(bf16[192,512]{1,0:T(8,128)(2,1)S(1)} %slice.86), channel_id=1, source_target_pairs={{0,24},{8,0},{16,8},{24,16},{1,25},{9,1},{17,9},{25,17},{2,26},{10... | collective-permute-start | bytes 589832 | tf_op jit(solution)/shard_map/ppermute | solution.py:439
  27.3 7.0 %collective-permute-start.10 = (bf16[192,512]{1,0:T(8,128)(2,1)S(1)}, bf16[192,512]{1,0:T(8,128)(2,1)S(1)}, u32[]{:S(2)}, u32[]{:S(2)}) collective-permute-start(bf16[192,512]{1,0:T(8,128)(2,1)S(1)} %slice.85), channel_id=1, source_target_pairs={{0,8},{8,16},{16,24},{24,0},{1,9},{9,17},{17,25},{25,1},{2,10},{10... | collective-permute-start | bytes 589832 | tf_op jit(solution)/shard_map/ppermute | solution.py:439
  27.4 7.7 %collective-permute-start.7 = (bf16[256,256]{1,0:T(8,128)(2,1)S(1)}, bf16[256,256]{1,0:T(8,128)(2,1)S(1)}, u32[]{:S(2)}, u32[]{:S(2)}) collective-permute-start(bf16[256,256]{1,0:T(8,128)(2,1)S(1)} %slice.84), channel_id=1, source_target_pairs={{0,224},{32,0},{64,32},{96,64},{128,96},{160,128},{192,160},{224,1... | collective-permute-start | bytes 393224 | tf_op jit(solution)/shard_map/ppermute | solution.py:439
  31.0 6.3 %collective-permute-start.6 = (bf16[256,256]{1,0:T(8,128)(2,1)S(1)}, bf16[256,256]{1,0:T(8,128)(2,1)S(1)}, u32[]{:S(2)}, u32[]{:S(2)}) collective-permute-start(bf16[256,256]{1,0:T(8,128)(2,1)S(1)} %slice.83), channel_id=1, source_target_pairs={{0,32},{32,64},{64,96},{96,128},{128,160},{160,192},{192,224},{224... | collective-permute-start | bytes 393224 | tf_op jit(solution)/shard_map/ppermute | solution.py:439
  43.1 4.2 %collective-permute-start.14 = (f32[48,256]{1,0:T(8,128)S(1)}, f32[48,256]{1,0:T(8,128)S(1)}, u32[]{:S(2)}, u32[]{:S(2)}) collective-permute-start(f32[48,256]{1,0:T(8,128)S(1)} %get-tuple-element.24.st0), channel_id=1, source_target_pairs={{0,24},{8,0},{16,8},{24,16},{1,25},{9,1},{17,9},{25,17},{2,26},{10... | collective-permute-start | bytes 147464 | tf_op jit(solution)/shard_map/ppermute | solution.py:439
  43.3 5.7 %collective-permute-start.13 = (f32[48,256]{1,0:T(8,128)S(1)}, f32[48,256]{1,0:T(8,128)S(1)}, u32[]{:S(2)}, u32[]{:S(2)}) collective-permute-start(f32[48,256]{1,0:T(8,128)S(1)} %get-tuple-element.24.st0), channel_id=1, source_target_pairs={{0,16},{8,24},{16,0},{24,8},{1,17},{9,25},{17,1},{25,9},{2,18},{10... | collective-permute-start | bytes 147464 | tf_op jit(solution)/shard_map/ppermute | solution.py:439
  44.9 5.3 %collective-permute-start.12 = (f32[48,256]{1,0:T(8,128)S(1)}, f32[48,256]{1,0:T(8,128)S(1)}, u32[]{:S(2)}, u32[]{:S(2)}) collective-permute-start(f32[48,256]{1,0:T(8,128)S(1)} %get-tuple-element.24.st0), channel_id=1, source_target_pairs={{0,8},{8,16},{16,24},{24,0},{1,9},{9,17},{17,25},{25,1},{2,10},{10... | collective-permute-start | bytes 147464 | tf_op jit(solution)/shard_map/ppermute | solution.py:439
  62.4 41.1 %all-to-all-start = ((bf16[8,384,256]{2,1,0:T(8,128)(2,1)}), bf16[8,384,256]{2,1,0:T(8,128)(2,1)S(1)}, u32[]{:S(2)}, u32[]{:S(2)}) async-start(bf16[8,384,256]{2,1,0:T(8,128)(2,1)} %bitcast.10), calls=%async_computation | async-start | bytes 3145728 | tf_op jit(solution)/shard_map/all_to_all | solution.py:539
  68.8 14.9 %collective-permute-start.15 = (bf16[512,384]{1,0:T(8,128)(2,1)S(1)}, bf16[512,384]{1,0:T(8,128)(2,1)S(1)}, u32[]{:S(2)}, u32[]{:S(2)}) collective-permute-start(bf16[512,384]{1,0:T(8,128)(2,1)S(1)} %get-tuple-element.27), channel_id=1, source_target_pairs={{0,8},{8,16},{16,24},{24,0},{1,9},{9,17},{17,25},{25,1},{2,10},{10... | collective-permute-start | bytes 1179656 | tf_op jit(solution)/shard_map/ppermute | solution.py:439
  68.8 14.9 %collective-permute-start.16 = (bf16[512,384]{1,0:T(8,128)(2,1)S(1)}, bf16[512,384]{1,0:T(8,128)(2,1)S(1)}, u32[]{:S(2)}, u32[]{:S(2)}) collective-permute-start(bf16[512,384]{1,0:T(8,128)(2,1)S(1)} %get-tuple-element.28), channel_id=1, source_target_pairs={{0,16},{8,24},{16,0},{24,8},{1,17},{9,25},{17,1},{25,9},{2,18},{10... | collective-permute-start | bytes 1179656 | tf_op jit(solution)/shard_map/ppermute | solution.py:439
  69.3 15.1 %collective-permute-start.17 = (bf16[512,384]{1,0:T(8,128)(2,1)S(1)}, bf16[512,384]{1,0:T(8,128)(2,1)S(1)}, u32[]{:S(2)}, u32[]{:S(2)}) collective-permute-start(bf16[512,384]{1,0:T(8,128)(2,1)S(1)} %get-tuple-element.29), channel_id=1, source_target_pairs={{0,24},{8,0},{16,8},{24,16},{1,25},{9,1},{17,9},{25,17},{2,26},{10... | collective-permute-start | bytes 1179656 | tf_op jit(solution)/shard_map/ppermute | solution.py:439
  89.9 13.7 %copy-start.3 = (bf16[1024,384]{1,0:T(8,128)(2,1)S(1)}, bf16[1024,384]{1,0:T(8,128)(2,1)}, u32[]{:S(2)}) copy-start(bf16[1024,384]{1,0:T(8,128)(2,1)} %get-tuple-element.30.turned_any) | copy-start | bytes 2359300
  91.9 16.6 %collective-permute-start.22 = (bf16[256,512]{1,0:T(8,128)(2,1)}, bf16[256,512]{1,0:T(8,128)(2,1)S(1)}, u32[]{:S(2)}, u32[]{:S(2)}) collective-permute-start(bf16[256,512]{1,0:T(8,128)(2,1)} %get-tuple-element.44), channel_id=1, source_target_pairs={{0,8},{8,16},{16,24},{24,0},{1,9},{9,17},{17,25},{25,1},{2,10},{10... | collective-permute-start | bytes 786440 | tf_op jit(solution)/shard_map/ppermute | solution.py:439
  92.1 16.5 %collective-permute-start.24 = (bf16[256,512]{1,0:T(8,128)(2,1)}, bf16[256,512]{1,0:T(8,128)(2,1)S(1)}, u32[]{:S(2)}, u32[]{:S(2)}) collective-permute-start(bf16[256,512]{1,0:T(8,128)(2,1)} %get-tuple-element.45), channel_id=1, source_target_pairs={{0,24},{8,0},{16,8},{24,16},{1,25},{9,1},{17,9},{25,17},{2,26},{10... | collective-permute-start | bytes 786440 | tf_op jit(solution)/shard_map/ppermute | solution.py:439
  95.2 13.8 %collective-permute-start.23 = (bf16[256,512]{1,0:T(8,128)(2,1)S(1)}, bf16[256,512]{1,0:T(8,128)(2,1)S(1)}, u32[]{:S(2)}, u32[]{:S(2)}) collective-permute-start(bf16[256,512]{1,0:T(8,128)(2,1)S(1)} %get-tuple-element.46), channel_id=1, source_target_pairs={{0,16},{8,24},{16,0},{24,8},{1,17},{9,25},{17,1},{25,9},{2,18},{10... | collective-permute-start | bytes 786440 | tf_op jit(solution)/shard_map/ppermute | solution.py:439
  104.4 6.3 %collective-permute-start.25 = (bf16[256,256]{1,0:T(8,128)(2,1)S(1)}, bf16[256,256]{1,0:T(8,128)(2,1)S(1)}, u32[]{:S(2)}, u32[]{:S(2)}) collective-permute-start(bf16[256,256]{1,0:T(8,128)(2,1)S(1)} %get-tuple-element.47), channel_id=1, source_target_pairs={{0,8},{8,16},{16,24},{24,0},{1,9},{9,17},{17,25},{25,1},{2,10},{10... | collective-permute-start | bytes 393224 | tf_op jit(solution)/shard_map/ppermute | solution.py:439
  104.5 6.2 %collective-permute-start.27 = (bf16[256,256]{1,0:T(8,128)(2,1)S(1)}, bf16[256,256]{1,0:T(8,128)(2,1)S(1)}, u32[]{:S(2)}, u32[]{:S(2)}) collective-permute-start(bf16[256,256]{1,0:T(8,128)(2,1)S(1)} %get-tuple-element.48), channel_id=1, source_target_pairs={{0,24},{8,0},{16,8},{24,16},{1,25},{9,1},{17,9},{25,17},{2,26},{10... | collective-permute-start | bytes 393224 | tf_op jit(solution)/shard_map/ppermute | solution.py:439
  108.5 6.6 %collective-permute-start.26 = (bf16[256,256]{1,0:T(8,128)(2,1)S(1)}, bf16[256,256]{1,0:T(8,128)(2,1)S(1)}, u32[]{:S(2)}, u32[]{:S(2)}) collective-permute-start(bf16[256,256]{1,0:T(8,128)(2,1)S(1)} %get-tuple-element.49), channel_id=1, source_target_pairs={{0,16},{8,24},{16,0},{24,8},{1,17},{9,25},{17,1},{25,9},{2,18},{10... | collective-permute-start | bytes 393224 | tf_op jit(solution)/shard_map/ppermute | solution.py:439
  108.6 10.8 %collective-permute-start.18 = (bf16[512,384]{1,0:T(8,128)(2,1)S(1)}, bf16[512,384]{1,0:T(8,128)(2,1)S(1)}, u32[]{:S(2)}, u32[]{:S(2)}) collective-permute-start(bf16[512,384]{1,0:T(8,128)(2,1)S(1)} %get-tuple-element.34), channel_id=1, source_target_pairs={{0,1},{1,0},{2,3},{3,2},{4,5},{5,4},{6,7},{7,6},{8,9},{9,8},{10,11... | collective-permute-start | bytes 1179656 | tf_op jit(solution)/shard_map/ppermute | solution.py:439
  115.9 15.3 %all-to-all-start.1 = ((bf16[8,32,768]{2,1,0:T(8,128)(2,1)}), bf16[8,32,768]{2,1,0:T(8,128)(2,1)S(1)}, u32[]{:S(2)}, u32[]{:S(2)}) async-start(bf16[8,32,768]{2,1,0:T(8,128)(2,1)} %bitcast.20), calls=%async_computation.1 | async-start | bytes 786432 | tf_op jit(solution)/shard_map/all_to_all | solution.py:551
  119.5 4.7 %collective-permute-start.19 = (bf16[128,384]{1,0:T(8,128)(2,1)S(1)}, bf16[128,384]{1,0:T(8,128)(2,1)S(1)}, u32[]{:S(2)}, u32[]{:S(2)}) collective-permute-start(bf16[128,384]{1,0:T(8,128)(2,1)S(1)} %get-tuple-element.50), channel_id=1, source_target_pairs={{0,2},{2,4},{4,6},{6,0},{1,3},{3,5},{5,7},{7,1},{8,10},{10,12},{12... | collective-permute-start | bytes 294920 | tf_op jit(solution)/shard_map/ppermute | solution.py:439
  120.1 5.8 %collective-permute-start.21 = (bf16[128,384]{1,0:T(8,128)(2,1)S(1)}, bf16[128,384]{1,0:T(8,128)(2,1)S(1)}, u32[]{:S(2)}, u32[]{:S(2)}) collective-permute-start(bf16[128,384]{1,0:T(8,128)(2,1)S(1)} %get-tuple-element.51), channel_id=1, source_target_pairs={{0,6},{2,0},{4,2},{6,4},{1,7},{3,1},{5,3},{7,5},{8,14},{10,8},{12,... | collective-permute-start | bytes 294920 | tf_op jit(solution)/shard_map/ppermute | solution.py:439
  121.6 6.1 %collective-permute-start.20 = (bf16[128,384]{1,0:T(8,128)(2,1)S(1)}, bf16[128,384]{1,0:T(8,128)(2,1)S(1)}, u32[]{:S(2)}, u32[]{:S(2)}) collective-permute-start(bf16[128,384]{1,0:T(8,128)(2,1)S(1)} %get-tuple-element.52), channel_id=1, source_target_pairs={{0,4},{2,6},{4,0},{6,2},{1,5},{3,7},{5,1},{7,3},{8,12},{10,14},{12... | collective-permute-start | bytes 294920 | tf_op jit(solution)/shard_map/ppermute | solution.py:439
  (9 other events, 28.3 us)

commit v6 on v5

--- a/solution.py
+++ b/solution.py
@@ -507,6 +507,26 @@
     )(d, key_weight, value_weight, back)
 
 
+def finish_kernel(got_ref, q_ref, o_ref, k_ref, v_ref):
+    total = sum(got_ref[t].astype(f32) for t in range(NZ))
+    q_ref[...] = total[:, :PAIR]
+    o_ref[...] = total[:, PAIR : 2 * PAIR]
+    k_ref[...] = total[:, 2 * PAIR : 2 * PAIR + HEAD_WIDTH]
+    v_ref[...] = total[:, 2 * PAIR + HEAD_WIDTH :]
+
+
+def finish_call(got):
+    rows = got.shape[1]
+    return pl.pallas_call(
+        finish_kernel,
+        out_shape=tuple(jax.ShapeDtypeStruct((rows, n), f32) for n in (PAIR, PAIR, HEAD_WIDTH, HEAD_WIDTH)),
+        in_specs=[VMEM_SPEC],
+        out_specs=(VMEM_SPEC,) * 4,
+        compiler_params=vmem(4),
+        name="finish",
+    )(got)
+
+
 def ring_gather(own, plan):
     up, down = [own], [own]
     for step in range(3):
@@ -548,7 +568,7 @@
     kv_got = [kv_part[0]] + [shift(kv_part[s], "y", NY, s) for s in range(1, NY)]
     sums = [sum(g.astype(f32) for g in got).astype(bf16) for got in (qo_got, kv_got)]
     sums = jnp.concatenate(sums, axis=1).reshape(NZ, part_rows, 2 * PAIR + 2 * HEAD_WIDTH)
-    sums = jnp.sum(lax.all_to_all(sums, "z", 0, 0, tiled=True).astype(f32), axis=0)
+    q_grad, o_grad, k_grad, v_grad = finish_call(lax.all_to_all(sums, "z", 0, 0, tiled=True))
 
     width = model // (nx * nc)
     side = nx * width
@@ -560,10 +580,10 @@
         input_grad = input_grad + shift(piece, "x", nx, s).astype(f32)
     return (
         input_grad.astype(bf16).T,
-        sums[:, :PAIR],
-        sums[:, 2 * PAIR : 2 * PAIR + HEAD_WIDTH],
-        sums[:, 2 * PAIR + HEAD_WIDTH :],
-        sums[:, PAIR : 2 * PAIR].T,
+        q_grad,
+        k_grad,
+        v_grad,
+        o_grad.T,
     )
 
 

time: 135 us -> 133 us (0.985)
  no operation moved by 1% of the time
where the time goes in v6:
time: 133 us; the launch traced here: 132 us
  starting transfers between devices  49.5 us (37%)
  waiting for transfers between devices  42.2 us (32%)
  Pallas kernels  32.6 us (25%)
  local copies, waits for them, and re-layouts  4.44 us (3%)
  other arithmetic  2.09 us (2%)
    ppermute x28, starting transfers between devices, shift(): return lax.ppermute(x, axis, [(i, (i + by) % size) for i in range(size)])  39.7 us
    ppermute x28, waiting for transfers between devices, shift(): return lax.ppermute(x, axis, [(i, (i + by) % size) for i in range(size)])  32 us
    pallas_call x1, Pallas kernels, grads_call(): pl.pallas_call(grads_kernel, out_shape=(*[jax.ShapeDtypeStruct((2 * PAIR,...  11.5 us
    all_to_all x1, waiting for transfers between devices, per_device(): lax.all_to_all(col_part.reshape(NZ, DEV_BLOCKS * BLOCK, 2 * HEAD_WIDTH),...  7.58 us
    all_to_all x1, starting transfers between devices, per_device(): lax.all_to_all(col_part.reshape(NZ, DEV_BLOCKS * BLOCK, 2 * HEAD_WIDTH),...  6.32 us
    pallas_call x1, Pallas kernels, stats_call(): pl.pallas_call(stats_kernel, out_shape=(jax.ShapeDtypeStruct((3 * STAT_RO...  5.8 us
    pallas_call x1, Pallas kernels, rows_call(): pl.pallas_call(functools.partial(rows_kernel, nx, nc), out_shape=(jax.Sha...  4.73 us
    all_to_all x1, starting transfers between devices, per_device(): lax.all_to_all(sums, 'z', 0, 0, tiled=True)  3.45 us
  transfers between devices with their start and end apart: 30, of which 14 were waited for; matrix products, arithmetic and copies ran while one was open for 4% of the time, Pallas kernels for 10%

profile of v6, /device:TPU:6, one launch (start us, length us, event | category | flops | bytes accessed | tf_op | source)
XLA Modules:
  0.0 131.8 jit_solution(13726808029804840215)
XLA Ops:
  0.6 1.6 %join.1 = bf16[384,256]{1,0:T(8,128)(2,1)} custom-call(bf16[384,128]{1,0:T(8,128)(2,1)} %key_any.1, bf16[384,128]{1,0:T(8,128)(2,1)} %value_any.1), custom_call_target="tpu_custom_call" | custom-call | tf_op jit(solution)/shard_map/join/pallas_call | solution.py:342
  2.3 5.9 %collective-permute-start.3 = (bf16[384,256]{1,0:T(8,128)(2,1)}, bf16[384,256]{1,0:T(8,128)(2,1)S(1)}, u32[]{:S(2)}, u32[]{:S(2)}) collective-permute-start(bf16[384,256]{1,0:T(8,128)(2,1)} %join.1), channel_id=1, source_target_pairs={{0,224},{32,0},{64,32},{96,64},{128,96},{160,128},{192,160},{224,1... | collective-permute-start | bytes 589832 | tf_op jit(solution)/shard_map/ppermute | solution.py:439
  8.2 2.5 %start.1.own = bf16[384,512]{1,0:T(8,128)(2,1)} custom-call(bf16[384,256]{1,0:T(8,128)(2,1)} %query_any.1, bf16[384,1024]{1,0:T(8,128)(2,1)} %grad_any.3, bf16[256,1024]{1,0:T(8,128)(2,1)} %weight_any.1), custom_call_target="tpu_custom_call" | custom-call | tf_op jit(solution)/shard_map/start/pallas_call | solution.py:354
  10.7 3.1 %collective-permute-start.9 = (bf16[384,512]{1,0:T(8,128)(2,1)}, bf16[384,512]{1,0:T(8,128)(2,1)S(1)}, u32[]{:S(2)}, u32[]{:S(2)}) collective-permute-start(bf16[384,512]{1,0:T(8,128)(2,1)} %start.1.own), channel_id=1, source_target_pairs={{0,24},{8,0},{16,8},{24,16},{1,25},{9,1},{17,9},{25,17},{2,26},{10... | collective-permute-start | bytes 1179656 | tf_op jit(solution)/shard_map/ppermute | solution.py:439
  13.8 3.2 %collective-permute-start.4 = (bf16[384,256]{1,0:T(8,128)(2,1)S(1)}, bf16[384,256]{1,0:T(8,128)(2,1)S(1)}, u32[]{:S(2)}, u32[]{:S(2)}) collective-permute-start(bf16[384,256]{1,0:T(8,128)(2,1)S(1)} %collective-permute-done.3), channel_id=1, source_target_pairs={{0,224},{32,0},{64,32},{96,64},{128,96},{160,128},{192,160},{224,1... | collective-permute-start | bytes 589832 | tf_op jit(solution)/shard_map/ppermute | solution.py:439
  17.0 3.4 %plan.1.plan_any = s32[896]{0:T(1024)} custom-call(s32[16,96]{1,0:T(8,128)} %bitcast.42), custom_call_target="tpu_custom_call" | custom-call | tf_op jit(solution)/shard_map/plan/pallas_call | solution.py:370
  20.4 3.6 %collective-permute-start.5 = (bf16[384,256]{1,0:T(8,128)(2,1)S(1)}, bf16[384,256]{1,0:T(8,128)(2,1)S(1)}, u32[]{:S(2)}, u32[]{:S(2)}) collective-permute-start(bf16[384,256]{1,0:T(8,128)(2,1)S(1)} %collective-permute-done.4), channel_id=1, source_target_pairs={{0,224},{32,0},{64,32},{96,64},{128,96},{160,128},{192,160},{224,1... | collective-permute-start | bytes 589832 | tf_op jit(solution)/shard_map/ppermute | solution.py:439
  24.1 3.2 %collective-permute-start.11 = (bf16[192,512]{1,0:T(8,128)(2,1)S(1)}, bf16[192,512]{1,0:T(8,128)(2,1)S(1)}, u32[]{:S(2)}, u32[]{:S(2)}) collective-permute-start(bf16[192,512]{1,0:T(8,128)(2,1)S(1)} %slice.70), channel_id=1, source_target_pairs={{0,24},{8,0},{16,8},{24,16},{1,25},{9,1},{17,9},{25,17},{2,26},{10... | collective-permute-start | bytes 589832 | tf_op jit(solution)/shard_map/ppermute | solution.py:439
  27.4 3.6 %collective-permute-start.7 = (bf16[256,256]{1,0:T(8,128)(2,1)S(1)}, bf16[256,256]{1,0:T(8,128)(2,1)S(1)}, u32[]{:S(2)}, u32[]{:S(2)}) collective-permute-start(bf16[256,256]{1,0:T(8,128)(2,1)S(1)} %slice.68), channel_id=1, source_target_pairs={{0,224},{32,0},{64,32},{96,64},{128,96},{160,128},{192,160},{224,1... | collective-permute-start | bytes 393224 | tf_op jit(solution)/shard_map/ppermute | solution.py:439
  31.2 3.1 %collective-permute-done.10.top = bf16[192,512]{1,0:T(8,128)(2,1)S(1)} collective-permute-done((bf16[192,512]{1,0:T(8,128)(2,1)S(1)}, bf16[192,512]{1,0:T(8,128)(2,1)S(1)}, u32[]{:S(2)}, u32[]{:S(2)}) %collective-permute-start.10) | collective-permute-done | bytes 196640 | tf_op jit(solution)/shard_map/ppermute | solution.py:439
  35.1 2.2 %collective-permute-done.6 = bf16[256,256]{1,0:T(8,128)(2,1)S(1)} collective-permute-done((bf16[256,256]{1,0:T(8,128)(2,1)S(1)}, bf16[256,256]{1,0:T(8,128)(2,1)S(1)}, u32[]{:S(2)}, u32[]{:S(2)}) %collective-permute-start.6) | collective-permute-done | bytes 131104 | tf_op jit(solution)/shard_map/ppermute | solution.py:439
  37.3 5.8 %stats.1 = (f32[48,256]{1,0:T(8,128)S(1)}, bf16[24,128,256]{2,1,0:T(8,128)(2,1)S(1)}) custom-call(s32[896]{0:T(1024)S(1)} %copy-done.7, bf16[3,128,256]{2,1,0:T(8,128)(2,1)S(1)} %bitcast.33, bf16[3,128,256]{2,1,0:T(8,128)(2,1)S(1)} %bitcast.37, bf16[3,128,256]{2,1,0:T(8,128)(2,1)S(1)} %bitcast.39, bf16[3,128,256]{2,1,0:T(8,128)(2,1)S(1)} %bitcast.35, ...), custom_call_target="tpu_custom_call" | custom-call | tf_op jit(solution)/shard_map/stats/pallas_call | solution.py:392
  43.4 1.5 %collective-permute-start.13 = (f32[48,256]{1,0:T(8,128)S(1)}, f32[48,256]{1,0:T(8,128)S(1)}, u32[]{:S(2)}, u32[]{:S(2)}) collective-permute-start(f32[48,256]{1,0:T(8,128)S(1)} %get-tuple-element.28.st0), channel_id=1, source_target_pairs={{0,16},{8,24},{16,0},{24,8},{1,17},{9,25},{17,1},{25,9},{2,18},{10... | collective-permute-start | bytes 147464 | tf_op jit(solution)/shard_map/ppermute | solution.py:439
  45.3 2.0 %collective-permute-done.14.st3 = f32[48,256]{1,0:T(8,128)S(1)} collective-permute-done((f32[48,256]{1,0:T(8,128)S(1)}, f32[48,256]{1,0:T(8,128)S(1)}, u32[]{:S(2)}, u32[]{:S(2)}) %collective-permute-start.14) | collective-permute-done | bytes 49184 | tf_op jit(solution)/shard_map/ppermute | solution.py:439
  47.3 1.8 %collective-permute-done.13.st2 = f32[48,256]{1,0:T(8,128)S(1)} collective-permute-done((f32[48,256]{1,0:T(8,128)S(1)}, f32[48,256]{1,0:T(8,128)S(1)}, u32[]{:S(2)}, u32[]{:S(2)}) %collective-permute-start.13) | collective-permute-done | bytes 49184 | tf_op jit(solution)/shard_map/ppermute | solution.py:439
  50.2 11.5 %grads.1 = (bf16[512,384]{1,0:T(8,128)(2,1)S(1)}, bf16[512,384]{1,0:T(8,128)(2,1)S(1)}, bf16[512,384]{1,0:T(8,128)(2,1)S(1)}, bf16[512,384]{1,0:T(8,128)(2,1)S(1)}, bf16[24,128,256]{2,1,0:T(8,128)(2,1)}) custom-call(s32[896]{0:T(1024)S(1)} %copy-done.7, bf16[24,128,256]{2,1,0:T(8,128)(2,1)S(1)} %get-tuple-element.27.kv_any, ...), custom_call_target="tpu_custom_call" | custom-call | tf_op jit(solution)/shard_map/grads/pallas_call | solution.py:410
  62.5 6.3 %all-to-all-start = ((bf16[8,384,256]{2,1,0:T(8,128)(2,1)}), bf16[8,384,256]{2,1,0:T(8,128)(2,1)S(1)}, u32[]{:S(2)}, u32[]{:S(2)}) async-start(bf16[8,384,256]{2,1,0:T(8,128)(2,1)} %bitcast.10), calls=%async_computation | async-start | bytes 3145728 | tf_op jit(solution)/shard_map/all_to_all | solution.py:559
  69.5 2.8 %collective-permute-start.17 = (bf16[512,384]{1,0:T(8,128)(2,1)S(1)}, bf16[512,384]{1,0:T(8,128)(2,1)S(1)}, u32[]{:S(2)}, u32[]{:S(2)}) collective-permute-start(bf16[512,384]{1,0:T(8,128)(2,1)S(1)} %get-tuple-element.33), channel_id=1, source_target_pairs={{0,24},{8,0},{16,8},{24,16},{1,25},{9,1},{17,9},{25,17},{2,26},{10... | collective-permute-start | bytes 1179656 | tf_op jit(solution)/shard_map/ppermute | solution.py:439
  72.3 11.4 %collective-permute-done.15.row1 = bf16[512,384]{1,0:T(8,128)(2,1)S(1)} collective-permute-done((bf16[512,384]{1,0:T(8,128)(2,1)S(1)}, bf16[512,384]{1,0:T(8,128)(2,1)S(1)}, u32[]{:S(2)}, u32[]{:S(2)}) %collective-permute-start.15) | collective-permute-done | bytes 393248 | tf_op jit(solution)/shard_map/ppermute | solution.py:439
  85.1 4.7 %rows.1 = (bf16[4,256,512]{2,1,0:T(8,128)(2,1)}, f32[1024,384]{1,0:T(8,128)}, bf16[1024,384]{1,0:T(8,128)(2,1)}) custom-call(bf16[512,384]{1,0:T(8,128)(2,1)} %copy-done.4, bf16[512,384]{1,0:T(8,128)(2,1)} %copy-done.8, bf16[512,384]{1,0:T(8,128)(2,1)} %copy-done.9, bf16[512,384]{1,0:T(8,128)(2,1)} %copy-done.10, bf16[384,1024]{1,0:T(8,128)(2,1)} %input_any.1, ...), custom_call_target="tpu_custom_call" | custom-call | tf_op jit(solution)/shard_map/rows/pallas_call | solution.py:444
  89.8 2.0 %slice_bitcast_fusion.2 = (bf16[256,512]{1,0:T(8,128)(2,1)}, bf16[256,512]{1,0:T(8,128)(2,1)}, bf16[256,512]{1,0:T(8,128)(2,1)S(1)}) fusion(bf16[4,256,512]{2,1,0:T(8,128)(2,1)} %get-tuple-element.39), kind=kLoop, calls=%fused_computation.12 | loop fusion | bytes 1572864 | tf_op jit(solution)/shard_map/squeeze | solution.py:564
  92.9 2.2 %collective-permute-start.24 = (bf16[256,512]{1,0:T(8,128)(2,1)}, bf16[256,512]{1,0:T(8,128)(2,1)S(1)}, u32[]{:S(2)}, u32[]{:S(2)}) collective-permute-start(bf16[256,512]{1,0:T(8,128)(2,1)} %get-tuple-element.53), channel_id=1, source_target_pairs={{0,24},{8,0},{16,8},{24,16},{1,25},{9,1},{17,9},{25,17},{2,26},{10... | collective-permute-start | bytes 786440 | tf_op jit(solution)/shard_map/ppermute | solution.py:439
  95.9 7.6 %all-to-all-done.got_any = bf16[8,384,256]{2,1,0:T(8,128)(2,1)S(1)} async-done(((bf16[8,384,256]{2,1,0:T(8,128)(2,1)}), bf16[8,384,256]{2,1,0:T(8,128)(2,1)S(1)}, u32[]{:S(2)}, u32[]{:S(2)}) %all-to-all-start) | async-done | bytes 1572896 | tf_op jit(solution)/shard_map/all_to_all | solution.py:559
  104.4 1.3 collective-permute-start.25
  105.7 2.0 %collective-permute-start.27 = (bf16[256,256]{1,0:T(8,128)(2,1)S(1)}, bf16[256,256]{1,0:T(8,128)(2,1)S(1)}, u32[]{:S(2)}, u32[]{:S(2)}) collective-permute-start(bf16[256,256]{1,0:T(8,128)(2,1)S(1)} %get-tuple-element.56), channel_id=1, source_target_pairs={{0,24},{8,0},{16,8},{24,16},{1,25},{9,1},{17,9},{25,17},{2,26},{10... | collective-permute-start | bytes 393224 | tf_op jit(solution)/shard_map/ppermute | solution.py:439
  110.8 4.1 %collective-permute-done.26 = bf16[256,256]{1,0:T(8,128)(2,1)S(1)} collective-permute-done((bf16[256,256]{1,0:T(8,128)(2,1)S(1)}, bf16[256,256]{1,0:T(8,128)(2,1)S(1)}, u32[]{:S(2)}, u32[]{:S(2)}) %collective-permute-start.26) | collective-permute-done | bytes 131104 | tf_op jit(solution)/shard_map/ppermute | solution.py:439
  115.9 3.5 %all-to-all-start.1 = ((bf16[8,32,768]{2,1,0:T(8,128)(2,1)}), bf16[8,32,768]{2,1,0:T(8,128)(2,1)S(1)}, u32[]{:S(2)}, u32[]{:S(2)}) async-start(bf16[8,32,768]{2,1,0:T(8,128)(2,1)} %bitcast.20), calls=%async_computation.1 | async-start | bytes 786432 | tf_op jit(solution)/shard_map/all_to_all | solution.py:571
  120.0 1.5 %collective-permute-start.21 = (bf16[128,384]{1,0:T(8,128)(2,1)S(1)}, bf16[128,384]{1,0:T(8,128)(2,1)S(1)}, u32[]{:S(2)}, u32[]{:S(2)}) collective-permute-start(bf16[128,384]{1,0:T(8,128)(2,1)S(1)} %get-tuple-element.59), channel_id=1, source_target_pairs={{0,6},{2,0},{4,2},{6,4},{1,7},{3,1},{5,3},{7,5},{8,14},{10,8},{12,... | collective-permute-start | bytes 294920 | tf_op jit(solution)/shard_map/ppermute | solution.py:439
  121.6 1.4 %collective-permute-start.20 = (bf16[128,384]{1,0:T(8,128)(2,1)S(1)}, bf16[128,384]{1,0:T(8,128)(2,1)S(1)}, u32[]{:S(2)}, u32[]{:S(2)}) collective-permute-start(bf16[128,384]{1,0:T(8,128)(2,1)S(1)} %get-tuple-element.60), channel_id=1, source_target_pairs={{0,4},{2,6},{4,0},{6,2},{1,5},{3,7},{5,1},{7,3},{8,12},{10,14},{12... | collective-permute-start | bytes 294920 | tf_op jit(solution)/shard_map/ppermute | solution.py:439
  124.2 1.7 %collective-permute-done.21 = bf16[128,384]{1,0:T(8,128)(2,1)S(1)} collective-permute-done((bf16[128,384]{1,0:T(8,128)(2,1)S(1)}, bf16[128,384]{1,0:T(8,128)(2,1)S(1)}, u32[]{:S(2)}, u32[]{:S(2)}) %collective-permute-start.21) | collective-permute-done | bytes 98336 | tf_op jit(solution)/shard_map/ppermute | solution.py:439
  125.9 1.8 %collective-permute-done.20 = bf16[128,384]{1,0:T(8,128)(2,1)S(1)} collective-permute-done((bf16[128,384]{1,0:T(8,128)(2,1)S(1)}, bf16[128,384]{1,0:T(8,128)(2,1)S(1)}, u32[]{:S(2)}, u32[]{:S(2)}) %collective-permute-start.20) | collective-permute-done | bytes 98336 | tf_op jit(solution)/shard_map/ppermute | solution.py:439
  128.5 2.6 %all-to-all-done.1.got_ref = bf16[8,32,768]{2,1,0:T(8,128)(2,1)S(1)} async-done(((bf16[8,32,768]{2,1,0:T(8,128)(2,1)}), bf16[8,32,768]{2,1,0:T(8,128)(2,1)S(1)}, u32[]{:S(2)}, u32[]{:S(2)}) %all-to-all-start.1) | async-done | bytes 393248 | tf_op jit(solution)/shard_map/all_to_all | solution.py:571
  (73 shorter events, 15.7 us)
Async XLA Ops:
  2.3 11.5 %collective-permute-start.3 = (bf16[384,256]{1,0:T(8,128)(2,1)}, bf16[384,256]{1,0:T(8,128)(2,1)S(1)}, u32[]{:S(2)}, u32[]{:S(2)}) collective-permute-start(bf16[384,256]{1,0:T(8,128)(2,1)} %join.1), channel_id=1, source_target_pairs={{0,224},{32,0},{64,32},{96,64},{128,96},{160,128},{192,160},{224,1... | collective-permute-start | bytes 589832 | tf_op jit(solution)/shard_map/ppermute | solution.py:439
  8.2 8.8 %collective-permute-start = (bf16[384,256]{1,0:T(8,128)(2,1)}, bf16[384,256]{1,0:T(8,128)(2,1)S(1)}, u32[]{:S(2)}, u32[]{:S(2)}) collective-permute-start(bf16[384,256]{1,0:T(8,128)(2,1)} %join.1), channel_id=1, source_target_pairs={{0,32},{32,64},{64,96},{96,128},{128,160},{160,192},{192,224},{224... | collective-permute-start | bytes 589832 | tf_op jit(solution)/shard_map/ppermute | solution.py:439
  10.7 23.5 %copy-start.1 = (bf16[384,512]{1,0:T(8,128)(2,1)S(1)}, bf16[384,512]{1,0:T(8,128)(2,1)}, u32[]{:S(2)}) copy-start(bf16[384,512]{1,0:T(8,128)(2,1)} %start.1.own) | copy-start | bytes 1179652
  10.7 13.3 %collective-permute-start.9 = (bf16[384,512]{1,0:T(8,128)(2,1)}, bf16[384,512]{1,0:T(8,128)(2,1)S(1)}, u32[]{:S(2)}, u32[]{:S(2)}) collective-permute-start(bf16[384,512]{1,0:T(8,128)(2,1)} %start.1.own), channel_id=1, source_target_pairs={{0,24},{8,0},{16,8},{24,16},{1,25},{9,1},{17,9},{25,17},{2,26},{10... | collective-permute-start | bytes 1179656 | tf_op jit(solution)/shard_map/ppermute | solution.py:439
  13.8 13.5 %collective-permute-start.8 = (bf16[384,512]{1,0:T(8,128)(2,1)}, bf16[384,512]{1,0:T(8,128)(2,1)S(1)}, u32[]{:S(2)}, u32[]{:S(2)}) collective-permute-start(bf16[384,512]{1,0:T(8,128)(2,1)} %start.1.own), channel_id=1, source_target_pairs={{0,8},{8,16},{16,24},{24,0},{1,9},{9,17},{17,25},{25,1},{2,10},{10... | collective-permute-start | bytes 1179656 | tf_op jit(solution)/shard_map/ppermute | solution.py:439
  13.8 6.6 %collective-permute-start.4 = (bf16[384,256]{1,0:T(8,128)(2,1)S(1)}, bf16[384,256]{1,0:T(8,128)(2,1)S(1)}, u32[]{:S(2)}, u32[]{:S(2)}) collective-permute-start(bf16[384,256]{1,0:T(8,128)(2,1)S(1)} %collective-permute-done.3), channel_id=1, source_target_pairs={{0,224},{32,0},{64,32},{96,64},{128,96},{160,128},{192,160},{224,1... | collective-permute-start | bytes 589832 | tf_op jit(solution)/shard_map/ppermute | solution.py:439
  17.0 7.0 %collective-permute-start.1 = (bf16[384,256]{1,0:T(8,128)(2,1)S(1)}, bf16[384,256]{1,0:T(8,128)(2,1)S(1)}, u32[]{:S(2)}, u32[]{:S(2)}) collective-permute-start(bf16[384,256]{1,0:T(8,128)(2,1)S(1)} %collective-permute-done), channel_id=1, source_target_pairs={{0,32},{32,64},{64,96},{96,128},{128,160},{160,192},{192,224},{224... | collective-permute-start | bytes 589832 | tf_op jit(solution)/shard_map/ppermute | solution.py:439
  20.4 6.9 %collective-permute-start.5 = (bf16[384,256]{1,0:T(8,128)(2,1)S(1)}, bf16[384,256]{1,0:T(8,128)(2,1)S(1)}, u32[]{:S(2)}, u32[]{:S(2)}) collective-permute-start(bf16[384,256]{1,0:T(8,128)(2,1)S(1)} %collective-permute-done.4), channel_id=1, source_target_pairs={{0,224},{32,0},{64,32},{96,64},{128,96},{160,128},{192,160},{224,1... | collective-permute-start | bytes 589832 | tf_op jit(solution)/shard_map/ppermute | solution.py:439
  24.1 7.0 %collective-permute-start.2 = (bf16[384,256]{1,0:T(8,128)(2,1)S(1)}, bf16[384,256]{1,0:T(8,128)(2,1)S(1)}, u32[]{:S(2)}, u32[]{:S(2)}) collective-permute-start(bf16[384,256]{1,0:T(8,128)(2,1)S(1)} %collective-permute-done.1), channel_id=1, source_target_pairs={{0,32},{32,64},{64,96},{96,128},{128,160},{160,192},{192,224},{224... | collective-permute-start | bytes 589832 | tf_op jit(solution)/shard_map/ppermute | solution.py:439
  24.1 7.1 %collective-permute-start.11 = (bf16[192,512]{1,0:T(8,128)(2,1)S(1)}, bf16[192,512]{1,0:T(8,128)(2,1)S(1)}, u32[]{:S(2)}, u32[]{:S(2)}) collective-permute-start(bf16[192,512]{1,0:T(8,128)(2,1)S(1)} %slice.70), channel_id=1, source_target_pairs={{0,24},{8,0},{16,8},{24,16},{1,25},{9,1},{17,9},{25,17},{2,26},{10... | collective-permute-start | bytes 589832 | tf_op jit(solution)/shard_map/ppermute | solution.py:439
  27.3 7.0 %collective-permute-start.10 = (bf16[192,512]{1,0:T(8,128)(2,1)S(1)}, bf16[192,512]{1,0:T(8,128)(2,1)S(1)}, u32[]{:S(2)}, u32[]{:S(2)}) collective-permute-start(bf16[192,512]{1,0:T(8,128)(2,1)S(1)} %slice.69), channel_id=1, source_target_pairs={{0,8},{8,16},{16,24},{24,0},{1,9},{9,17},{17,25},{25,1},{2,10},{10... | collective-permute-start | bytes 589832 | tf_op jit(solution)/shard_map/ppermute | solution.py:439
  27.4 7.7 %collective-permute-start.7 = (bf16[256,256]{1,0:T(8,128)(2,1)S(1)}, bf16[256,256]{1,0:T(8,128)(2,1)S(1)}, u32[]{:S(2)}, u32[]{:S(2)}) collective-permute-start(bf16[256,256]{1,0:T(8,128)(2,1)S(1)} %slice.68), channel_id=1, source_target_pairs={{0,224},{32,0},{64,32},{96,64},{128,96},{160,128},{192,160},{224,1... | collective-permute-start | bytes 393224 | tf_op jit(solution)/shard_map/ppermute | solution.py:439
  31.1 6.3 %collective-permute-start.6 = (bf16[256,256]{1,0:T(8,128)(2,1)S(1)}, bf16[256,256]{1,0:T(8,128)(2,1)S(1)}, u32[]{:S(2)}, u32[]{:S(2)}) collective-permute-start(bf16[256,256]{1,0:T(8,128)(2,1)S(1)} %slice.67), channel_id=1, source_target_pairs={{0,32},{32,64},{64,96},{96,128},{128,160},{160,192},{192,224},{224... | collective-permute-start | bytes 393224 | tf_op jit(solution)/shard_map/ppermute | solution.py:439
  43.1 4.2 %collective-permute-start.14 = (f32[48,256]{1,0:T(8,128)S(1)}, f32[48,256]{1,0:T(8,128)S(1)}, u32[]{:S(2)}, u32[]{:S(2)}) collective-permute-start(f32[48,256]{1,0:T(8,128)S(1)} %get-tuple-element.28.st0), channel_id=1, source_target_pairs={{0,24},{8,0},{16,8},{24,16},{1,25},{9,1},{17,9},{25,17},{2,26},{10... | collective-permute-start | bytes 147464 | tf_op jit(solution)/shard_map/ppermute | solution.py:439
  43.4 5.7 %collective-permute-start.13 = (f32[48,256]{1,0:T(8,128)S(1)}, f32[48,256]{1,0:T(8,128)S(1)}, u32[]{:S(2)}, u32[]{:S(2)}) collective-permute-start(f32[48,256]{1,0:T(8,128)S(1)} %get-tuple-element.28.st0), channel_id=1, source_target_pairs={{0,16},{8,24},{16,0},{24,8},{1,17},{9,25},{17,1},{25,9},{2,18},{10... | collective-permute-start | bytes 147464 | tf_op jit(solution)/shard_map/ppermute | solution.py:439
  44.9 5.3 %collective-permute-start.12 = (f32[48,256]{1,0:T(8,128)S(1)}, f32[48,256]{1,0:T(8,128)S(1)}, u32[]{:S(2)}, u32[]{:S(2)}) collective-permute-start(f32[48,256]{1,0:T(8,128)S(1)} %get-tuple-element.28.st0), channel_id=1, source_target_pairs={{0,8},{8,16},{16,24},{24,0},{1,9},{9,17},{17,25},{25,1},{2,10},{10... | collective-permute-start | bytes 147464 | tf_op jit(solution)/shard_map/ppermute | solution.py:439
  62.5 41.0 %all-to-all-start = ((bf16[8,384,256]{2,1,0:T(8,128)(2,1)}), bf16[8,384,256]{2,1,0:T(8,128)(2,1)S(1)}, u32[]{:S(2)}, u32[]{:S(2)}) async-start(bf16[8,384,256]{2,1,0:T(8,128)(2,1)} %bitcast.10), calls=%async_computation | async-start | bytes 3145728 | tf_op jit(solution)/shard_map/all_to_all | solution.py:559
  68.8 14.8 %collective-permute-start.15 = (bf16[512,384]{1,0:T(8,128)(2,1)S(1)}, bf16[512,384]{1,0:T(8,128)(2,1)S(1)}, u32[]{:S(2)}, u32[]{:S(2)}) collective-permute-start(bf16[512,384]{1,0:T(8,128)(2,1)S(1)} %get-tuple-element.31), channel_id=1, source_target_pairs={{0,8},{8,16},{16,24},{24,0},{1,9},{9,17},{17,25},{25,1},{2,10},{10... | collective-permute-start | bytes 1179656 | tf_op jit(solution)/shard_map/ppermute | solution.py:439
  69.5 14.2 %collective-permute-start.16 = (bf16[512,384]{1,0:T(8,128)(2,1)S(1)}, bf16[512,384]{1,0:T(8,128)(2,1)S(1)}, u32[]{:S(2)}, u32[]{:S(2)}) collective-permute-start(bf16[512,384]{1,0:T(8,128)(2,1)S(1)} %get-tuple-element.32), channel_id=1, source_target_pairs={{0,16},{8,24},{16,0},{24,8},{1,17},{9,25},{17,1},{25,9},{2,18},{10... | collective-permute-start | bytes 1179656 | tf_op jit(solution)/shard_map/ppermute | solution.py:439
  69.5 14.8 %collective-permute-start.17 = (bf16[512,384]{1,0:T(8,128)(2,1)S(1)}, bf16[512,384]{1,0:T(8,128)(2,1)S(1)}, u32[]{:S(2)}, u32[]{:S(2)}) collective-permute-start(bf16[512,384]{1,0:T(8,128)(2,1)S(1)} %get-tuple-element.33), channel_id=1, source_target_pairs={{0,24},{8,0},{16,8},{24,16},{1,25},{9,1},{17,9},{25,17},{2,26},{10... | collective-permute-start | bytes 1179656 | tf_op jit(solution)/shard_map/ppermute | solution.py:439
  89.8 13.7 %copy-start.3 = (bf16[1024,384]{1,0:T(8,128)(2,1)S(1)}, bf16[1024,384]{1,0:T(8,128)(2,1)}, u32[]{:S(2)}) copy-start(bf16[1024,384]{1,0:T(8,128)(2,1)} %get-tuple-element.34.turned_any) | copy-start | bytes 2359300
  91.8 16.6 %collective-permute-start.22 = (bf16[256,512]{1,0:T(8,128)(2,1)}, bf16[256,512]{1,0:T(8,128)(2,1)S(1)}, u32[]{:S(2)}, u32[]{:S(2)}) collective-permute-start(bf16[256,512]{1,0:T(8,128)(2,1)} %get-tuple-element.52), channel_id=1, source_target_pairs={{0,8},{8,16},{16,24},{24,0},{1,9},{9,17},{17,25},{25,1},{2,10},{10... | collective-permute-start | bytes 786440 | tf_op jit(solution)/shard_map/ppermute | solution.py:439
  92.9 15.8 %collective-permute-start.24 = (bf16[256,512]{1,0:T(8,128)(2,1)}, bf16[256,512]{1,0:T(8,128)(2,1)S(1)}, u32[]{:S(2)}, u32[]{:S(2)}) collective-permute-start(bf16[256,512]{1,0:T(8,128)(2,1)} %get-tuple-element.53), channel_id=1, source_target_pairs={{0,24},{8,0},{16,8},{24,16},{1,25},{9,1},{17,9},{25,17},{2,26},{10... | collective-permute-start | bytes 786440 | tf_op jit(solution)/shard_map/ppermute | solution.py:439
  95.1 13.8 %collective-permute-start.23 = (bf16[256,512]{1,0:T(8,128)(2,1)S(1)}, bf16[256,512]{1,0:T(8,128)(2,1)S(1)}, u32[]{:S(2)}, u32[]{:S(2)}) collective-permute-start(bf16[256,512]{1,0:T(8,128)(2,1)S(1)} %get-tuple-element.54), channel_id=1, source_target_pairs={{0,16},{8,24},{16,0},{24,8},{1,17},{9,25},{17,1},{25,9},{2,18},{10... | collective-permute-start | bytes 786440 | tf_op jit(solution)/shard_map/ppermute | solution.py:439
  104.4 6.5 %collective-permute-start.25 = (bf16[256,256]{1,0:T(8,128)(2,1)S(1)}, bf16[256,256]{1,0:T(8,128)(2,1)S(1)}, u32[]{:S(2)}, u32[]{:S(2)}) collective-permute-start(bf16[256,256]{1,0:T(8,128)(2,1)S(1)} %get-tuple-element.55), channel_id=1, source_target_pairs={{0,8},{8,16},{16,24},{24,0},{1,9},{9,17},{17,25},{25,1},{2,10},{10... | collective-permute-start | bytes 393224 | tf_op jit(solution)/shard_map/ppermute | solution.py:439
  105.7 5.2 %collective-permute-start.27 = (bf16[256,256]{1,0:T(8,128)(2,1)S(1)}, bf16[256,256]{1,0:T(8,128)(2,1)S(1)}, u32[]{:S(2)}, u32[]{:S(2)}) collective-permute-start(bf16[256,256]{1,0:T(8,128)(2,1)S(1)} %get-tuple-element.56), channel_id=1, source_target_pairs={{0,24},{8,0},{16,8},{24,16},{1,25},{9,1},{17,9},{25,17},{2,26},{10... | collective-permute-start | bytes 393224 | tf_op jit(solution)/shard_map/ppermute | solution.py:439
  108.4 6.6 %collective-permute-start.26 = (bf16[256,256]{1,0:T(8,128)(2,1)S(1)}, bf16[256,256]{1,0:T(8,128)(2,1)S(1)}, u32[]{:S(2)}, u32[]{:S(2)}) collective-permute-start(bf16[256,256]{1,0:T(8,128)(2,1)S(1)} %get-tuple-element.57), channel_id=1, source_target_pairs={{0,16},{8,24},{16,0},{24,8},{1,17},{9,25},{17,1},{25,9},{2,18},{10... | collective-permute-start | bytes 393224 | tf_op jit(solution)/shard_map/ppermute | solution.py:439
  108.7 10.6 %collective-permute-start.18 = (bf16[512,384]{1,0:T(8,128)(2,1)S(1)}, bf16[512,384]{1,0:T(8,128)(2,1)S(1)}, u32[]{:S(2)}, u32[]{:S(2)}) collective-permute-start(bf16[512,384]{1,0:T(8,128)(2,1)S(1)} %get-tuple-element.38), channel_id=1, source_target_pairs={{0,1},{1,0},{2,3},{3,2},{4,5},{5,4},{6,7},{7,6},{8,9},{9,8},{10,11... | collective-permute-start | bytes 1179656 | tf_op jit(solution)/shard_map/ppermute | solution.py:439
  115.9 15.3 %all-to-all-start.1 = ((bf16[8,32,768]{2,1,0:T(8,128)(2,1)}), bf16[8,32,768]{2,1,0:T(8,128)(2,1)S(1)}, u32[]{:S(2)}, u32[]{:S(2)}) async-start(bf16[8,32,768]{2,1,0:T(8,128)(2,1)} %bitcast.20), calls=%async_computation.1 | async-start | bytes 786432 | tf_op jit(solution)/shard_map/all_to_all | solution.py:571
  119.5 4.7 %collective-permute-start.19 = (bf16[128,384]{1,0:T(8,128)(2,1)S(1)}, bf16[128,384]{1,0:T(8,128)(2,1)S(1)}, u32[]{:S(2)}, u32[]{:S(2)}) collective-permute-start(bf16[128,384]{1,0:T(8,128)(2,1)S(1)} %get-tuple-element.58), channel_id=1, source_target_pairs={{0,2},{2,4},{4,6},{6,0},{1,3},{3,5},{5,7},{7,1},{8,10},{10,12},{12... | collective-permute-start | bytes 294920 | tf_op jit(solution)/shard_map/ppermute | solution.py:439
  120.0 5.8 %collective-permute-start.21 = (bf16[128,384]{1,0:T(8,128)(2,1)S(1)}, bf16[128,384]{1,0:T(8,128)(2,1)S(1)}, u32[]{:S(2)}, u32[]{:S(2)}) collective-permute-start(bf16[128,384]{1,0:T(8,128)(2,1)S(1)} %get-tuple-element.59), channel_id=1, source_target_pairs={{0,6},{2,0},{4,2},{6,4},{1,7},{3,1},{5,3},{7,5},{8,14},{10,8},{12,... | collective-permute-start | bytes 294920 | tf_op jit(solution)/shard_map/ppermute | solution.py:439
  121.6 6.1 %collective-permute-start.20 = (bf16[128,384]{1,0:T(8,128)(2,1)S(1)}, bf16[128,384]{1,0:T(8,128)(2,1)S(1)}, u32[]{:S(2)}, u32[]{:S(2)}) collective-permute-start(bf16[128,384]{1,0:T(8,128)(2,1)S(1)} %get-tuple-element.60), channel_id=1, source_target_pairs={{0,4},{2,6},{4,0},{6,2},{1,5},{3,7},{5,1},{7,3},{8,12},{10,14},{12... | collective-permute-start | bytes 294920 | tf_op jit(solution)/shard_map/ppermute | solution.py:439
  (9 other events, 28.3 us)
